TPU v7x, 128 devices: a whole 4x4x4 slice. The times are simulated.
128 devices in a mesh: bins: 8 (over y, core), cells: 16 (over z, x).
Axes of the slice: x: 4, y: 4, z: 4, core: 2. Of those that a mesh axis runs over, the one named last changes fastest.
Arguments:
- concen: bfloat16 [1024, 128, 1024], P('bins', 'cells'), may hold values from 0.049804688 to 2
- courant: float32 [2, 128, 1024], P(None, 'cells'), may hold values from -0.45 to 0.45
- saturation: float32 [128, 1024], P('cells', 'bins'), may hold values from 0.2 to 1.5
- growth: float32 [1024], replicated, may hold values from 0.05 to 0.5
- kernel: bfloat16 [8, 8, 128, 128], replicated, may hold values from 9.9658966e-05 to 0.0039978027
- redist: bfloat16 [8, 8, 128, 128], replicated, may hold values from 0.00019454956 to 0.0078125
- pair_lists: int32 [128, 64], replicated, may hold values from 0 to 63, each once within a row
- active_count: int32 [128], replicated, may hold values from 4 to 48, as said below
Outputs:
- updated: bfloat16 [1024, 128, 1024], P('bins', 'cells')
Inputs may be any that keep to these rules, and one draw needn't show every extreme that they name: `pair_lists`: each row holds every pair number once. `active_count`: some tile has exactly 48 active pairs.
All inputs are finite; a program needn't handle non-finite values.
Results may differ from a plain program's by a relative error of at most 0.001.
The roundings to bfloat16 on the way count: a program that leaves them out, or rounds other values in their place, can miss the bound.
Values may be sent and summed in bfloat16 or wider, within the bound.
No kernel may reach another device: no remote copies, remote signals or barrier semaphores. Data moves between devices by JAX's collectives and lax.ppermute only.
A program may use at most 64 MiB of HBM per device.

v0:
```python
import jax
import jax.numpy as jnp
from jax import lax
from jax.sharding import PartitionSpec as P

SUB = 2


def padded(value, sides, width):
    for axis, dim in sides:
        size, length = (lax.axis_size(axis), value.shape[dim])
        up = [(i, (i + 1) % size) for i in range(size)]
        down = [(j, i) for i, j in up]
        last = lax.slice_in_dim(value, length - width, length, axis=dim)
        initial = lax.slice_in_dim(value, 0, width, axis=dim)
        before = lax.ppermute(last, axis, up)
        after = lax.ppermute(initial, axis, down)
        value = jnp.concatenate([before, value, after], axis=dim)
    return value


def shifted(value, axis, steps):
    count = lax.axis_size(axis)
    pairs = [(source, (source + steps) % count) for source in range(count)]
    return lax.ppermute(value, axis, pairs)


def advect_rows(extended, rates):
    face_x = rates[0, :-1]
    flux_x = (
        jnp.maximum(face_x, 0.0) * extended[:, :-1] + jnp.minimum(face_x, 0.0) * extended[:, 1:]
    )
    inner = extended[:, 1:-1]
    face_y = rates[1, 1:-1]
    above = jnp.roll(inner, -1, 2)
    flux_y = jnp.maximum(face_y, 0.0) * inner + jnp.minimum(face_y, 0.0) * above
    return inner - flux_x[:, 1:] + flux_x[:, :-1] - flux_y + jnp.roll(flux_y, 1, 2)


def advect_half(start_low, rates):
    fields = start_low.astype(jnp.float32)
    for substep in range(SUB):
        extended = padded(fields, (("cells", 1),), 1)
        fields = advect_rows(extended, rates)
    return fields


def block_sum(matrices, sources, pair_row, active):
    nblocks = matrices.shape[0]

    def add_pair(index, totals):
        pair_id = pair_row[index]
        row_block = pair_id // nblocks
        col_block = pair_id % nblocks
        tile_matrix = lax.dynamic_index_in_dim(
            lax.dynamic_index_in_dim(matrices, row_block, 0, False), col_block, 0, False
        )
        source = lax.dynamic_index_in_dim(sources, col_block, 0, False)
        current = lax.dynamic_index_in_dim(totals, row_block, 0, False)
        update = current + jnp.dot(tile_matrix, source, preferred_element_type=jnp.float32)
        return lax.dynamic_update_index_in_dim(totals, update, row_block, 0)

    start = jnp.zeros((nblocks, sources.shape[1], sources.shape[2]), jnp.float32)
    return lax.fori_loop(0, active, add_pair, start)


def coagulate(concen, kernel, redist, pair_row, active):
    nblocks = kernel.shape[0]
    block_size = kernel.shape[2]
    blocks = concen.reshape(nblocks, block_size, concen.shape[1])
    collide = block_sum(kernel, blocks, pair_row, active)
    losses = blocks.astype(jnp.float32) * collide
    formed = block_sum(redist, losses.astype(jnp.bfloat16), pair_row, active)
    return (blocks.astype(jnp.float32) - losses + formed).reshape(concen.shape)


def condense(after, satur, growth):
    flux = growth[:, None] * satur[None, :] * after
    inflow = jnp.concatenate([jnp.zeros_like(flux[:1]), flux[:-1]], 0)
    return (after - flux + inflow).astype(jnp.bfloat16)


def shards(concen, courant, saturation, growth, kernel, redist, pair_lists, active_count):
    below = shifted(courant[:, -1:], "cells", 1)
    rates = jnp.concatenate([below, courant, jnp.zeros_like(below)], 1)
    fields = advect_half(concen, rates)
    first = fields.astype(jnp.bfloat16)
    regrouped = lax.all_to_all(first, "bins", split_axis=2, concat_axis=0, tiled=True)
    bins_all, rows, width = regrouped.shape
    columns = regrouped.reshape(bins_all, rows * width)
    satur = saturation.reshape(rows * width)
    tile_id = lax.axis_index("bins") * lax.axis_size("cells") + lax.axis_index("cells")
    after = coagulate(columns, kernel, redist, pair_lists[tile_id], active_count[tile_id])
    middle = condense(after, satur, growth).reshape(bins_all, rows, width)
    scattered = lax.all_to_all(middle, "bins", split_axis=0, concat_axis=2, tiled=True)
    fields = advect_half(scattered, rates)
    return fields.astype(jnp.bfloat16)


def solution(mesh):
    return jax.shard_map(
        shards,
        mesh=mesh,
        in_specs=(
            P("bins", "cells", None),
            P(None, "cells", None),
            P("cells", "bins"),
            P(),
            P(),
            P(),
            P(),
            P(),
        ),
        out_specs=P("bins", "cells", None),
        check_vma=False,
    )
```

profile of v0, /device:TPU:0, one launch (start us, length us, event | category | flops | bytes accessed | tf_op | source)
XLA Modules:
  0.0 843.8 jit_solution(17611803082692331836)
XLA Ops:
  0.0 3.3 copy.15
  5.1 4.8 collective-permute-start.2
  10.5 2.8 fusion.29
  13.6 8.3 collective-permute-done
  21.9 3.0 fusion.14
  26.7 5.3 collective-permute-start.4
  32.3 2.8 fusion.30
  35.1 8.0 collective-permute-done.3
  43.1 3.0 fusion.15
  47.6 2.7 copy.16
  50.2 4.5 all-to-all-start
  55.5 26.4 %all-to-all-done = bf16[128,8,1024]{0,1,2:T(8,128)(2,1)S(1)} async-done(((bf16[128,8,1024]{0,1,2:T(8,128)(2,1)}), bf16[128,8,1024]{0,1,2:T(8,128)(2,1)S(1)}, u32[]{:S(2)}, u32[]{:S(2)}) %all-to-all-start) | async-done | bytes 2097184 | tf_op jit(solution)/shard_map/all_to_all | solution.py:88
  81.9 3.2 copy.17
  85.1 2.8 reshape_reshape.3
  87.9 2.5 broadcast.22.clone
  90.4 243.6 %while.26 = (s32[]{:T(128)}, f32[8,128,1024]{2,1,0:T(8,128)}, s32[]{:T(128)}, s32[64]{0:T(128)S(1)}, bf16[8,8,128,128]{3,2,1,0:T(8,128)(2,1)}, /*index=5*/bf16[8...) while((s32[]{:T(128)}, f32[8,128,1024]{2,1,0:T(8,128)}, ...), condition=%wide.region_1.2_spmd, body=%wide.region_0.1_spmd.sunk | while | flops 33685536 | bytes 2392542 | solution.py:64
  334.1 4.3 fusion.35
  338.4 2.5 broadcast.22
  340.9 249.7 %while.27 = (s32[]{:T(128)}, f32[8,128,1024]{2,1,0:T(8,128)}, s32[]{:T(128)}, s32[64]{0:T(128)S(1)}, bf16[8,8,128,128]{3,2,1,0:T(8,128)(2,1)}, /*index=5*/bf16[8...) while((s32[]{:T(128)}, f32[8,128,1024]{2,1,0:T(8,128)}, ...), condition=%wide.region_3.4_spmd, body=%wide.region_2.3_spmd.sunk | while | flops 33685536 | bytes 2392542 | solution.py:64
  359.6 2.0 fusion.51
  373.4 2.0 fusion.51
  380.3 2.0 fusion.51
  387.3 2.0 fusion.51
  394.2 2.0 fusion.51
  401.1 2.0 fusion.51
  414.9 2.0 fusion.51
  421.8 2.0 fusion.51
  428.7 2.0 fusion.51
  442.5 2.0 fusion.51
  449.5 2.0 fusion.51
  456.4 2.0 fusion.51
  463.3 2.0 fusion.51
  470.2 2.0 fusion.51
  477.1 2.0 fusion.51
  490.9 2.0 fusion.51
  497.8 2.0 fusion.51
  504.8 2.0 fusion.51
  511.7 2.0 fusion.51
  518.6 2.0 fusion.51
  525.5 2.0 fusion.51
  532.4 2.0 fusion.51
  539.3 2.0 fusion.51
  546.3 2.0 fusion.51
  553.2 2.0 fusion.51
  560.1 2.0 fusion.51
  567.0 2.0 fusion.51
  573.9 2.0 fusion.51
  580.8 2.0 fusion.51
  587.7 2.0 fusion.51
  590.6 5.1 fusion.18
  597.6 30.0 %all_to_all.24 = bf16[1024,8,128]{2,1,0:T(8,128)(2,1)S(1)} all-to-all(bf16[1024,8,128]{2,1,0:T(8,128)(2,1)S(1)} %bitcast.95), channel_id=1, replica_groups=mesh['bins'=8,'cells'=16] {'bins'}, dimensions={0} | all-to-all | bytes 4194304 | tf_op jit(solution)/shard_map/all_to_all | solution.py:95
  627.6 2.2 convert_bitcast_fusion
  629.8 5.3 copy.18
  636.4 50.3 %collective-permute-start.5 = (f32[128,1,1024]{0,2,1:T(8,128)S(1)}, f32[128,1,1024]{0,2,1:T(8,128)S(1)}, u32[]{:S(2)}, u32[]{:S(2)}) collective-permute-start(f32[128,1,1024]{0,2,1:T(8,128)S(1)} %get-tuple-element.256), channel_id=1, source_target_pairs={{0,1},{1,2},{2,3},{3,4},{4,5},{5,6},{6,7},{7,8},{8,9},{9,10},{10,1... | collective-permute-start | bytes 1572872 | tf_op jit(solution)/shard_map/ppermute | solution.py:16
  686.7 117.3 %collective-permute-start.6 = (f32[128,1,1024]{0,2,1:T(8,128)S(1)}, f32[128,1,1024]{0,2,1:T(8,128)S(1)}, u32[]{:S(2)}, u32[]{:S(2)}) collective-permute-start(f32[128,1,1024]{0,2,1:T(8,128)S(1)} %get-tuple-element.255), channel_id=1, source_target_pairs={{1,0},{2,1},{3,2},{4,3},{5,4},{6,5},{7,6},{8,7},{9,8},{10,9},{11,1... | collective-permute-start | bytes 1572872 | tf_op jit(solution)/shard_map/ppermute | solution.py:17
  804.0 2.5 slice.192
  806.5 3.1 fusion.31
  809.6 5.9 collective-permute-done.5
  815.5 3.0 fusion.16
  820.4 5.3 collective-permute-start.8
  826.1 2.8 fusion.32
  828.9 7.5 collective-permute-done.7
  836.4 3.0 fusion.17
  840.9 2.9 copy.19
  (237 shorter events, 212.4 us)
Async XLA Ops:
  0.0 55.3 %copy-start = (s32[128,64]{0,1:T(8,128)S(1)}, s32[128,64]{0,1:T(8,128)}, u32[]{:S(2)}) copy-start(s32[128,64]{0,1:T(8,128)} %param.18) | copy-start | bytes 98308
  0.0 9.9 %copy-start.3 = (f32[2,8,1024]{2,1,0:T(8,128)S(1)}, f32[2,8,1024]{2,1,0:T(8,128)}, u32[]{:S(2)}) copy-start(f32[2,8,1024]{2,1,0:T(8,128)} %param.13) | copy-start | bytes 196612
  3.4 18.5 %collective-permute-start.1 = (f32[128,1,1024]{0,2,1:T(8,128)S(1)}, f32[128,1,1024]{0,2,1:T(8,128)S(1)}, u32[]{:S(2)}, u32[]{:S(2)}) collective-permute-start(f32[128,1,1024]{0,2,1:T(8,128)S(1)} %get-tuple-element.260), channel_id=1, source_target_pairs={{0,1},{1,2},{2,3},{3,4},{4,5},{5,6},{6,7},{7,8},{8,9},{9,10},{10,1... | collective-permute-start | bytes 1572872 | tf_op jit(solution)/shard_map/ppermute | solution.py:16
  5.1 16.9 %collective-permute-start.2 = (f32[128,1,1024]{0,2,1:T(8,128)S(1)}, f32[128,1,1024]{0,2,1:T(8,128)S(1)}, u32[]{:S(2)}, u32[]{:S(2)}) collective-permute-start(f32[128,1,1024]{0,2,1:T(8,128)S(1)} %get-tuple-element.259), channel_id=1, source_target_pairs={{1,0},{2,1},{3,2},{4,3},{5,4},{6,5},{7,6},{8,7},{9,8},{10,9},{11,1... | collective-permute-start | bytes 1572872 | tf_op jit(solution)/shard_map/ppermute | solution.py:17
  9.9 12.0 %collective-permute-start = (f32[2,1,1024]{2,1,0:T(1,128)S(1)}, f32[2,1,1024]{2,1,0:T(1,128)S(1)}, u32[]{:S(2)}, u32[]{:S(2)}) collective-permute-start(f32[2,1,1024]{2,1,0:T(1,128)S(1)} %slice.135), channel_id=1, source_target_pairs={{0,1},{1,2},{2,3},{3,4},{4,5},{5,6},{6,7},{7,8},{8,9},{9,10},{10,1... | collective-permute-start | bytes 24584 | tf_op jit(solution)/shard_map/ppermute | solution.py:25
  26.6 16.5 %collective-permute-start.3 = (f32[128,1,1024]{0,2,1:T(8,128)S(1)}, f32[128,1,1024]{0,2,1:T(8,128)S(1)}, u32[]{:S(2)}, u32[]{:S(2)}) collective-permute-start(f32[128,1,1024]{0,2,1:T(8,128)S(1)} %get-tuple-element.258), channel_id=1, source_target_pairs={{0,1},{1,2},{2,3},{3,4},{4,5},{5,6},{6,7},{7,8},{8,9},{9,10},{10,1... | collective-permute-start | bytes 1572872 | tf_op jit(solution)/shard_map/ppermute | solution.py:16
  26.7 16.4 %collective-permute-start.4 = (f32[128,1,1024]{0,2,1:T(8,128)S(1)}, f32[128,1,1024]{0,2,1:T(8,128)S(1)}, u32[]{:S(2)}, u32[]{:S(2)}) collective-permute-start(f32[128,1,1024]{0,2,1:T(8,128)S(1)} %get-tuple-element.257), channel_id=1, source_target_pairs={{1,0},{2,1},{3,2},{4,3},{5,4},{6,5},{7,6},{8,7},{9,8},{10,9},{11,1... | collective-permute-start | bytes 1572872 | tf_op jit(solution)/shard_map/ppermute | solution.py:17
  47.5 7.2 copy-start.6
  50.2 31.7 %all-to-all-start = ((bf16[128,8,1024]{0,1,2:T(8,128)(2,1)}), bf16[128,8,1024]{0,1,2:T(8,128)(2,1)S(1)}, u32[]{:S(2)}, u32[]{:S(2)}) async-start(bf16[128,8,1024]{0,1,2:T(8,128)(2,1)} %copy.16), calls=%async_computation | async-start | bytes 4194304 | tf_op jit(solution)/shard_map/all_to_all | solution.py:88
  590.5 5.1 copy-start.4
  590.6 5.1 copy-start.5
  636.4 179.1 %collective-permute-start.5 = (f32[128,1,1024]{0,2,1:T(8,128)S(1)}, f32[128,1,1024]{0,2,1:T(8,128)S(1)}, u32[]{:S(2)}, u32[]{:S(2)}) collective-permute-start(f32[128,1,1024]{0,2,1:T(8,128)S(1)} %get-tuple-element.256), channel_id=1, source_target_pairs={{0,1},{1,2},{2,3},{3,4},{4,5},{5,6},{6,7},{7,8},{8,9},{9,10},{10,1... | collective-permute-start | bytes 1572872 | tf_op jit(solution)/shard_map/ppermute | solution.py:16
  686.7 119.8 %copy-start.2 = (f32[128,8,8,128]{0,3,2,1:T(8,128)S(1)}, f32[128,8,8,128]{0,3,2,1:T(8,128)}, u32[]{:S(2)}) copy-start(f32[128,8,8,128]{0,3,2,1:T(8,128)} %copy.18) | copy-start | bytes 12582916
  686.7 128.8 %collective-permute-start.6 = (f32[128,1,1024]{0,2,1:T(8,128)S(1)}, f32[128,1,1024]{0,2,1:T(8,128)S(1)}, u32[]{:S(2)}, u32[]{:S(2)}) collective-permute-start(f32[128,1,1024]{0,2,1:T(8,128)S(1)} %get-tuple-element.255), channel_id=1, source_target_pairs={{1,0},{2,1},{3,2},{4,3},{5,4},{6,5},{7,6},{8,7},{9,8},{10,9},{11,1... | collective-permute-start | bytes 1572872 | tf_op jit(solution)/shard_map/ppermute | solution.py:17
  820.4 16.1 %collective-permute-start.7 = (f32[128,1,1024]{0,2,1:T(8,128)S(1)}, f32[128,1,1024]{0,2,1:T(8,128)S(1)}, u32[]{:S(2)}, u32[]{:S(2)}) collective-permute-start(f32[128,1,1024]{0,2,1:T(8,128)S(1)} %get-tuple-element.254), channel_id=1, source_target_pairs={{0,1},{1,2},{2,3},{3,4},{4,5},{5,6},{6,7},{7,8},{8,9},{9,10},{10,1... | collective-permute-start | bytes 1572872 | tf_op jit(solution)/shard_map/ppermute | solution.py:16
  820.4 16.0 %collective-permute-start.8 = (f32[128,1,1024]{0,2,1:T(8,128)S(1)}, f32[128,1,1024]{0,2,1:T(8,128)S(1)}, u32[]{:S(2)}, u32[]{:S(2)}) collective-permute-start(f32[128,1,1024]{0,2,1:T(8,128)S(1)} %get-tuple-element.253), channel_id=1, source_target_pairs={{1,0},{2,1},{3,2},{4,3},{5,4},{6,5},{7,6},{8,7},{9,8},{10,9},{11,1... | collective-permute-start | bytes 1572872 | tf_op jit(solution)/shard_map/ppermute | solution.py:17
  839.5 4.4 copy-start.1
where the time goes:
time: 857 us; the launch traced here: 844 us
  loops' own time  235 us (27%)
  starting transfers between devices  189 us (22%)
  local copies, waits for them, and re-layouts  154 us (18%)
  matrix products  136 us (16%)
  waiting for transfers between devices  56.1 us (7%)
  other arithmetic  42.9 us (5%)
  blocking collectives  30 us (4%)
    another operation x2, loops' own time, block_sum(): return lax.fori_loop(0, active, add_pair, start)  235 us
    dot_general x72, matrix products, add_pair(): jnp.dot(tile_matrix, source, preferred_element_type=jnp.float32)  136 us
    ppermute x4, starting transfers between devices, padded(): after = lax.ppermute(initial, axis, down)  133 us
    dynamic_slice x72, local copies, waits for them, and re-layouts, add_pair(): current = lax.dynamic_index_in_dim(totals, row_block, 0, False)  77.9 us
    ppermute x4, starting transfers between devices, padded(): before = lax.ppermute(last, axis, up)  52.1 us
    dynamic_slice x72, local copies, waits for them, and re-layouts, add_pair(): pair_id = pair_row[index]  44.5 us
    all_to_all x1, blocking collectives, shards(): lax.all_to_all(middle, 'bins', split_axis=0, concat_axis=2, tiled=True)  30 us
    all_to_all x1, waiting for transfers between devices, shards(): lax.all_to_all(first, 'bins', split_axis=2, concat_axis=0, tiled=True)  26.4 us
  transfers between devices with their start and end apart: 10, of which 5 were waited for; matrix products, arithmetic and copies ran while one was open for 2% of the time, Pallas kernels for 0%

commit v1 on v0

v1 whole, which is shorter than its diff:
```python
import jax
import jax.numpy as jnp
from jax import lax
from jax.experimental import pallas as pl
from jax.experimental.pallas import tpu as pltpu
from jax.sharding import PartitionSpec as P

STEP = 32
GROUP = 16
VMEM = 56 * 2**20


def shifted(value, axis, steps):
    count = lax.axis_size(axis)
    pairs = [(source, (source + steps) % count) for source in range(count)]
    return lax.ppermute(value, axis, pairs)


def params():
    return pltpu.CompilerParams(vmem_limit_bytes=VMEM)


def cost(flops, read):
    return pl.CostEstimate(flops=flops, bytes_accessed=read, transcendentals=0)


def split_rows_kernel(x_ref, low_ref, mid_ref, high_ref, scratch):
    rows, width = x_ref.shape[1], x_ref.shape[2]
    for group in range(STEP // GROUP):
        part = x_ref[pl.ds(group * GROUP, GROUP)].astype(jnp.float32)
        part = part.reshape(GROUP * rows, width)
        for tile in range(width // 128):
            scratch[tile] = part[:, tile * 128 : (tile + 1) * 128]
        for row in range(rows):
            for lane in range(0, width, 128):
                value = scratch[lane // 128, pl.ds(row, GROUP, stride=rows), :].astype(jnp.bfloat16)
                dest, index = (low_ref, row) if row < 2 else (mid_ref, row - 2) if row < 6 else (high_ref, row - 6)
                dest[index, pl.ds(group * GROUP, GROUP), pl.ds(lane, 128)] = value


def split_rows(concen):
    bins, rows, width = concen.shape
    out = lambda n: jax.ShapeDtypeStruct((n, bins, width), concen.dtype)
    spec = lambda n: pl.BlockSpec((n, STEP, width), lambda i: (0, i, 0))
    return pl.pallas_call(
        split_rows_kernel,
        grid=(bins // STEP,),
        in_specs=[pl.BlockSpec((STEP, rows, width), lambda i: (i, 0, 0))],
        out_specs=[spec(2), spec(4), spec(2)],
        out_shape=[out(2), out(4), out(2)],
        scratch_shapes=[pltpu.VMEM((width // 128, GROUP * rows, 128), jnp.float32)],
        compiler_params=params(),
        cost_estimate=cost(0, 4 * bins * rows * width),
        name="split_rows",
    )(concen)


def fill_coefs(coef, rates, first_row, last_row):
    for row in range(first_row, last_row + 1):
        face_x, face_y = rates(0, row), rates(1, row)
        under = rates(0, row - 1)
        left = pltpu.roll(jnp.broadcast_to(face_y, (8, face_y.shape[1])), 1, 1)
        face_x, face_y, under = (jnp.broadcast_to(v, left.shape) for v in (face_x, face_y, under))
        out_y, in_y = jnp.maximum(face_y, 0.0), jnp.minimum(left, 0.0)
        own = 1.0 - jnp.maximum(face_x, 0.0) + jnp.minimum(under, 0.0) - out_y + in_y
        base = 5 * (row - first_row)
        coef[base] = own
        coef[base + 1] = -jnp.minimum(face_x, 0.0)
        coef[base + 2] = jnp.maximum(under, 0.0)
        coef[base + 3] = -jnp.minimum(face_y, 0.0)
        coef[base + 4] = jnp.maximum(left, 0.0)


def substep(coef, base, before, value, after):
    width = value.shape[-1]
    total = coef[base][None] * value + coef[base + 1][None] * after + coef[base + 2][None] * before
    total += coef[base + 3][None] * pltpu.roll(value, width - 1, 2)
    return total + coef[base + 4][None] * pltpu.roll(value, 1, 2)


def two_substeps(coef, first_row, load, rows, store):
    start, stop = rows[0], rows[-1]
    once = {}
    raw = {row: load(row) for row in (start - 2, start - 1)}
    for row in range(start - 1, stop + 2):
        raw[row + 1] = load(row + 1)
        once[row] = substep(coef, 5 * (row - first_row), raw[row - 1], raw[row], raw[row + 1])
        if row - 1 >= start:
            mid = row - 1
            store(mid, substep(coef, 5 * (mid - first_row), once[mid - 1], once[mid], once[mid + 1]))


def as_groups(value):
    return value.astype(jnp.float32).reshape(GROUP // 8, 8, value.shape[-1])


def inner_kernel(rate_ref, low_ref, mid_ref, high_ref, out_ref, coef):
    width = low_ref.shape[2]

    @pl.when(pl.program_id(0) == 0)
    def _():
        fill_coefs(coef, lambda k, row: rate_ref[k, row : row + 1, :], 1, 6)

    def group_step(group, carry):
        at = pl.ds(pl.multiple_of(group * GROUP, GROUP), GROUP)

        def load(row):
            ref, index = (low_ref, row) if row < 2 else (mid_ref, row - 2) if row < 6 else (high_ref, row - 6)
            return as_groups(ref[index, at, :])

        def store(row, value):
            value = value.reshape(GROUP, width).astype(jnp.bfloat16)
            for tile in range(width // 128):
                out_ref[tile, row - 2, at, :] = value[:, tile * 128 : (tile + 1) * 128]

        two_substeps(coef, 1, load, range(2, 6), store)
        return carry

    lax.fori_loop(0, STEP // GROUP, group_step, 0)


def inner_rows(courant, low, mid, high):
    _, bins, width = low.shape
    tiles = width // 128
    spec = lambda n: pl.BlockSpec((n, STEP, width), lambda i: (0, i, 0))
    return pl.pallas_call(
        inner_kernel,
        grid=(bins // STEP,),
        in_specs=[pl.BlockSpec(courant.shape, lambda i: (0, 0, 0)), spec(2), spec(4), spec(2)],
        out_specs=pl.BlockSpec((tiles, 4, STEP, 128), lambda i: (0, 0, i, 0)),
        out_shape=jax.ShapeDtypeStruct((tiles, 4, bins, 128), low.dtype),
        scratch_shapes=[pltpu.VMEM((30, 8, width), jnp.float32)],
        compiler_params=params(),
        cost_estimate=cost(10 * 12 * bins * width, 24 * bins * width),
        name="inner_rows",
    )(courant, low, mid, high)


def all_rates(below_ref, rate_ref, above_ref):
    def rates(k, row):
        if row < 0:
            return below_ref[k, row + 2 : row + 3, :]
        if row > 7:
            return above_ref[k, row - 8 : row - 7, :]
        return rate_ref[k, row : row + 1, :]

    return rates


def outer_kernel(below_ref, rate_ref, above_ref, under_ref, low_ref, mid_ref, high_ref, over_ref, out_ref, coef):
    width = low_ref.shape[2]

    @pl.when(pl.program_id(0) == 0)
    def _():
        fill_coefs(coef, all_rates(below_ref, rate_ref, above_ref), -1, 8)

    def group_step(group, carry):
        at = pl.ds(pl.multiple_of(group * GROUP, GROUP), GROUP)

        def load(row):
            for ref, start, stop in ((under_ref, -2, 0), (low_ref, 0, 2), (mid_ref, 2, 6), (high_ref, 6, 8), (over_ref, 8, 10)):
                if start <= row < stop:
                    return as_groups(ref[row - start, at, :])

        def store(row, value):
            value = value.reshape(GROUP, width).astype(jnp.bfloat16)
            for tile in range(width // 128):
                out_ref[tile, row if row < 2 else row - 4, at, :] = value[:, tile * 128 : (tile + 1) * 128]

        two_substeps(coef, -1, load, range(0, 2), store)
        two_substeps(coef, -1, load, range(6, 8), store)
        return carry

    lax.fori_loop(0, STEP // GROUP, group_step, 0)


def outer_rows(below, courant, above, under, low, mid, high, over):
    _, bins, width = low.shape
    tiles = width // 128
    spec = lambda n: pl.BlockSpec((n, STEP, width), lambda i: (0, i, 0))
    whole = lambda a: pl.BlockSpec(a.shape, lambda i: (0, 0, 0))
    return pl.pallas_call(
        outer_kernel,
        grid=(bins // STEP,),
        in_specs=[whole(below), whole(courant), whole(above), spec(2), spec(2), spec(4), spec(2), spec(2)],
        out_specs=pl.BlockSpec((tiles, 4, STEP, 128), lambda i: (0, 0, i, 0)),
        out_shape=jax.ShapeDtypeStruct((tiles, 4, bins, 128), low.dtype),
        scratch_shapes=[pltpu.VMEM((50, 8, width), jnp.float32)],
        compiler_params=params(),
        cost_estimate=cost(12 * 12 * bins * width, 32 * bins * width),
        name="outer_rows",
    )(below, courant, above, under, low, mid, high, over)


def final_kernel(below_ref, rate_ref, above_ref, under_ref, outer_ref, inner_ref, over_ref, out_ref, coef, scratch):
    tiles = inner_ref.shape[0]
    rows, width = out_ref.shape[1], out_ref.shape[2]

    @pl.when(pl.program_id(0) == 0)
    def _():
        fill_coefs(coef, all_rates(below_ref, rate_ref, above_ref), -1, 8)

    for group in range(STEP // GROUP):
        at = pl.ds(group * GROUP, GROUP)

        def load(row):
            for ref, start, stop, shift in (
                (under_ref, -2, 0, 2),
                (outer_ref, 0, 2, 0),
                (inner_ref, 2, 6, -2),
                (outer_ref, 6, 8, -4),
                (over_ref, 8, 10, -8),
            ):
                if start <= row < stop:
                    return as_groups(jnp.concatenate([ref[tile, row + shift, at, :] for tile in range(tiles)], 1))

        def store(row, value):
            value = value.reshape(GROUP, width)
            for lane in range(0, width, 128):
                scratch[lane // 128, pl.ds(row, GROUP, stride=rows), :] = value[:, lane : lane + 128]

        two_substeps(coef, -1, load, range(0, 8), store)
        part = jnp.concatenate([scratch[tile] for tile in range(tiles)], 1)
        out_ref[at] = part.reshape(GROUP, rows, width).astype(out_ref.dtype)


def final_rows(below, courant, above, under, outer, inner, over):
    tiles, _, bins, lanes = inner.shape
    rows, width = courant.shape[1], tiles * lanes
    spec = lambda n: pl.BlockSpec((tiles, n, STEP, lanes), lambda i: (0, 0, i, 0))
    whole = lambda a: pl.BlockSpec(a.shape, lambda i: (0, 0, 0))
    return pl.pallas_call(
        final_kernel,
        grid=(bins // STEP,),
        in_specs=[whole(below), whole(courant), whole(above), spec(2), spec(4), spec(4), spec(2)],
        out_specs=pl.BlockSpec((STEP, rows, width), lambda i: (i, 0, 0)),
        out_shape=jax.ShapeDtypeStruct((bins, rows, width), inner.dtype),
        scratch_shapes=[
            pltpu.VMEM((50, 8, width), jnp.float32),
            pltpu.VMEM((tiles, GROUP * rows, lanes), jnp.float32),
        ],
        compiler_params=params(),
        cost_estimate=cost(18 * 12 * bins * width, 40 * bins * width),
        name="final_rows",
    )(below, courant, above, under, outer, inner, over)


def coagulate_kernel(pair_ref, count_ref, x_ref, satur_ref, growth_ref, kernel_ref, redist_ref, out_ref, flags, matrix, losses, kept):
    nblocks, rows, size, lanes = x_ref.shape
    bins, cells = nblocks * size, rows * lanes

    def clear(index, carry):
        flags[index] = 0
        return carry

    lax.fori_loop(0, nblocks * nblocks, clear, 0)

    def mark(index, carry):
        flags[pair_ref[index]] = 1
        return carry

    lax.fori_loop(0, count_ref[0], mark, 0)

    def select(source, row):
        for col in range(nblocks):
            live = flags[row * nblocks + col] > 0
            block = source[row, col]
            matrix[:, col * size : (col + 1) * size] = jnp.where(live, block, jnp.zeros_like(block))
        return matrix[...]

    def part(row):
        return jnp.concatenate([x_ref[row, r] for r in range(rows)], 1)

    field = jnp.concatenate([part(row) for row in range(nblocks)], 0)
    for row in range(nblocks):
        collide = jnp.dot(select(kernel_ref, row), field, preferred_element_type=jnp.float32)
        own = part(row).astype(jnp.float32)
        loss = own * collide
        losses[row * size : (row + 1) * size, :] = loss.astype(jnp.bfloat16)
        kept[row * size : (row + 1) * size, :] = own - loss
    satur = jnp.concatenate([satur_ref[r : r + 1, :] for r in range(rows)], 1)
    last = jnp.zeros((1, cells), jnp.float32)
    for row in range(nblocks):
        formed = jnp.dot(select(redist_ref, row), losses[...], preferred_element_type=jnp.float32)
        after = kept[row * size : (row + 1) * size, :] + formed
        growth = jnp.concatenate([growth_ref[row * size : (row + 1) * size, :]] * rows, 1)
        flux = growth * satur * after
        inflow = pltpu.roll(flux, 1, 0)
        at_first = lax.broadcasted_iota(jnp.int32, flux.shape, 0) == 0
        inflow = jnp.where(at_first, last, inflow)
        last = flux[size - 1 : size, :]
        middle = (after - flux + inflow).astype(out_ref.dtype)
        for r in range(rows):
            out_ref[row, r] = middle[:, r * lanes : (r + 1) * lanes]


def coagulate(pair_row, active, x, satur, growth, kernel, redist):
    nblocks, rows, size, lanes = x.shape
    bins, cells = nblocks * size, rows * lanes
    vmem = pl.BlockSpec(memory_space=pltpu.VMEM)
    smem = pl.BlockSpec(memory_space=pltpu.SMEM)
    return pl.pallas_call(
        coagulate_kernel,
        in_specs=[smem, smem, vmem, vmem, vmem, vmem, vmem],
        out_specs=vmem,
        out_shape=jax.ShapeDtypeStruct(x.shape, x.dtype),
        scratch_shapes=[
            pltpu.SMEM((nblocks * nblocks,), jnp.int32),
            pltpu.VMEM((size, bins), kernel.dtype),
            pltpu.VMEM((bins, cells), jnp.bfloat16),
            pltpu.VMEM((bins, cells), jnp.float32),
        ],
        compiler_params=params(),
        cost_estimate=cost(4 * bins * bins * cells, 4 * bins * cells + 4 * bins * bins),
        name="coagulate",
    )(pair_row, active, x, satur, growth, kernel, redist)


def exchange(value):
    return lax.all_to_all(value, "bins", split_axis=0, concat_axis=0, tiled=True)


def shards(concen, courant, saturation, growth, kernel, redist, pair_lists, active_count):
    below = shifted(courant[:, -2:], "cells", 1)
    above = shifted(courant[:, :1], "cells", -1)
    low, mid, high = split_rows(concen)
    under, over = shifted(high, "cells", 1), shifted(low, "cells", -1)
    inner = exchange(inner_rows(courant, low, mid, high))
    outer = exchange(outer_rows(below, courant, above, under, low, mid, high, over))

    tile_id = lax.axis_index("bins") * lax.axis_size("cells") + lax.axis_index("cells")
    pair_row = lax.dynamic_index_in_dim(pair_lists, tile_id, 0, False)
    active = lax.dynamic_slice_in_dim(active_count, tile_id, 1)
    satur_inner = saturation[2:6]
    satur_outer = jnp.concatenate([saturation[:2], saturation[6:]], 0)
    growth_wide = jnp.broadcast_to(growth[:, None], (growth.shape[0], 128))
    inner = coagulate(pair_row, active, inner, satur_inner, growth_wide, kernel, redist)
    outer = coagulate(pair_row, active, outer, satur_outer, growth_wide, kernel, redist)

    outer = exchange(outer)
    inner = exchange(inner)
    under, over = shifted(outer[:, 2:], "cells", 1), shifted(outer[:, :2], "cells", -1)
    return final_rows(below, courant, above, under, outer, inner, over)


def solution(mesh):
    return jax.shard_map(
        shards,
        mesh=mesh,
        in_specs=(
            P("bins", "cells", None),
            P(None, "cells", None),
            P("cells", "bins"),
            P(),
            P(),
            P(),
            P(),
            P(),
        ),
        out_specs=P("bins", "cells", None),
        check_vma=False,
    )
```

time: 857 us -> 125 us (0.15); the launches traced: 844 us -> 124 us
  loops' own time: 235 us -> 0 us
  starting transfers between devices: 189 us -> 31.8 us
  local copies, waits for them, and re-layouts: 154 us -> 6.54 us
  matrix products: 136 us -> 0 us
  other arithmetic: 42.9 us -> 0.59 us
  Pallas kernels: 0 us -> 39.2 us
  blocking collectives: 30 us -> 0 us
  waiting for transfers between devices: 56.1 us -> 46.2 us
    another operation x2 -> x0, loops' own time: 235 us -> none  [block_sum(): return lax.fori_loop(0, active, add_pair, start)]
    ppermute x8 -> x0, starting transfers between devices: 185 us -> none  [the longest x4 133 us: padded(): after = lax.ppermute(initial, axis, down)]
    dot_general x72 -> x0, matrix products: 136 us -> none  [add_pair(): jnp.dot(tile_matrix, source, preferred_element_type=jnp.float32)]
    dynamic_slice x146 -> x2, local copies, waits for them, and re-layouts: 123 us -> 1.29 us  [the longest x1 0.7 us: shards(): pair_row = lax.dynamic_index_in_dim(pair_lists, tile_id, 0, False)]
    pallas_call x0 -> x6, Pallas kernels: none -> 39.2 us  [the longest x2 15.2 us: coagulate(): pl.pallas_call(coagulate_kernel, in_specs=[smem, smem, vmem, vmem, vmem,...]
    add x11 -> x0, other arithmetic: 31.9 us -> none  [the longest x4 12.1 us: advect_rows(): jnp.maximum(face_x, 0.0) * extended[:, :-1]]
    all_to_all x1 -> x0, blocking collectives: 30 us -> none  [shards(): lax.all_to_all(middle, 'bins', split_axis=0, concat_axis=2, tiled=True)]
    ppermute x8 -> x0, waiting for transfers between devices: 21.4 us -> none  [the longest x4 21.3 us: padded(): before = lax.ppermute(last, axis, up)]
  transfers between devices with their start and end apart: 10 -> 10, of which waited for: 5 -> 8; matrix products, arithmetic and copies ran while one was open for 2% -> 4% of each run, Pallas kernels for 0% -> 17%
where the time goes in v1:
time: 125 us; the launch traced here: 124 us
  waiting for transfers between devices  46.2 us (37%)
  Pallas kernels  39.2 us (31%)
  starting transfers between devices  31.8 us (25%)
  local copies, waits for them, and re-layouts  6.54 us (5%)
    all_to_all x4, waiting for transfers between devices, exchange(): lax.all_to_all(value, 'bins', split_axis=0, concat_axis=0, tiled=True)  34.2 us
    ppermute x6, starting transfers between devices, shifted(): return lax.ppermute(value, axis, pairs)  16.6 us
    pallas_call x2, Pallas kernels, coagulate(): pl.pallas_call(coagulate_kernel, in_specs=[smem, smem, vmem, vmem, vmem,...  15.2 us
    all_to_all x4, starting transfers between devices, exchange(): lax.all_to_all(value, 'bins', split_axis=0, concat_axis=0, tiled=True)  15.1 us
    ppermute x6, waiting for transfers between devices, shifted(): return lax.ppermute(value, axis, pairs)  11.9 us
    pallas_call x1, Pallas kernels, final_rows(): pl.pallas_call(final_kernel, grid=(bins // STEP,), in_specs=[whole(below)...  7.88 us
    pallas_call x1, Pallas kernels, outer_rows(): pl.pallas_call(outer_kernel, grid=(bins // STEP,), in_specs=[whole(below)...  6.27 us
    pallas_call x1, Pallas kernels, inner_rows(): pl.pallas_call(inner_kernel, grid=(bins // STEP,), in_specs=[pl.BlockSpec...  5.5 us
  transfers between devices with their start and end apart: 10, of which 8 were waited for; matrix products, arithmetic and copies ran while one was open for 4% of the time, Pallas kernels for 17%

profile of v1, /device:TPU:0, one launch (start us, length us, event | category | flops | bytes accessed | tf_op | source)
XLA Modules:
  0.0 124.4 jit_solution(1406475580421947317)
XLA Ops:
  0.0 0.0 copy-start
  0.0 4.3 %split_rows.1 = (bf16[2,128,1024]{2,1,0:T(8,128)(2,1)}, bf16[4,128,1024]{2,1,0:T(8,128)(2,1)}, bf16[2,128,1024]{2,1,0:T(8,128)(2,1)}) custom-call(bf16[128,8,1024]{2,1,0:T(8,128)(2,1)} %x_ref.1), custom_call_target="tpu_custom_call" | custom-call | bytes 4194304 | tf_op jit(solution)/shard_map/split_rows/pallas_call | solution.py:45
  4.3 1.6 %collective-permute-start.2 = (bf16[2,128,1024]{2,1,0:T(8,128)(2,1)}, bf16[2,128,1024]{2,1,0:T(8,128)(2,1)S(1)}, u32[]{:S(2)}, u32[]{:S(2)}) collective-permute-start(bf16[2,128,1024]{2,1,0:T(8,128)(2,1)} %get-tuple-element.8.high_ref), channel_id=1, source_target_pairs={{0,1},{1,2},{2,3},{3,4},{4,5},{5,6},{6,7},{7,8},{8,9},{9,10},{10,1... | collective-permute-start | bytes 1572872 | tf_op jit(solution)/shard_map/ppermute | solution.py:16
  5.9 4.7 %collective-permute-start.3 = (bf16[2,128,1024]{2,1,0:T(8,128)(2,1)}, bf16[2,128,1024]{2,1,0:T(8,128)(2,1)S(1)}, u32[]{:S(2)}, u32[]{:S(2)}) collective-permute-start(bf16[2,128,1024]{2,1,0:T(8,128)(2,1)} %get-tuple-element.9.low_ref), channel_id=1, source_target_pairs={{0,15},{1,0},{2,1},{3,2},{4,3},{5,4},{6,5},{7,6},{8,7},{9,8},{10,9... | collective-permute-start | bytes 1572872 | tf_op jit(solution)/shard_map/ppermute | solution.py:16
  10.6 0.8 slice.21
  11.5 0.0 collective-permute-start
  11.5 0.8 slice.22
  12.3 5.3 %collective-permute-start.1 = (f32[2,1,1024]{2,1,0:T(1,128)S(1)}, f32[2,1,1024]{2,1,0:T(1,128)S(1)}, u32[]{:S(2)}, u32[]{:S(2)}) collective-permute-start(f32[2,1,1024]{2,1,0:T(1,128)S(1)} %slice.22), channel_id=1, source_target_pairs={{0,15},{1,0},{2,1},{3,2},{4,3},{5,4},{6,5},{7,6},{8,7},{9,8},{10,9... | collective-permute-start | bytes 24584 | tf_op jit(solution)/shard_map/ppermute | solution.py:16
  17.6 4.5 %collective-permute-done.1.above_ref = f32[2,1,1024]{2,1,0:T(1,128)S(1)} collective-permute-done((f32[2,1,1024]{2,1,0:T(1,128)S(1)}, f32[2,1,1024]{2,1,0:T(1,128)S(1)}, u32[]{:S(2)}, u32[]{:S(2)}) %collective-permute-start.1) | collective-permute-done | bytes 8224 | tf_op jit(solution)/shard_map/ppermute | solution.py:16
  22.2 0.0 copy-start.10
  22.2 0.9 collective-permute-done.below_ref
  23.1 0.0 copy-start.9
  23.1 0.0 collective-permute-done.2.under_ref
  23.1 0.0 copy-start.5
  23.1 0.0 collective-permute-done.3.over_ref
  23.1 0.0 copy-start.6
  23.1 0.0 copy-done.10
  23.1 0.6 copy-done.9
  23.7 0.2 copy-done.5
  23.9 0.2 copy-done.6
  24.1 6.3 %outer_rows.1 = bf16[8,4,128,128]{3,2,1,0:T(8,128)(2,1)} custom-call(f32[2,2,1024]{2,1,0:T(2,128)} %copy-done.9, f32[2,8,1024]{2,1,0:T(8,128)} %rate_ref.5, f32[2,1,1024]{2,1,0:T(1,128)} %copy-done.10, bf16[2,128,1024]{2,1,0:T(8,128)(2,1)} %copy-done.5, bf16[2,128,1024]{2,1,0:T(8,128)(2,1)} %get-tuple-element.9.low_ref, ...), custom_call_target="tpu_custom_call" | custom-call | flops 18874368 | bytes 4194304 | tf_op jit(solution)/shard_map/outer_rows/pallas_call | solution.py:182
  30.4 4.5 %all-to-all-start = ((bf16[8,4,128,128]{3,2,1,0:T(8,128)(2,1)}), bf16[8,4,128,128]{3,2,1,0:T(8,128)(2,1)S(1)}, u32[]{:S(2)}, u32[]{:S(2)}) async-start(bf16[8,4,128,128]{3,2,1,0:T(8,128)(2,1)} %outer_rows.1), calls=%async_computation | async-start | bytes 2097152 | tf_op jit(solution)/shard_map/all_to_all | solution.py:320
  34.9 0.0 copy-start.13
  34.9 0.0 copy-start.12
  34.9 0.0 copy-start.11
  34.9 5.5 %inner_rows.1 = bf16[8,4,128,128]{3,2,1,0:T(8,128)(2,1)} custom-call(f32[2,8,1024]{2,1,0:T(8,128)} %rate_ref.5, bf16[2,128,1024]{2,1,0:T(8,128)(2,1)} %get-tuple-element.9.low_ref, bf16[4,128,1024]{2,1,0:T(8,128)(2,1)} %get-tuple-element.10.mid_ref, bf16[2,128,1024]{2,1,0:T(8,128)(2,1)} %get-tuple-element.8.high_ref), custom_call_target="tpu_custom_call" | custom-call | flops 15728640 | bytes 3145728 | tf_op jit(solution)/shard_map/inner_rows/pallas_call | solution.py:126
  40.4 10.4 %all-to-all-done.x_ref = bf16[8,4,128,128]{3,2,1,0:T(8,128)(2,1)S(1)} async-done(((bf16[8,4,128,128]{3,2,1,0:T(8,128)(2,1)}), bf16[8,4,128,128]{3,2,1,0:T(8,128)(2,1)S(1)}, u32[]{:S(2)}, u32[]{:S(2)}) %all-to-all-start) | async-done | bytes 1048608 | tf_op jit(solution)/shard_map/all_to_all | solution.py:320
  50.8 0.0 copy-start.3
  50.8 3.6 %all-to-all-start.2 = ((bf16[8,4,128,128]{3,2,1,0:T(8,128)(2,1)}), bf16[8,4,128,128]{3,2,1,0:T(8,128)(2,1)S(1)}, u32[]{:S(2)}, u32[]{:S(2)}) async-start(bf16[8,4,128,128]{3,2,1,0:T(8,128)(2,1)} %inner_rows.1), calls=%async_computation.2 | async-start | bytes 2097152 | tf_op jit(solution)/shard_map/all_to_all | solution.py:320
  54.4 0.0 copy-done.13
  54.4 0.6 dynamic_slice.8.count_ref
  55.0 0.0 copy-done
  55.0 0.7 dynamic-slice_reduce_fusion.pair_ref
  55.7 0.0 copy-done.12
  55.7 0.6 pad_maximum_fusion.satur_ref
  56.3 0.0 copy-done.11
  56.3 1.0 broadcast_in_dim.2.growth_ref
  57.3 0.0 copy-done.3
  57.3 7.6 %coagulate.2 = bf16[8,4,128,128]{3,2,1,0:T(8,128)(2,1)} custom-call(s32[64]{0:T(128)} %dynamic-slice_reduce_fusion.pair_ref, s32[1]{0:T(128)} %dynamic_slice.8.count_ref, bf16[8,4,128,128]{3,2,1,0:T(8,128)(2,1)} %copy-done.3, f32[4,128]{1,0:T(4,128)} %pad_maximum_fusion.satur_ref, f32[1024,128]{1,0:T(8,128)} %broadcast_in_dim.2.growth_ref, ...), custom_call_target="tpu_custom_call" | custom-call | flops 2147483648 | bytes 6291456 | tf_op jit(solution)/shard_map/coagulate/pallas_call | solution.py:302
  64.9 5.4 %all-to-all-done.2.x_ref = bf16[8,4,128,128]{3,2,1,0:T(8,128)(2,1)S(1)} async-done(((bf16[8,4,128,128]{3,2,1,0:T(8,128)(2,1)}), bf16[8,4,128,128]{3,2,1,0:T(8,128)(2,1)S(1)}, u32[]{:S(2)}, u32[]{:S(2)}) %all-to-all-start.2) | async-done | bytes 1048608 | tf_op jit(solution)/shard_map/all_to_all | solution.py:320
  70.3 0.0 copy-start.4
  70.3 3.6 %all-to-all-start.1 = ((bf16[8,4,128,128]{3,2,1,0:T(8,128)(2,1)}), bf16[8,4,128,128]{3,2,1,0:T(8,128)(2,1)S(1)}, u32[]{:S(2)}, u32[]{:S(2)}) async-start(bf16[8,4,128,128]{3,2,1,0:T(8,128)(2,1)} %coagulate.2), calls=%async_computation.1 | async-start | bytes 2097152 | tf_op jit(solution)/shard_map/all_to_all | solution.py:320
  73.8 0.6 slice.26.satur_ref
  74.4 0.0 copy-done.4
  74.4 7.6 %coagulate.3 = bf16[8,4,128,128]{3,2,1,0:T(8,128)(2,1)} custom-call(s32[64]{0:T(128)} %dynamic-slice_reduce_fusion.pair_ref, s32[1]{0:T(128)} %dynamic_slice.8.count_ref, bf16[8,4,128,128]{3,2,1,0:T(8,128)(2,1)} %copy-done.4, f32[4,128]{1,0:T(4,128)} %slice.26.satur_ref, f32[1024,128]{1,0:T(8,128)} %broadcast_in_dim.2.growth_ref, ...), custom_call_target="tpu_custom_call" | custom-call | flops 2147483648 | bytes 6291456 | tf_op jit(solution)/shard_map/coagulate/pallas_call | solution.py:302
  82.1 7.6 %all-to-all-done.1.outer_ref = bf16[8,4,128,128]{3,2,1,0:T(8,128)(2,1)S(1)} async-done(((bf16[8,4,128,128]{3,2,1,0:T(8,128)(2,1)}), bf16[8,4,128,128]{3,2,1,0:T(8,128)(2,1)S(1)}, u32[]{:S(2)}, u32[]{:S(2)}) %all-to-all-start.1) | async-done | bytes 1048608 | tf_op jit(solution)/shard_map/all_to_all | solution.py:320
  89.7 0.0 copy-start.1
  89.7 3.6 %all-to-all-start.3 = ((bf16[8,4,128,128]{3,2,1,0:T(8,128)(2,1)}), bf16[8,4,128,128]{3,2,1,0:T(8,128)(2,1)S(1)}, u32[]{:S(2)}, u32[]{:S(2)}) async-start(bf16[8,4,128,128]{3,2,1,0:T(8,128)(2,1)} %coagulate.3), calls=%async_computation.3 | async-start | bytes 2097152 | tf_op jit(solution)/shard_map/all_to_all | solution.py:320
  93.3 0.1 fusion
  93.4 0.0 copy-done.1
  93.4 5.0 %collective-permute-start.5 = (bf16[8,2,128,128]{3,2,1,0:T(8,128)(2,1)S(1)}, bf16[8,2,128,128]{3,2,1,0:T(8,128)(2,1)S(1)}, u32[]{:S(2)}, u32[]{:S(2)}) collective-permute-start(bf16[8,2,128,128]{3,2,1,0:T(8,128)(2,1)S(1)} %get-tuple-element.11), channel_id=1, source_target_pairs={{0,15},{1,0},{2,1},{3,2},{4,3},{5,4},{6,5},{7,6},{8,7},{9,8},{10,9... | collective-permute-start | bytes 1572872 | tf_op jit(solution)/shard_map/ppermute | solution.py:16
  98.4 0.0 collective-permute-start.4
  98.4 10.8 %all-to-all-done.3.inner_ref = bf16[8,4,128,128]{3,2,1,0:T(8,128)(2,1)S(1)} async-done(((bf16[8,4,128,128]{3,2,1,0:T(8,128)(2,1)}), bf16[8,4,128,128]{3,2,1,0:T(8,128)(2,1)S(1)}, u32[]{:S(2)}, u32[]{:S(2)}) %all-to-all-start.3) | async-done | bytes 1048608 | tf_op jit(solution)/shard_map/all_to_all | solution.py:320
  109.2 0.0 copy-start.2
  109.2 1.0 collective-permute-done.5.over_ref
  110.2 0.0 copy-start.7
  110.2 5.5 %collective-permute-done.4.under_ref = bf16[8,2,128,128]{3,2,1,0:T(8,128)(2,1)S(1)} collective-permute-done((bf16[8,2,128,128]{3,2,1,0:T(8,128)(2,1)S(1)}, bf16[8,2,128,128]{3,2,1,0:T(8,128)(2,1)S(1)}, u32[]{:S(2)}, u32[]{:S(2)}) %collective-permute-start.4) | collective-permute-done | bytes 524320 | tf_op jit(solution)/shard_map/ppermute | solution.py:16
  115.7 0.0 copy-done.2
  115.7 0.0 copy-done.7
  115.7 0.0 copy-start.8
  115.7 0.8 copy-done.8
  116.5 7.9 %final_rows.1 = bf16[128,8,1024]{2,1,0:T(8,128)(2,1)} custom-call(f32[2,2,1024]{2,1,0:T(2,128)} %copy-done.9, f32[2,8,1024]{2,1,0:T(8,128)} %rate_ref.5, f32[2,1,1024]{2,1,0:T(1,128)} %copy-done.10, bf16[8,2,128,128]{3,2,1,0:T(8,128)(2,1)} %copy-done.8, bf16[8,4,128,128]{3,2,1,0:T(8,128)(2,1)} %copy-done.1, bf16[8,4,128,128]{3,2,1,0:T(8,128)(2,1)} %copy-done.2, ...), custom_call_target="tpu_custom_call" | custom-call | flops 28311552 | bytes 5242880 | tf_op jit(solution)/shard_map/final_rows/pallas_call | solution.py:232
  (1 shorter events, 0.0 us)
Async XLA Ops:
  0.0 55.0 %copy-start = (s32[128,64]{0,1:T(8,128)S(1)}, s32[128,64]{0,1:T(8,128)}, u32[]{:S(2)}) copy-start(s32[128,64]{0,1:T(8,128)} %param.14) | copy-start | bytes 98308
  4.3 18.8 %collective-permute-start.2 = (bf16[2,128,1024]{2,1,0:T(8,128)(2,1)}, bf16[2,128,1024]{2,1,0:T(8,128)(2,1)S(1)}, u32[]{:S(2)}, u32[]{:S(2)}) collective-permute-start(bf16[2,128,1024]{2,1,0:T(8,128)(2,1)} %get-tuple-element.8.high_ref), channel_id=1, source_target_pairs={{0,1},{1,2},{2,3},{3,4},{4,5},{5,6},{6,7},{7,8},{8,9},{9,10},{10,1... | collective-permute-start | bytes 1572872 | tf_op jit(solution)/shard_map/ppermute | solution.py:16
  5.9 17.2 %collective-permute-start.3 = (bf16[2,128,1024]{2,1,0:T(8,128)(2,1)}, bf16[2,128,1024]{2,1,0:T(8,128)(2,1)S(1)}, u32[]{:S(2)}, u32[]{:S(2)}) collective-permute-start(bf16[2,128,1024]{2,1,0:T(8,128)(2,1)} %get-tuple-element.9.low_ref), channel_id=1, source_target_pairs={{0,15},{1,0},{2,1},{3,2},{4,3},{5,4},{6,5},{7,6},{8,7},{9,8},{10,9... | collective-permute-start | bytes 1572872 | tf_op jit(solution)/shard_map/ppermute | solution.py:16
  11.5 11.6 %collective-permute-start = (f32[2,2,1024]{2,1,0:T(2,128)S(1)}, f32[2,2,1024]{2,1,0:T(2,128)S(1)}, u32[]{:S(2)}, u32[]{:S(2)}) collective-permute-start(f32[2,2,1024]{2,1,0:T(2,128)S(1)} %slice.21), channel_id=1, source_target_pairs={{0,1},{1,2},{2,3},{3,4},{4,5},{5,6},{6,7},{7,8},{8,9},{9,10},{10,1... | collective-permute-start | bytes 49160 | tf_op jit(solution)/shard_map/ppermute | solution.py:16
  12.3 9.9 %collective-permute-start.1 = (f32[2,1,1024]{2,1,0:T(1,128)S(1)}, f32[2,1,1024]{2,1,0:T(1,128)S(1)}, u32[]{:S(2)}, u32[]{:S(2)}) collective-permute-start(f32[2,1,1024]{2,1,0:T(1,128)S(1)} %slice.22), channel_id=1, source_target_pairs={{0,15},{1,0},{2,1},{3,2},{4,3},{5,4},{6,5},{7,6},{8,7},{9,8},{10,9... | collective-permute-start | bytes 24584 | tf_op jit(solution)/shard_map/ppermute | solution.py:16
  22.2 0.9 copy-start.10
  23.1 0.6 copy-start.9
  23.1 0.8 copy-start.5
  23.1 1.0 copy-start.6
  30.4 20.4 %all-to-all-start = ((bf16[8,4,128,128]{3,2,1,0:T(8,128)(2,1)}), bf16[8,4,128,128]{3,2,1,0:T(8,128)(2,1)S(1)}, u32[]{:S(2)}, u32[]{:S(2)}) async-start(bf16[8,4,128,128]{3,2,1,0:T(8,128)(2,1)} %outer_rows.1), calls=%async_computation | async-start | bytes 2097152 | tf_op jit(solution)/shard_map/all_to_all | solution.py:320
  34.9 19.5 %copy-start.13 = (s32[128]{0:T(128)S(1)}, s32[128]{0:T(128)}, u32[]{:S(2)}) copy-start(s32[128]{0:T(128)} %param.15) | copy-start | bytes 1540
  34.9 20.8 %copy-start.12 = (f32[8,128]{1,0:T(8,128)S(1)}, f32[8,128]{1,0:T(8,128)}, u32[]{:S(2)}) copy-start(f32[8,128]{1,0:T(8,128)} %param.10) | copy-start | bytes 12292
  34.9 21.4 %copy-start.11 = (f32[1024]{0:T(1024)S(1)}, f32[1024]{0:T(1024)}, u32[]{:S(2)}) copy-start(f32[1024]{0:T(1024)} %param.11) | copy-start | bytes 12292
  50.8 6.5 %copy-start.3 = (bf16[8,4,128,128]{3,2,1,0:T(8,128)(2,1)}, bf16[8,4,128,128]{3,2,1,0:T(8,128)(2,1)S(1)}, u32[]{:S(2)}) copy-start(bf16[8,4,128,128]{3,2,1,0:T(8,128)(2,1)S(1)} %all-to-all-done.x_ref) | copy-start | bytes 3145732
  50.8 19.4 %all-to-all-start.2 = ((bf16[8,4,128,128]{3,2,1,0:T(8,128)(2,1)}), bf16[8,4,128,128]{3,2,1,0:T(8,128)(2,1)S(1)}, u32[]{:S(2)}, u32[]{:S(2)}) async-start(bf16[8,4,128,128]{3,2,1,0:T(8,128)(2,1)} %inner_rows.1), calls=%async_computation.2 | async-start | bytes 2097152 | tf_op jit(solution)/shard_map/all_to_all | solution.py:320
  70.3 4.2 %copy-start.4 = (bf16[8,4,128,128]{3,2,1,0:T(8,128)(2,1)}, bf16[8,4,128,128]{3,2,1,0:T(8,128)(2,1)S(1)}, u32[]{:S(2)}) copy-start(bf16[8,4,128,128]{3,2,1,0:T(8,128)(2,1)S(1)} %all-to-all-done.2.x_ref) | copy-start | bytes 3145732
  70.3 19.4 %all-to-all-start.1 = ((bf16[8,4,128,128]{3,2,1,0:T(8,128)(2,1)}), bf16[8,4,128,128]{3,2,1,0:T(8,128)(2,1)S(1)}, u32[]{:S(2)}, u32[]{:S(2)}) async-start(bf16[8,4,128,128]{3,2,1,0:T(8,128)(2,1)} %coagulate.2), calls=%async_computation.1 | async-start | bytes 2097152 | tf_op jit(solution)/shard_map/all_to_all | solution.py:320
  89.7 3.7 %copy-start.1 = (bf16[8,4,128,128]{3,2,1,0:T(8,128)(2,1)}, bf16[8,4,128,128]{3,2,1,0:T(8,128)(2,1)S(1)}, u32[]{:S(2)}) copy-start(bf16[8,4,128,128]{3,2,1,0:T(8,128)(2,1)S(1)} %all-to-all-done.1.outer_ref) | copy-start | bytes 3145732
  89.7 19.4 %all-to-all-start.3 = ((bf16[8,4,128,128]{3,2,1,0:T(8,128)(2,1)}), bf16[8,4,128,128]{3,2,1,0:T(8,128)(2,1)S(1)}, u32[]{:S(2)}, u32[]{:S(2)}) async-start(bf16[8,4,128,128]{3,2,1,0:T(8,128)(2,1)} %coagulate.3), calls=%async_computation.3 | async-start | bytes 2097152 | tf_op jit(solution)/shard_map/all_to_all | solution.py:320
  93.4 16.7 %collective-permute-start.5 = (bf16[8,2,128,128]{3,2,1,0:T(8,128)(2,1)S(1)}, bf16[8,2,128,128]{3,2,1,0:T(8,128)(2,1)S(1)}, u32[]{:S(2)}, u32[]{:S(2)}) collective-permute-start(bf16[8,2,128,128]{3,2,1,0:T(8,128)(2,1)S(1)} %get-tuple-element.11), channel_id=1, source_target_pairs={{0,15},{1,0},{2,1},{3,2},{4,3},{5,4},{6,5},{7,6},{8,7},{9,8},{10,9... | collective-permute-start | bytes 1572872 | tf_op jit(solution)/shard_map/ppermute | solution.py:16
  98.4 17.3 %collective-permute-start.4 = (bf16[8,2,128,128]{3,2,1,0:T(8,128)(2,1)S(1)}, bf16[8,2,128,128]{3,2,1,0:T(8,128)(2,1)S(1)}, u32[]{:S(2)}, u32[]{:S(2)}) collective-permute-start(bf16[8,2,128,128]{3,2,1,0:T(8,128)(2,1)S(1)} %get-tuple-element.12), channel_id=1, source_target_pairs={{0,1},{1,2},{2,3},{3,4},{4,5},{5,6},{6,7},{7,8},{8,9},{9,10},{10,1... | collective-permute-start | bytes 1572872 | tf_op jit(solution)/shard_map/ppermute | solution.py:16
  109.2 6.5 %copy-start.2 = (bf16[8,4,128,128]{3,2,1,0:T(8,128)(2,1)}, bf16[8,4,128,128]{3,2,1,0:T(8,128)(2,1)S(1)}, u32[]{:S(2)}) copy-start(bf16[8,4,128,128]{3,2,1,0:T(8,128)(2,1)S(1)} %all-to-all-done.3.inner_ref) | copy-start | bytes 3145732
  110.2 5.5 %copy-start.7 = (bf16[8,2,128,128]{3,2,1,0:T(8,128)(2,1)}, bf16[8,2,128,128]{3,2,1,0:T(8,128)(2,1)S(1)}, u32[]{:S(2)}) copy-start(bf16[8,2,128,128]{3,2,1,0:T(8,128)(2,1)S(1)} %collective-permute-done.5.over_ref) | copy-start | bytes 1572868
  115.7 0.8 copy-start.8

commit v2 on v0

v2 whole, which is shorter than its diff:
```python
import functools

import jax
import jax.numpy as jnp
from jax import lax
from jax.experimental import pallas as pl
from jax.experimental.pallas import tpu as pltpu
from jax.sharding import PartitionSpec as P

STEP = 32
CHIPS = 4
ROWS = 8
PACK = 16
MIB = 2**20
SHRINK = 64


def shifted(value, axis, steps):
    count = lax.axis_size(axis)
    pairs = [(source, (source + steps) % count) for source in range(count)]
    return lax.ppermute(value, axis, pairs)


def swapped(value):
    return lax.ppermute(value, "bins", [(i, i ^ 1) for i in range(2 * CHIPS)])


def tied(value, *others):
    return lax.optimization_barrier((value, *others))[0]


def in_hbm(value):
    return pltpu.with_memory_space_constraint(value, pltpu.HBM)


def call(body, name, place, operands, outs, scratch, mib, flops, smem=0, far=()):
    vmem_spec = pl.BlockSpec(memory_space=pltpu.VMEM)
    smem_spec = pl.BlockSpec(memory_space=pltpu.SMEM)
    specs = [smem_spec] * (1 + smem) + [vmem_spec] * (len(operands) - smem)
    operands = list(operands)
    for index in far:
        specs[1 + index] = pl.BlockSpec(memory_space=pl.ANY)
        operands[index] = in_hbm(operands[index])
    moved = sum(a.size * a.dtype.itemsize for a in (*operands, *outs))
    return pl.pallas_call(
        body,
        in_specs=specs,
        out_specs=[vmem_spec] * len(outs),
        out_shape=outs,
        scratch_shapes=scratch,
        compiler_params=pltpu.CompilerParams(vmem_limit_bytes=mib * MIB),
        cost_estimate=pl.CostEstimate(flops=flops // SHRINK, bytes_accessed=moved // SHRINK, transcendentals=0),
        name=name,
    )(place, *operands)


def steps(bins, body):
    def step(index, carry):
        body(pl.multiple_of(index * STEP, STEP))
        return carry

    lax.fori_loop(0, bins // STEP, step, 0)


def struct(shape, dtype):
    return jax.ShapeDtypeStruct(shape, dtype)


def rows_first(picked):
    shape = (len(picked) * STEP, STEP * ROWS)
    out = lax.broadcasted_iota(jnp.int32, shape, 0)
    inp = lax.broadcasted_iota(jnp.int32, shape, 1)
    slot, bin_of = out // STEP, out % STEP
    row = slot
    for index, value in enumerate(picked):
        row = jnp.where(slot == index, value, row)
    return jnp.where(inp == bin_of * ROWS + row, 1.0, 0.0).astype(jnp.bfloat16)


def bins_first():
    shape = (STEP * ROWS, ROWS * STEP)
    out = lax.broadcasted_iota(jnp.int32, shape, 0)
    inp = lax.broadcasted_iota(jnp.int32, shape, 1)
    return jnp.where(inp == (out % ROWS) * STEP + out // ROWS, 1.0, 0.0).astype(jnp.bfloat16)


def thirds(value):
    high = value.astype(jnp.bfloat16)
    rest = value - high.astype(jnp.float32)
    mid = rest.astype(jnp.bfloat16)
    low = (rest - mid.astype(jnp.float32)).astype(jnp.bfloat16)
    return [v.astype(jnp.float32) for v in (high, mid, low)]


def packed(rows):
    parts = [part for row in rows for part in thirds(row)]
    parts.append(jnp.zeros((PACK - len(parts), rows[0].shape[1]), jnp.float32))
    return jnp.concatenate(parts, 0).astype(jnp.bfloat16)


def unpacked(halo_ref, index):
    parts = halo_ref[0, halo_ref.shape[1] - PACK :, :].astype(jnp.float32)[3 * index : 3 * index + 3]
    return parts[0:1] + parts[1:2] + parts[2:3]


def edge_kernel(place_ref, source_ref, far_rate_ref, low_ref, high_ref, x_ref, rate_ref, onehot, sems, rate_sem):
    bins, width = low_ref.shape[1] - PACK, x_ref.shape[1]
    size = STEP * ROWS
    part_at = lambda index: pl.ds(index * size, size)
    copies = [
        pltpu.make_async_copy(source_ref.at[part_at(i)], x_ref.at[part_at(i)], sems.at[i]) for i in range(bins // STEP)
    ]
    rates_in = pltpu.make_async_copy(far_rate_ref, rate_ref, rate_sem)
    for copy in copies:
        copy.start()
    rates_in.start()
    onehot[...] = rows_first((0, 1, 6, 7))
    for index, copy in enumerate(copies):
        copy.wait()
        at = slice(index * STEP, (index + 1) * STEP)
        for lane in range(0, width, 256):
            lanes = slice(lane, lane + 256)
            part = jnp.dot(onehot[...], x_ref[part_at(index), lanes], preferred_element_type=jnp.float32)
            part = part.astype(jnp.bfloat16)
            for row in range(2):
                low_ref[row, at, lanes] = part[row * STEP : (row + 1) * STEP]
                high_ref[row, at, lanes] = part[(row + 2) * STEP : (row + 3) * STEP]
    rates_in.wait()
    low_ref[0, bins:, :] = packed([rate_ref[0, 0:1, :], rate_ref[1, 0:1, :]])
    high_ref[0, bins:, :] = packed([rate_ref[0, 6:7, :], rate_ref[0, 7:8, :], rate_ref[1, 7:8, :]])
    low_ref[1, bins:, :] = jnp.zeros((PACK, width), low_ref.dtype)
    high_ref[1, bins:, :] = jnp.zeros((PACK, width), low_ref.dtype)


def edge_rows(place, flat, courant):
    width, bins = flat.shape[1], flat.shape[0] // ROWS
    edge = struct((2, bins + PACK, width), flat.dtype)
    outs = [edge, edge, struct(flat.shape, flat.dtype), struct(courant.shape, courant.dtype)]
    scratch = [
        pltpu.VMEM((4 * STEP, STEP * ROWS), jnp.bfloat16),
        pltpu.SemaphoreType.DMA((bins // STEP,)),
        pltpu.SemaphoreType.DMA(()),
    ]
    return call(edge_kernel, "edge_rows", place, (flat, courant), outs, scratch, 8, 8 * STEP * flat.size, far=(0, 1))


def fill_coefs(coef, rates, first_row, last_row):
    for row in range(first_row, last_row + 1):
        face_x, face_y, under = rates(0, row), rates(1, row), rates(0, row - 1)
        face_x, face_y, under = (jnp.broadcast_to(v, (8, v.shape[1])) for v in (face_x, face_y, under))
        left = pltpu.roll(face_y, 1, 1)
        base = 5 * (row - first_row)
        own = 1.0 - jnp.maximum(face_x, 0.0) + jnp.minimum(under, 0.0)
        coef[base] = own - jnp.maximum(face_y, 0.0) + jnp.minimum(left, 0.0)
        coef[base + 1] = -jnp.minimum(face_x, 0.0)
        coef[base + 2] = jnp.maximum(under, 0.0)
        coef[base + 3] = -jnp.minimum(face_y, 0.0)
        coef[base + 4] = jnp.maximum(left, 0.0)


def substep(coef, base, before, value, after):
    width = value.shape[-1]
    total = coef[base][None] * value + coef[base + 1][None] * after + coef[base + 2][None] * before
    total += coef[base + 3][None] * pltpu.roll(value, width - 1, 2)
    return total + coef[base + 4][None] * pltpu.roll(value, 1, 2)


def two_substeps(coef, first_row, load, rows, store):
    start, stop = rows[0], rows[-1]
    once = {}
    raw = {row: load(row) for row in (start - 2, start - 1)}
    for row in range(start - 1, stop + 2):
        raw[row + 1] = load(row + 1)
        once[row] = substep(coef, 5 * (row - first_row), raw[row - 1], raw[row], raw[row + 1])
        if row - 1 >= start:
            mid = row - 1
            store(mid, substep(coef, 5 * (mid - first_row), once[mid - 1], once[mid], once[mid + 1]))


def grouped(value):
    return value.astype(jnp.float32).reshape(STEP // 8, 8, value.shape[-1])


def transpose_in(onehot, x_ref, field, start):
    width = x_ref.shape[1]
    source = pl.ds(pl.multiple_of(start * ROWS, STEP * ROWS), STEP * ROWS)
    for lane in range(0, width, 256):
        part = jnp.dot(onehot[...], x_ref[source, lane : lane + 256], preferred_element_type=jnp.float32)
        field[:, :, lane : lane + 256] = part.reshape(ROWS, STEP, 256)


def inner_kernel(place_ref, rate_ref, x_ref, out0, out1, out2, out3, coef, onehot, field, tiles):
    onehot[...] = rows_first(range(ROWS))
    fill_coefs(coef, lambda k, row: rate_ref[k, row : row + 1, :], 1, 6)

    def step(start):
        transpose_in(onehot, x_ref, field, start)
        load = lambda row: grouped(field[row])
        store = lambda row, value: send_row(place_ref, tiles, (out0, out1, out2, out3), row - 2, start, value)
        two_substeps(coef, 1, load, range(2, 6), store)

    steps(out0.shape[2], step)


def send_row(place_ref, tiles, outs, slot, start, value):
    value = value.reshape(STEP, value.shape[-1]).astype(jnp.bfloat16)
    for tile in range(2 * CHIPS):
        tiles[tile] = value[:, tile * 128 : (tile + 1) * 128]
    for away, out_ref in enumerate(outs):
        chip = lax.rem(place_ref[0] + away, CHIPS)
        for core in range(2):
            out_ref[core, slot, pl.ds(start, STEP), :] = tiles[2 * chip + core]


def first_scratch(coefs, width, dtype):
    return [
        pltpu.VMEM((5 * coefs, 8, width), jnp.float32),
        pltpu.VMEM((ROWS * STEP, ROWS * STEP), jnp.bfloat16),
        pltpu.VMEM((ROWS, STEP, width), jnp.float32),
        pltpu.VMEM((2 * CHIPS, STEP, 128), dtype),
    ]


def inner_rows(place, courant, flat):
    width, bins = flat.shape[1], flat.shape[0] // ROWS
    outs = [struct((2, 4, bins, 128), flat.dtype)] * CHIPS
    scratch = first_scratch(6, width, flat.dtype)
    return call(inner_kernel, "inner_rows", place, (courant, flat), outs, scratch, 12, 120 * bins * width)


def all_rates(below_ref, rate_ref, above_ref):
    def rates(k, row):
        if row < 0:
            return unpacked(below_ref, row + 2 + k)
        if row > 7:
            return unpacked(above_ref, k)
        return rate_ref[k, row : row + 1, :]

    return rates


def outer_kernel(place_ref, rate_ref, under_ref, x_ref, over_ref, out0, out1, out2, out3, coef, onehot, field, tiles):
    onehot[...] = rows_first(range(ROWS))
    fill_coefs(coef, all_rates(under_ref, rate_ref, over_ref), -1, 8)

    def step(start):
        transpose_in(onehot, x_ref, field, start)

        def load(row):
            if row < 0:
                return grouped(under_ref[row + 2, pl.ds(start, STEP), :])
            if row > 7:
                return grouped(over_ref[row - 8, pl.ds(start, STEP), :])
            return grouped(field[row])

        def store(row, value):
            send_row(place_ref, tiles, (out0, out1, out2, out3), row if row < 2 else row - 4, start, value)

        two_substeps(coef, -1, load, range(0, 2), store)
        two_substeps(coef, -1, load, range(6, 8), store)

    steps(out0.shape[2], step)


def outer_rows(place, courant, under, flat, over):
    width, bins = flat.shape[1], flat.shape[0] // ROWS
    outs = [struct((2, 4, bins, 128), flat.dtype)] * CHIPS
    scratch = first_scratch(10, width, flat.dtype)
    operands = (courant, under, flat, over)
    return call(outer_kernel, "outer_rows", place, operands, outs, scratch, 12, 144 * bins * width)


def arrived_kernel(place_ref, *refs):
    slots, (low_ref, high_ref) = refs[:8], refs[8:]
    core = place_ref[1]
    for away in range(CHIPS):
        for other in range(2):
            tile = 2 * lax.rem(place_ref[0] + away, CHIPS) + lax.bitwise_xor(core, other)
            lanes = pl.ds(pl.multiple_of(tile * 128, 128), 128)
            for row in range(2):
                low_ref[row, :, lanes] = slots[2 * away + other][core, row]
                high_ref[row, :, lanes] = slots[2 * away + other][core, row + 2]


def arrived_rows(place, slots):
    _, _, bins, lanes = slots[0].shape
    outs = [struct((2, bins, 2 * CHIPS * lanes), slots[0].dtype)] * 2
    return call(arrived_kernel, "arrived_rows", place, slots, outs, [], 4, 0)


def final_kernel(place_ref, first_under, rate_ref, first_over, under_ref, low_ref, high_ref, over_ref, *refs):
    slots, (out_ref, coef, onehot, tiles, back) = refs[:8], refs[8:]
    width = out_ref.shape[1]
    core = place_ref[1]
    onehot[...] = bins_first()
    fill_coefs(coef, all_rates(first_under, rate_ref, first_over), -1, 8)

    def step(start):
        at = pl.ds(start, STEP)
        for away in range(CHIPS):
            for other in range(2):
                tile = 2 * lax.rem(place_ref[0] + away, CHIPS) + lax.bitwise_xor(core, other)
                for row in range(4):
                    tiles[tile, row] = slots[2 * away + other][core, row, at, :]

        def load(row):
            for ref, first, stop in ((under_ref, -2, 0), (low_ref, 0, 2), (high_ref, 6, 8), (over_ref, 8, 10)):
                if first <= row < stop:
                    return grouped(ref[row - first, at, :])
            return grouped(jnp.concatenate([tiles[tile, row - 2] for tile in range(2 * CHIPS)], 1))

        def store(row, value):
            back[row * STEP : (row + 1) * STEP, :] = value.reshape(STEP, width).astype(jnp.bfloat16)

        two_substeps(coef, -1, load, range(ROWS), store)
        target = pl.ds(pl.multiple_of(start * ROWS, STEP * ROWS), STEP * ROWS)
        for lane in range(0, width, 256):
            part = jnp.dot(onehot[...], back[:, lane : lane + 256], preferred_element_type=jnp.float32)
            out_ref[target, lane : lane + 256] = part.astype(out_ref.dtype)

    steps(low_ref.shape[1], step)


def final_rows(place, courant, first_under, first_over, under, low, slots, high, over):
    _, bins, width = low.shape
    scratch = [
        pltpu.VMEM((50, 8, width), jnp.float32),
        pltpu.VMEM((ROWS * STEP, ROWS * STEP), jnp.bfloat16),
        pltpu.VMEM((2 * CHIPS, 4, STEP, 128), low.dtype),
        pltpu.VMEM((ROWS * STEP, width), low.dtype),
    ]
    operands = (first_under, courant, first_over, under, low, high, over, *slots)
    outs = [struct((bins * ROWS, width), low.dtype)]
    return call(final_kernel, "final_rows", place, operands, outs, scratch, 12, 216 * bins * width)[0]


def block_of(place_ref, away, other):
    return 2 * lax.rem(place_ref[0] + CHIPS - away, CHIPS) + lax.bitwise_xor(place_ref[1], other)


def matrices_kernel(place_ref, pair_ref, count_ref, growth_ref, far_kernel, far_redist, first_ref, second_ref, wide_ref, flags, kernel_ref, redist_ref, sems):
    nblocks, size = kernel_ref.shape[0], kernel_ref.shape[2]
    tile = place_ref[2]
    count = count_ref[tile]

    def copies(slot):
        row = block_of(place_ref, slot // 2, lax.rem(slot, 2))
        return [
            pltpu.make_async_copy(far.at[row], near.at[row], sems.at[side, slot])
            for side, (far, near) in enumerate(((far_kernel, kernel_ref), (far_redist, redist_ref)))
        ]

    for slot in range(nblocks):
        for copy in copies(slot):
            copy.start()
    for index in range(nblocks * nblocks):
        flags[pair_ref[tile, index]] = jnp.where(index < count, 1, 0)
    blocks = [block_of(place_ref, away, other) for away in range(CHIPS) for other in range(2)]

    def row_step(slot, carry):
        row = block_of(place_ref, slot // 2, lax.rem(slot, 2))
        at = pl.ds(pl.multiple_of(slot * size, size), size)
        for copy in copies(slot):
            copy.wait()
        for index, col in enumerate(blocks):
            live = flags[row * nblocks + col] > 0
            lanes = slice(index * size, (index + 1) * size)
            for source, dest in ((kernel_ref, first_ref), (redist_ref, second_ref)):
                block = source[row, col]
                dest[at, lanes] = jnp.where(live, block, jnp.zeros_like(block))
        wide_ref[at, :] = jnp.broadcast_to(growth_ref[pl.ds(row, 1), :], (size, size)).T
        return carry

    lax.fori_loop(0, nblocks, row_step, 0)


def matrices(place, pair_lists, active_count, growth, kernel, redist):
    nblocks, size = kernel.shape[0], kernel.shape[2]
    bins = nblocks * size
    matrix = struct((bins, bins), kernel.dtype)
    outs = [matrix, matrix, struct((bins, size), jnp.float32)]
    operands = (pair_lists, active_count, growth, kernel, redist)
    scratch = [
        pltpu.SMEM((nblocks * nblocks,), jnp.int32),
        pltpu.VMEM(kernel.shape, kernel.dtype),
        pltpu.VMEM(redist.shape, redist.dtype),
        pltpu.SemaphoreType.DMA((2, nblocks)),
    ]
    return call(matrices_kernel, "matrices", place, operands, outs, scratch, 8, 0, smem=2, far=(3, 4))


def coagulate_kernel(picked, place_ref, satur_ref, growth_ref, first_ref, second_ref, *refs):
    slots, outs, (field, losses, kept, moved) = refs[:8], refs[8:12], refs[12:]
    rows, size, lanes = slots[0].shape[1:]
    bins, cells = field.shape
    chip, core = place_ref[0], place_ref[1]
    half = bins // 2
    blocks = [block_of(place_ref, away, other) for away in range(CHIPS) for other in range(2)]
    for slot in range(2 * CHIPS):
        for r in range(rows):
            field[slot * size : (slot + 1) * size, r * lanes : (r + 1) * lanes] = slots[slot][core, r]
    for start in (0, half):
        at = slice(start, start + half)
        collide = jnp.dot(first_ref[at, :], field[...], preferred_element_type=jnp.float32)
        own = field[at, :].astype(jnp.float32)
        loss = own * collide
        losses[at, :] = loss.astype(jnp.bfloat16)
        kept[at, :] = own - loss
    satur = jnp.concatenate([satur_ref[r : r + 1, :] for r in picked], 1)
    for start in (0, half):
        at = slice(start, start + half)
        formed = jnp.dot(second_ref[at, :], losses[...], preferred_element_type=jnp.float32)
        after = kept[at, :] + formed
        growth = jnp.concatenate([growth_ref[at, :]] * rows, 1)
        flux = growth * satur * after
        kept[at, :] = after - flux
        moved[at, :] = flux
    for slot in range(2 * CHIPS):
        away, other = divmod(slot, 2)
        block = blocks[slot]
        below = lax.rem(block + 2 * CHIPS - 1, 2 * CHIPS)
        source = 2 * lax.rem(chip + CHIPS - below // 2, CHIPS) + lax.bitwise_xor(lax.rem(below, 2), core)
        last = moved[pl.ds(pl.multiple_of(source * size + size - 8, 8), 8), :][7:8, :]
        last = jnp.where(block > 0, last, jnp.zeros_like(last))
        at = slice(slot * size, (slot + 1) * size)
        inflow = pltpu.roll(moved[at, :], 1, 0)
        inflow = jnp.where(lax.broadcasted_iota(jnp.int32, inflow.shape, 0) == 0, last, inflow)
        middle = (kept[at, :] + inflow).astype(jnp.bfloat16)
        for r in range(rows):
            outs[away][lax.bitwise_xor(core, other), r] = middle[:, r * lanes : (r + 1) * lanes]


def coagulate(picked, place, satur, growth, first, second, slots):
    _, rows, size, lanes = slots[0].shape
    bins, cells = 2 * CHIPS * size, rows * lanes
    outs = [struct(slots[0].shape, slots[0].dtype)] * CHIPS
    scratch = [
        pltpu.VMEM((bins, cells), jnp.bfloat16),
        pltpu.VMEM((bins, cells), jnp.bfloat16),
        pltpu.VMEM((bins, cells), jnp.float32),
        pltpu.VMEM((bins, cells), jnp.float32),
    ]
    body = functools.partial(coagulate_kernel, picked)
    operands = (satur, growth, first, second, *slots)
    return call(body, "coagulate", place, operands, outs, scratch, 16, 4 * bins * bins * cells)


def travel(parts, direction):
    return [parts[0]] + [shifted(parts[away], "bins", 2 * direction * away) for away in range(1, CHIPS)]


def with_other_core(parts):
    slots = []
    for part in parts:
        slots += [part, swapped(part)]
    return slots


def shards(concen, courant, saturation, growth, kernel, redist, pair_lists, active_count):
    bins, rows, width = concen.shape
    device = lax.axis_index("bins")
    tile_id = device * lax.axis_size("cells") + lax.axis_index("cells")
    place = jnp.stack([device // 2, device % 2, tile_id]).astype(jnp.int32)
    flat = concen.reshape(bins * rows, width)
    low, high, flat, courant = edge_rows(place, flat, courant)
    first_under, first_over = shifted(high, "cells", 1), shifted(low, "cells", -1)
    inner = inner_rows(place, courant, tied(flat, low))
    growth = growth.reshape(2 * CHIPS, bins)
    first, second, growth = matrices(tied(place, inner[0]), pair_lists, active_count, growth, kernel, redist)
    outer = outer_rows(place, courant, first_under, tied(flat, inner[0], first), first_over)
    inner_slots = with_other_core([tied(part, outer[0]) for part in travel(inner, 1)])
    inner = coagulate((2, 3, 4, 5), place, saturation, growth, first, second, inner_slots)
    outer_slots = with_other_core([tied(part, inner[0]) for part in travel(outer, 1)])
    outer = coagulate((0, 1, 6, 7), place, saturation, growth, first, second, outer_slots)

    outer_slots = with_other_core(travel(outer, -1))
    inner_slots = with_other_core(travel([tied(part, outer[0]) for part in inner], -1))
    low, high = arrived_rows(place, outer_slots)
    under, over = shifted(high, "cells", 1), shifted(low, "cells", -1)
    out = final_rows(place, courant, first_under, first_over, under, low, inner_slots, high, over)
    return out.reshape(bins, rows, width)


def solution(mesh):
    return jax.shard_map(
        shards,
        mesh=mesh,
        in_specs=(
            P("bins", "cells", None),
            P(None, "cells", None),
            P("cells", "bins"),
            P(),
            P(),
            P(),
            P(),
            P(),
        ),
        out_specs=P("bins", "cells", None),
        check_vma=False,
    )
```

time: 857 us -> 100 us (0.12); the launches traced: 844 us -> 99.8 us
  loops' own time: 235 us -> 0 us
  starting transfers between devices: 189 us -> 28.9 us
  local copies, waits for them, and re-layouts: 154 us -> 0.84 us
  matrix products: 136 us -> 0 us
  other arithmetic: 42.9 us -> 0.08 us
  Pallas kernels: 0 us -> 35.3 us
  blocking collectives: 30 us -> 0 us
  waiting for transfers between devices: 56.1 us -> 34.6 us
    another operation x2 -> x0, loops' own time: 235 us -> none  [block_sum(): return lax.fori_loop(0, active, add_pair, start)]
    ppermute x8 -> x16, starting transfers between devices: 185 us -> 2.22 us  [swapped(): return lax.ppermute(value, 'bins', [(i, i ^ 1) for i in range(2 * CHIPS)])]
    dot_general x72 -> x0, matrix products: 136 us -> none  [add_pair(): jnp.dot(tile_matrix, source, preferred_element_type=jnp.float32)]
    dynamic_slice x146 -> x0, local copies, waits for them, and re-layouts: 123 us -> none  [the longest x72 77.9 us: add_pair(): current = lax.dynamic_index_in_dim(totals, row_block, 0, False)]
    pallas_call x0 -> x8, Pallas kernels: none -> 35.3 us  [call(): pl.pallas_call(body, in_specs=specs, out_specs=[vmem_spec] * len(outs), o...]
    add x11 -> x0, other arithmetic: 31.9 us -> none  [the longest x4 12.1 us: advect_rows(): jnp.maximum(face_x, 0.0) * extended[:, :-1]]
    all_to_all x1 -> x0, blocking collectives: 30 us -> none  [shards(): lax.all_to_all(middle, 'bins', split_axis=0, concat_axis=2, tiled=True)]
    ppermute x1 -> x16, starting transfers between devices: 0.07 us -> 26.6 us  [shifted(): return lax.ppermute(value, axis, pairs)]
  transfers between devices with their start and end apart: 10 -> 32, of which waited for: 5 -> 13; matrix products, arithmetic and copies ran while one was open for 2% -> 0% of each run, Pallas kernels for 0% -> 20%
where the time goes in v2:
time: 100 us; the launch traced here: 99.8 us
  Pallas kernels  35.3 us (35%)
  waiting for transfers between devices  34.6 us (35%)
  starting transfers between devices  28.9 us (29%)
    pallas_call x8, Pallas kernels, call(): pl.pallas_call(body, in_specs=specs, out_specs=[vmem_spec] * len(outs), o...  35.3 us
    ppermute x16, waiting for transfers between devices, shifted(): return lax.ppermute(value, axis, pairs)  31.6 us
    ppermute x16, starting transfers between devices, shifted(): return lax.ppermute(value, axis, pairs)  26.6 us
    ppermute x16, waiting for transfers between devices, swapped(): return lax.ppermute(value, 'bins', [(i, i ^ 1) for i in range(2 * CHIPS)])  3.07 us
    ppermute x16, starting transfers between devices, swapped(): return lax.ppermute(value, 'bins', [(i, i ^ 1) for i in range(2 * CHIPS)])  2.22 us
  transfers between devices with their start and end apart: 32, of which 13 were waited for; matrix products, arithmetic and copies ran while one was open for 0% of the time, Pallas kernels for 20%

profile of v2, /device:TPU:0, one launch (start us, length us, event | category | flops | bytes accessed | tf_op | source)
XLA Modules:
  0.0 99.8 jit_solution(4379364905334864725)
XLA Ops:
  0.0 0.1 pad_add_fusion.place_ref
  0.1 3.7 %edge_rows.1 = (bf16[2,144,1024]{2,1,0:T(8,128)(2,1)}, bf16[2,144,1024]{2,1,0:T(8,128)(2,1)}, bf16[1024,1024]{1,0:T(8,128)(2,1)S(1)}, f32[2,8,1024]{2,1,0:T(8,128)S(1)}) custom-call(s32[3]{0:T(128)S(1)} %pad_add_fusion.place_ref, bf16[1024,1024]{1,0:T(8,128)(2,1)} %bitcast.7, f32[2,8,1024]{2,1,0:T(8,128)} %far_rate_ref.1), custom_call_target="tpu_custom_call" | custom-call | flops 4194304 | bytes 86016 | tf_op jit(solution)/shard_map/edge_rows/pallas_call | solution.py:45
  3.8 1.6 %collective-permute-start = (bf16[2,144,1024]{2,1,0:T(8,128)(2,1)}, bf16[2,144,1024]{2,1,0:T(8,128)(2,1)S(1)}, u32[]{:S(2)}, u32[]{:S(2)}) collective-permute-start(bf16[2,144,1024]{2,1,0:T(8,128)(2,1)} %get-tuple-element.45), channel_id=1, source_target_pairs={{0,1},{1,2},{2,3},{3,4},{4,5},{5,6},{6,7},{7,8},{8,9},{9,10},{10,1... | collective-permute-start | bytes 1769480 | tf_op jit(solution)/shard_map/ppermute | solution.py:21
  5.4 4.8 %collective-permute-start.1 = (bf16[2,144,1024]{2,1,0:T(8,128)(2,1)}, bf16[2,144,1024]{2,1,0:T(8,128)(2,1)S(1)}, u32[]{:S(2)}, u32[]{:S(2)}) collective-permute-start(bf16[2,144,1024]{2,1,0:T(8,128)(2,1)} %get-tuple-element.47), channel_id=1, source_target_pairs={{0,15},{1,0},{2,1},{3,2},{4,3},{5,4},{6,5},{7,6},{8,7},{9,8},{10,9... | collective-permute-start | bytes 1769480 | tf_op jit(solution)/shard_map/ppermute | solution.py:21
  10.2 5.8 %inner_rows.1 = (bf16[2,4,128,128]{3,2,1,0:T(8,128)(2,1)S(1)}, bf16[2,4,128,128]{3,2,1,0:T(8,128)(2,1)}, bf16[2,4,128,128]{3,2,1,0:T(8,128)(2,1)}, bf16[2,4,128,128]{3,2,1,0:T(8,128)(2,1)}) custom-call(s32[3]{0:T(128)S(1)} %pad_add_fusion.place_ref, f32[2,8,1024]{2,1,0:T(8,128)S(1)} %get-tuple-element.46.rate_ref, bf16[1024,1024]{1,0:T(8,128)(2,1)S(1)} %get-tuple-element.55.x_ref), custom_call_target="tpu_custom_call" | custom-call | flops 245760 | bytes 50176 | tf_op jit(solution)/shard_map/inner_rows/pallas_call | solution.py:45
  16.0 0.7 copy-done
  16.7 1.6 %collective-permute-start.3 = (bf16[2,4,128,128]{3,2,1,0:T(8,128)(2,1)}, bf16[2,4,128,128]{3,2,1,0:T(8,128)(2,1)}, u32[]{:S(2)}, u32[]{:S(2)}) collective-permute-start(bf16[2,4,128,128]{3,2,1,0:T(8,128)(2,1)} %get-tuple-element.58), channel_id=1, source_target_pairs={{0,32},{16,48},{32,64},{48,80},{64,96},{80,112},{96,0},{112,16},{1... | collective-permute-start | bytes 786440 | tf_op jit(solution)/shard_map/ppermute | solution.py:21
  18.3 1.7 %collective-permute-start.7 = (bf16[2,4,128,128]{3,2,1,0:T(8,128)(2,1)}, bf16[2,4,128,128]{3,2,1,0:T(8,128)(2,1)}, u32[]{:S(2)}, u32[]{:S(2)}) collective-permute-start(bf16[2,4,128,128]{3,2,1,0:T(8,128)(2,1)} %get-tuple-element.62), channel_id=1, source_target_pairs={{0,96},{16,112},{32,0},{48,16},{64,32},{80,48},{96,64},{112,80},{1... | collective-permute-start | bytes 786440 | tf_op jit(solution)/shard_map/ppermute | solution.py:21
  20.0 2.0 %collective-permute-start.5 = (bf16[2,4,128,128]{3,2,1,0:T(8,128)(2,1)}, bf16[2,4,128,128]{3,2,1,0:T(8,128)(2,1)}, u32[]{:S(2)}, u32[]{:S(2)}) collective-permute-start(bf16[2,4,128,128]{3,2,1,0:T(8,128)(2,1)} %get-tuple-element.60), channel_id=1, source_target_pairs={{0,64},{16,80},{32,96},{48,112},{64,0},{80,16},{96,32},{112,48},{1... | collective-permute-start | bytes 786440 | tf_op jit(solution)/shard_map/ppermute | solution.py:21
  21.9 0.1 copy.9.pair_ref
  22.1 4.3 %matrices.1 = (bf16[1024,1024]{1,0:T(8,128)(2,1)S(1)}, bf16[1024,1024]{1,0:T(8,128)(2,1)S(1)}, f32[1024,128]{1,0:T(8,128)S(1)}) custom-call(s32[3]{0:T(128)S(1)} %pad_add_fusion.place_ref, s32[128,64]{1,0:T(8,128)S(1)} %copy.9.pair_ref, s32[128]{0:T(128)S(1)} %copy-done.4, f32[8,128]{1,0:T(8,128)S(1)} %bitcast.6, bf16[8,8,128,128]{3,2,1,0:T(8,128)(2,1)} %far_kernel.1, ...), custom_call_target="tpu_custom_call" | custom-call | bytes 139848 | tf_op jit(solution)/shard_map/matrices/pallas_call | solution.py:45
  26.4 0.0 copy-start.2
  26.4 0.0 collective-permute-done.under_ref.first_under
  26.4 0.0 collective-permute-done.1.over_ref.first_over
  26.4 5.2 %outer_rows.1 = (bf16[2,4,128,128]{3,2,1,0:T(8,128)(2,1)S(1)}, bf16[2,4,128,128]{3,2,1,0:T(8,128)(2,1)S(1)}, bf16[2,4,128,128]{3,2,1,0:T(8,128)(2,1)S(1)}, bf16[2,4,128,128]{3,2,1,0:T(8,128)(2,1)S(1)}) custom-call(s32[3]{0:T(128)S(1)} %pad_add_fusion.place_ref, f32[2,8,1024]{2,1,0:T(8,128)S(1)} %get-tuple-element.46.rate_ref, ...), custom_call_target="tpu_custom_call" | custom-call | flops 294912 | bytes 68608 | tf_op jit(solution)/shard_map/outer_rows/pallas_call | solution.py:45
  31.7 0.1 collective-permute-start.2
  31.8 0.0 collective-permute-done.3.refs_2_
  31.8 0.5 collective-permute-start.4
  32.3 0.0 collective-permute-done.7.refs_6_
  32.3 0.6 collective-permute-done.5.refs_4_
  32.9 0.0 collective-permute-start.6
  32.9 0.5 collective-permute-start.8
  33.4 1.1 %collective-permute-start.10 = (bf16[2,4,128,128]{3,2,1,0:T(8,128)(2,1)S(1)}, bf16[2,4,128,128]{3,2,1,0:T(8,128)(2,1)S(1)}, u32[]{:S(2)}, u32[]{:S(2)}) collective-permute-start(bf16[2,4,128,128]{3,2,1,0:T(8,128)(2,1)S(1)} %get-tuple-element.66), channel_id=1, source_target_pairs={{0,32},{16,48},{32,64},{48,80},{64,96},{80,112},{96,0},{112,16},{1... | collective-permute-start | bytes 786440 | tf_op jit(solution)/shard_map/ppermute | solution.py:21
  34.5 2.1 %collective-permute-start.12 = (bf16[2,4,128,128]{3,2,1,0:T(8,128)(2,1)S(1)}, bf16[2,4,128,128]{3,2,1,0:T(8,128)(2,1)S(1)}, u32[]{:S(2)}, u32[]{:S(2)}) collective-permute-start(bf16[2,4,128,128]{3,2,1,0:T(8,128)(2,1)S(1)} %get-tuple-element.68), channel_id=1, source_target_pairs={{0,64},{16,80},{32,96},{48,112},{64,0},{80,16},{96,32},{112,48},{1... | collective-permute-start | bytes 786440 | tf_op jit(solution)/shard_map/ppermute | solution.py:21
  36.6 0.6 collective-permute-start.14
  37.2 0.0 collective-permute-done.6.refs_5_
  37.2 0.0 collective-permute-done.8.refs_7_
  37.2 4.1 %coagulate.2 = (bf16[2,4,128,128]{3,2,1,0:T(8,128)(2,1)S(1)}, bf16[2,4,128,128]{3,2,1,0:T(8,128)(2,1)S(1)}, bf16[2,4,128,128]{3,2,1,0:T(8,128)(2,1)S(1)}, bf16[2,4,128,128]{3,2,1,0:T(8,128)(2,1)S(1)}) custom-call(s32[3]{0:T(128)S(1)} %pad_add_fusion.place_ref, f32[8,128]{1,0:T(8,128)S(1)} %copy-done.2, f32[1024,128]{1,0:T(8,128)S(1)} %get-tuple-element.52.growth_ref, ...), custom_call_target="tpu_custom_call" | custom-call | flops 33554432 | bytes 122944 | tf_op jit(solution)/shard_map/coagulate/pallas_call | solution.py:45
  41.3 0.1 collective-permute-start.9
  41.4 2.3 %collective-permute-done.10.refs_2_ = bf16[2,4,128,128]{3,2,1,0:T(8,128)(2,1)S(1)} collective-permute-done((bf16[2,4,128,128]{3,2,1,0:T(8,128)(2,1)S(1)}, bf16[2,4,128,128]{3,2,1,0:T(8,128)(2,1)S(1)}, u32[]{:S(2)}, u32[]{:S(2)}) %collective-permute-start.10) | collective-permute-done | bytes 262176 | tf_op jit(solution)/shard_map/ppermute | solution.py:21
  43.8 0.0 collective-permute-start.11
  43.8 4.7 %collective-permute-done.12.refs_4_ = bf16[2,4,128,128]{3,2,1,0:T(8,128)(2,1)S(1)} collective-permute-done((bf16[2,4,128,128]{3,2,1,0:T(8,128)(2,1)S(1)}, bf16[2,4,128,128]{3,2,1,0:T(8,128)(2,1)S(1)}, u32[]{:S(2)}, u32[]{:S(2)}) %collective-permute-start.12) | collective-permute-done | bytes 262176 | tf_op jit(solution)/shard_map/ppermute | solution.py:21
  48.4 0.0 collective-permute-start.13
  48.4 0.6 collective-permute-done.14.refs_6_
  49.1 0.0 collective-permute-start.15
  49.1 0.9 collective-permute-done.13.refs_5_
  50.0 0.6 collective-permute-done.15.refs_7_
  50.6 3.5 %coagulate.3 = (bf16[2,4,128,128]{3,2,1,0:T(8,128)(2,1)S(1)}, bf16[2,4,128,128]{3,2,1,0:T(8,128)(2,1)S(1)}, bf16[2,4,128,128]{3,2,1,0:T(8,128)(2,1)S(1)}, bf16[2,4,128,128]{3,2,1,0:T(8,128)(2,1)S(1)}) custom-call(s32[3]{0:T(128)S(1)} %pad_add_fusion.place_ref, f32[8,128]{1,0:T(8,128)S(1)} %copy-done.2, f32[1024,128]{1,0:T(8,128)S(1)} %get-tuple-element.52.growth_ref, ...), custom_call_target="tpu_custom_call" | custom-call | flops 33554432 | bytes 122944 | tf_op jit(solution)/shard_map/coagulate/pallas_call | solution.py:45
  54.1 2.7 %collective-permute-start.17 = (bf16[2,4,128,128]{3,2,1,0:T(8,128)(2,1)S(1)}, bf16[2,4,128,128]{3,2,1,0:T(8,128)(2,1)S(1)}, u32[]{:S(2)}, u32[]{:S(2)}) collective-permute-start(bf16[2,4,128,128]{3,2,1,0:T(8,128)(2,1)S(1)} %get-tuple-element.73), channel_id=1, source_target_pairs={{0,96},{16,112},{32,0},{48,16},{64,32},{80,48},{96,64},{112,80},{1... | collective-permute-start | bytes 786440 | tf_op jit(solution)/shard_map/ppermute | solution.py:21
  56.8 0.3 collective-permute-start.19
  57.2 0.6 collective-permute-start.21
  57.8 10.6 %collective-permute-done.17.refs_2_ = bf16[2,4,128,128]{3,2,1,0:T(8,128)(2,1)S(1)} collective-permute-done((bf16[2,4,128,128]{3,2,1,0:T(8,128)(2,1)S(1)}, bf16[2,4,128,128]{3,2,1,0:T(8,128)(2,1)S(1)}, u32[]{:S(2)}, u32[]{:S(2)}) %collective-permute-start.17) | collective-permute-done | bytes 262176 | tf_op jit(solution)/shard_map/ppermute | solution.py:21
  68.3 0.0 collective-permute-start.18
  68.4 0.0 collective-permute-done.19.refs_4_
  68.4 0.5 collective-permute-start.20
  68.9 2.9 %collective-permute-done.21.refs_6_ = bf16[2,4,128,128]{3,2,1,0:T(8,128)(2,1)S(1)} collective-permute-done((bf16[2,4,128,128]{3,2,1,0:T(8,128)(2,1)S(1)}, bf16[2,4,128,128]{3,2,1,0:T(8,128)(2,1)S(1)}, u32[]{:S(2)}, u32[]{:S(2)}) %collective-permute-start.21) | collective-permute-done | bytes 262176 | tf_op jit(solution)/shard_map/ppermute | solution.py:21
  71.8 0.0 collective-permute-start.22
  71.8 0.5 collective-permute-start.25
  72.3 0.0 collective-permute-done.16.refs_1_
  72.3 0.8 collective-permute-start.26
  73.1 0.0 collective-permute-done.18.refs_3_
  73.1 0.3 collective-permute-start.28
  73.5 0.9 collective-permute-start.30
  74.4 0.8 arrived_rows.1
  75.3 0.1 collective-permute-start.23
  75.3 0.0 collective-permute-done.25.refs_1_
  75.3 5.3 %collective-permute-start.24 = (bf16[2,128,1024]{2,1,0:T(8,128)(2,1)S(1)}, bf16[2,128,1024]{2,1,0:T(8,128)(2,1)S(1)}, u32[]{:S(2)}, u32[]{:S(2)}) collective-permute-start(bf16[2,128,1024]{2,1,0:T(8,128)(2,1)S(1)} %get-tuple-element.77.low_ref), channel_id=1, source_target_pairs={{0,15},{1,0},{2,1},{3,2},{4,3},{5,4},{6,5},{7,6},{8,7},{9,8},{10,9... | collective-permute-start | bytes 1572872 | tf_op jit(solution)/shard_map/ppermute | solution.py:21
  80.7 0.8 collective-permute-done.26.refs_2_
  81.5 2.4 %collective-permute-done.28.refs_4_ = bf16[2,4,128,128]{3,2,1,0:T(8,128)(2,1)S(1)} collective-permute-done((bf16[2,4,128,128]{3,2,1,0:T(8,128)(2,1)S(1)}, bf16[2,4,128,128]{3,2,1,0:T(8,128)(2,1)S(1)}, u32[]{:S(2)}, u32[]{:S(2)}) %collective-permute-start.28) | collective-permute-done | bytes 262176 | tf_op jit(solution)/shard_map/ppermute | solution.py:21
  83.9 4.3 %collective-permute-done.30.refs_6_ = bf16[2,4,128,128]{3,2,1,0:T(8,128)(2,1)S(1)} collective-permute-done((bf16[2,4,128,128]{3,2,1,0:T(8,128)(2,1)S(1)}, bf16[2,4,128,128]{3,2,1,0:T(8,128)(2,1)S(1)}, u32[]{:S(2)}, u32[]{:S(2)}) %collective-permute-start.30) | collective-permute-done | bytes 262176 | tf_op jit(solution)/shard_map/ppermute | solution.py:21
  88.2 0.0 collective-permute-start.31
  88.2 1.5 %collective-permute-done.31.refs_7_ = bf16[2,4,128,128]{3,2,1,0:T(8,128)(2,1)S(1)} collective-permute-done((bf16[2,4,128,128]{3,2,1,0:T(8,128)(2,1)S(1)}, bf16[2,4,128,128]{3,2,1,0:T(8,128)(2,1)S(1)}, u32[]{:S(2)}, u32[]{:S(2)}) %collective-permute-start.31) | collective-permute-done | bytes 262176 | tf_op jit(solution)/shard_map/ppermute | solution.py:25
  89.7 2.3 %collective-permute-done.23.under_ref = bf16[2,128,1024]{2,1,0:T(8,128)(2,1)S(1)} collective-permute-done((bf16[2,128,1024]{2,1,0:T(8,128)(2,1)S(1)}, bf16[2,128,1024]{2,1,0:T(8,128)(2,1)S(1)}, u32[]{:S(2)}, u32[]{:S(2)}) %collective-permute-start.23) | collective-permute-done | bytes 524320 | tf_op jit(solution)/shard_map/ppermute | solution.py:21
  92.1 7.8 %final_rows.1 = bf16[1024,1024]{1,0:T(8,128)(2,1)} custom-call(s32[3]{0:T(128)S(1)} %pad_add_fusion.place_ref, bf16[2,144,1024]{2,1,0:T(8,128)(2,1)S(1)} %collective-permute-done.under_ref.first_under, f32[2,8,1024]{2,1,0:T(8,128)S(1)} %get-tuple-element.46.rate_ref, bf16[2,144,1024]{2,1,0:T(8,128)(2,1)S(1)} %collective-permute-done.1.over_ref.first_over, ...), custom_call_target="tpu_custom_call" | custom-call | flops 442368 | bytes 117760 | tf_op jit(solution)/shard_map/final_rows/pallas_call | solution.py:45
  (22 shorter events, 0.1 us)
Async XLA Ops:
  0.1 21.9 %copy-start.5 = (s32[128,64]{0,1:T(8,128)S(1)}, s32[128,64]{0,1:T(8,128)}, u32[]{:S(2)}) copy-start(s32[128,64]{0,1:T(8,128)} %param.14) | copy-start | bytes 98308
  0.1 22.0 %copy-start.3 = (f32[1024]{0:T(1024)S(1)}, f32[1024]{0:T(1024)}, u32[]{:S(2)}) copy-start(f32[1024]{0:T(1024)} %param.11) | copy-start | bytes 12292
  0.1 22.0 %copy-start.4 = (s32[128]{0:T(128)S(1)}, s32[128]{0:T(128)}, u32[]{:S(2)}) copy-start(s32[128]{0:T(128)} %count_ref.1) | copy-start | bytes 1540
  3.8 22.6 %collective-permute-start = (bf16[2,144,1024]{2,1,0:T(8,128)(2,1)}, bf16[2,144,1024]{2,1,0:T(8,128)(2,1)S(1)}, u32[]{:S(2)}, u32[]{:S(2)}) collective-permute-start(bf16[2,144,1024]{2,1,0:T(8,128)(2,1)} %get-tuple-element.45), channel_id=1, source_target_pairs={{0,1},{1,2},{2,3},{3,4},{4,5},{5,6},{6,7},{7,8},{8,9},{9,10},{10,1... | collective-permute-start | bytes 1769480 | tf_op jit(solution)/shard_map/ppermute | solution.py:21
  5.4 21.0 %collective-permute-start.1 = (bf16[2,144,1024]{2,1,0:T(8,128)(2,1)}, bf16[2,144,1024]{2,1,0:T(8,128)(2,1)S(1)}, u32[]{:S(2)}, u32[]{:S(2)}) collective-permute-start(bf16[2,144,1024]{2,1,0:T(8,128)(2,1)} %get-tuple-element.47), channel_id=1, source_target_pairs={{0,15},{1,0},{2,1},{3,2},{4,3},{5,4},{6,5},{7,6},{8,7},{9,8},{10,9... | collective-permute-start | bytes 1769480 | tf_op jit(solution)/shard_map/ppermute | solution.py:21
  16.0 0.7 copy-start
  16.7 15.0 %collective-permute-start.3 = (bf16[2,4,128,128]{3,2,1,0:T(8,128)(2,1)}, bf16[2,4,128,128]{3,2,1,0:T(8,128)(2,1)}, u32[]{:S(2)}, u32[]{:S(2)}) collective-permute-start(bf16[2,4,128,128]{3,2,1,0:T(8,128)(2,1)} %get-tuple-element.58), channel_id=1, source_target_pairs={{0,32},{16,48},{32,64},{48,80},{64,96},{80,112},{96,0},{112,16},{1... | collective-permute-start | bytes 786440 | tf_op jit(solution)/shard_map/ppermute | solution.py:21
  18.3 14.0 %collective-permute-start.7 = (bf16[2,4,128,128]{3,2,1,0:T(8,128)(2,1)}, bf16[2,4,128,128]{3,2,1,0:T(8,128)(2,1)}, u32[]{:S(2)}, u32[]{:S(2)}) collective-permute-start(bf16[2,4,128,128]{3,2,1,0:T(8,128)(2,1)} %get-tuple-element.62), channel_id=1, source_target_pairs={{0,96},{16,112},{32,0},{48,16},{64,32},{80,48},{96,64},{112,80},{1... | collective-permute-start | bytes 786440 | tf_op jit(solution)/shard_map/ppermute | solution.py:21
  20.0 12.9 %collective-permute-start.5 = (bf16[2,4,128,128]{3,2,1,0:T(8,128)(2,1)}, bf16[2,4,128,128]{3,2,1,0:T(8,128)(2,1)}, u32[]{:S(2)}, u32[]{:S(2)}) collective-permute-start(bf16[2,4,128,128]{3,2,1,0:T(8,128)(2,1)} %get-tuple-element.60), channel_id=1, source_target_pairs={{0,64},{16,80},{32,96},{48,112},{64,0},{80,16},{96,32},{112,48},{1... | collective-permute-start | bytes 786440 | tf_op jit(solution)/shard_map/ppermute | solution.py:21
  26.4 5.3 %copy-start.1 = (bf16[2,4,128,128]{3,2,1,0:T(8,128)(2,1)S(1)}, bf16[2,4,128,128]{3,2,1,0:T(8,128)(2,1)}, u32[]{:S(2)}) copy-start(bf16[2,4,128,128]{3,2,1,0:T(8,128)(2,1)} %copy-done) | copy-start | bytes 786436
  26.4 10.8 %copy-start.2 = (f32[8,128]{1,0:T(8,128)S(1)}, f32[8,128]{1,0:T(8,128)}, u32[]{:S(2)}) copy-start(f32[8,128]{1,0:T(8,128)} %satur_ref.3) | copy-start | bytes 12292
  31.7 2.9 %collective-permute-start.2 = (bf16[2,4,128,128]{3,2,1,0:T(8,128)(2,1)S(1)}, bf16[2,4,128,128]{3,2,1,0:T(8,128)(2,1)S(1)}, u32[]{:S(2)}, u32[]{:S(2)}) collective-permute-start(bf16[2,4,128,128]{3,2,1,0:T(8,128)(2,1)S(1)} %copy-done.1), channel_id=1, source_target_pairs={{0,16},{16,0},{32,48},{48,32},{64,80},{80,64},{96,112},{112,96},{1... | collective-permute-start | bytes 786440 | tf_op jit(solution)/shard_map/ppermute | solution.py:25
  31.8 4.9 %collective-permute-start.4 = (bf16[2,4,128,128]{3,2,1,0:T(8,128)(2,1)}, bf16[2,4,128,128]{3,2,1,0:T(8,128)(2,1)S(1)}, u32[]{:S(2)}, u32[]{:S(2)}) collective-permute-start(bf16[2,4,128,128]{3,2,1,0:T(8,128)(2,1)} %collective-permute-done.3.refs_2_), channel_id=1, source_target_pairs={{0,16},{16,0},{32,48},{48,32},{64,80},{80,64},{96,112},{112,96},{1... | collective-permute-start | bytes 786440 | tf_op jit(solution)/shard_map/ppermute | solution.py:25
  32.9 4.3 %collective-permute-start.6 = (bf16[2,4,128,128]{3,2,1,0:T(8,128)(2,1)}, bf16[2,4,128,128]{3,2,1,0:T(8,128)(2,1)S(1)}, u32[]{:S(2)}, u32[]{:S(2)}) collective-permute-start(bf16[2,4,128,128]{3,2,1,0:T(8,128)(2,1)} %collective-permute-done.5.refs_4_), channel_id=1, source_target_pairs={{0,16},{16,0},{32,48},{48,32},{64,80},{80,64},{96,112},{112,96},{1... | collective-permute-start | bytes 786440 | tf_op jit(solution)/shard_map/ppermute | solution.py:25
  32.9 4.3 %collective-permute-start.8 = (bf16[2,4,128,128]{3,2,1,0:T(8,128)(2,1)}, bf16[2,4,128,128]{3,2,1,0:T(8,128)(2,1)S(1)}, u32[]{:S(2)}, u32[]{:S(2)}) collective-permute-start(bf16[2,4,128,128]{3,2,1,0:T(8,128)(2,1)} %collective-permute-done.7.refs_6_), channel_id=1, source_target_pairs={{0,16},{16,0},{32,48},{48,32},{64,80},{80,64},{96,112},{112,96},{1... | collective-permute-start | bytes 786440 | tf_op jit(solution)/shard_map/ppermute | solution.py:25
  33.4 10.4 %collective-permute-start.10 = (bf16[2,4,128,128]{3,2,1,0:T(8,128)(2,1)S(1)}, bf16[2,4,128,128]{3,2,1,0:T(8,128)(2,1)S(1)}, u32[]{:S(2)}, u32[]{:S(2)}) collective-permute-start(bf16[2,4,128,128]{3,2,1,0:T(8,128)(2,1)S(1)} %get-tuple-element.66), channel_id=1, source_target_pairs={{0,32},{16,48},{32,64},{48,80},{64,96},{80,112},{96,0},{112,16},{1... | collective-permute-start | bytes 786440 | tf_op jit(solution)/shard_map/ppermute | solution.py:21
  34.5 13.9 %collective-permute-start.12 = (bf16[2,4,128,128]{3,2,1,0:T(8,128)(2,1)S(1)}, bf16[2,4,128,128]{3,2,1,0:T(8,128)(2,1)S(1)}, u32[]{:S(2)}, u32[]{:S(2)}) collective-permute-start(bf16[2,4,128,128]{3,2,1,0:T(8,128)(2,1)S(1)} %get-tuple-element.68), channel_id=1, source_target_pairs={{0,64},{16,80},{32,96},{48,112},{64,0},{80,16},{96,32},{112,48},{1... | collective-permute-start | bytes 786440 | tf_op jit(solution)/shard_map/ppermute | solution.py:21
  36.6 12.4 %collective-permute-start.14 = (bf16[2,4,128,128]{3,2,1,0:T(8,128)(2,1)S(1)}, bf16[2,4,128,128]{3,2,1,0:T(8,128)(2,1)S(1)}, u32[]{:S(2)}, u32[]{:S(2)}) collective-permute-start(bf16[2,4,128,128]{3,2,1,0:T(8,128)(2,1)S(1)} %get-tuple-element.70), channel_id=1, source_target_pairs={{0,96},{16,112},{32,0},{48,16},{64,32},{80,48},{96,64},{112,80},{1... | collective-permute-start | bytes 786440 | tf_op jit(solution)/shard_map/ppermute | solution.py:21
  41.3 7.7 %collective-permute-start.9 = (bf16[2,4,128,128]{3,2,1,0:T(8,128)(2,1)S(1)}, bf16[2,4,128,128]{3,2,1,0:T(8,128)(2,1)S(1)}, u32[]{:S(2)}, u32[]{:S(2)}) collective-permute-start(bf16[2,4,128,128]{3,2,1,0:T(8,128)(2,1)S(1)} %get-tuple-element.65.refs_0_), channel_id=1, source_target_pairs={{0,16},{16,0},{32,48},{48,32},{64,80},{80,64},{96,112},{112,96},{1... | collective-permute-start | bytes 786440 | tf_op jit(solution)/shard_map/ppermute | solution.py:25
  43.8 5.3 %collective-permute-start.11 = (bf16[2,4,128,128]{3,2,1,0:T(8,128)(2,1)S(1)}, bf16[2,4,128,128]{3,2,1,0:T(8,128)(2,1)S(1)}, u32[]{:S(2)}, u32[]{:S(2)}) collective-permute-start(bf16[2,4,128,128]{3,2,1,0:T(8,128)(2,1)S(1)} %collective-permute-done.10.refs_2_), channel_id=1, source_target_pairs={{0,16},{16,0},{32,48},{48,32},{64,80},{80,64},{96,112},{112,96},{1... | collective-permute-start | bytes 786440 | tf_op jit(solution)/shard_map/ppermute | solution.py:25
  48.4 1.5 %collective-permute-start.13 = (bf16[2,4,128,128]{3,2,1,0:T(8,128)(2,1)S(1)}, bf16[2,4,128,128]{3,2,1,0:T(8,128)(2,1)S(1)}, u32[]{:S(2)}, u32[]{:S(2)}) collective-permute-start(bf16[2,4,128,128]{3,2,1,0:T(8,128)(2,1)S(1)} %collective-permute-done.12.refs_4_), channel_id=1, source_target_pairs={{0,16},{16,0},{32,48},{48,32},{64,80},{80,64},{96,112},{112,96},{1... | collective-permute-start | bytes 786440 | tf_op jit(solution)/shard_map/ppermute | solution.py:25
  49.1 1.5 %collective-permute-start.15 = (bf16[2,4,128,128]{3,2,1,0:T(8,128)(2,1)S(1)}, bf16[2,4,128,128]{3,2,1,0:T(8,128)(2,1)S(1)}, u32[]{:S(2)}, u32[]{:S(2)}) collective-permute-start(bf16[2,4,128,128]{3,2,1,0:T(8,128)(2,1)S(1)} %collective-permute-done.14.refs_6_), channel_id=1, source_target_pairs={{0,16},{16,0},{32,48},{48,32},{64,80},{80,64},{96,112},{112,96},{1... | collective-permute-start | bytes 786440 | tf_op jit(solution)/shard_map/ppermute | solution.py:25
  54.1 14.2 %collective-permute-start.17 = (bf16[2,4,128,128]{3,2,1,0:T(8,128)(2,1)S(1)}, bf16[2,4,128,128]{3,2,1,0:T(8,128)(2,1)S(1)}, u32[]{:S(2)}, u32[]{:S(2)}) collective-permute-start(bf16[2,4,128,128]{3,2,1,0:T(8,128)(2,1)S(1)} %get-tuple-element.73), channel_id=1, source_target_pairs={{0,96},{16,112},{32,0},{48,16},{64,32},{80,48},{96,64},{112,80},{1... | collective-permute-start | bytes 786440 | tf_op jit(solution)/shard_map/ppermute | solution.py:21
  56.8 11.5 %collective-permute-start.19 = (bf16[2,4,128,128]{3,2,1,0:T(8,128)(2,1)S(1)}, bf16[2,4,128,128]{3,2,1,0:T(8,128)(2,1)S(1)}, u32[]{:S(2)}, u32[]{:S(2)}) collective-permute-start(bf16[2,4,128,128]{3,2,1,0:T(8,128)(2,1)S(1)} %get-tuple-element.74), channel_id=1, source_target_pairs={{0,64},{16,80},{32,96},{48,112},{64,0},{80,16},{96,32},{112,48},{1... | collective-permute-start | bytes 786440 | tf_op jit(solution)/shard_map/ppermute | solution.py:21
  57.2 14.6 %collective-permute-start.21 = (bf16[2,4,128,128]{3,2,1,0:T(8,128)(2,1)S(1)}, bf16[2,4,128,128]{3,2,1,0:T(8,128)(2,1)S(1)}, u32[]{:S(2)}, u32[]{:S(2)}) collective-permute-start(bf16[2,4,128,128]{3,2,1,0:T(8,128)(2,1)S(1)} %get-tuple-element.75), channel_id=1, source_target_pairs={{0,32},{16,48},{32,64},{48,80},{64,96},{80,112},{96,0},{112,16},{1... | collective-permute-start | bytes 786440 | tf_op jit(solution)/shard_map/ppermute | solution.py:21
  57.8 14.5 %collective-permute-start.16 = (bf16[2,4,128,128]{3,2,1,0:T(8,128)(2,1)S(1)}, bf16[2,4,128,128]{3,2,1,0:T(8,128)(2,1)S(1)}, u32[]{:S(2)}, u32[]{:S(2)}) collective-permute-start(bf16[2,4,128,128]{3,2,1,0:T(8,128)(2,1)S(1)} %get-tuple-element.72.refs_0_), channel_id=1, source_target_pairs={{0,16},{16,0},{32,48},{48,32},{64,80},{80,64},{96,112},{112,96},{1... | collective-permute-start | bytes 786440 | tf_op jit(solution)/shard_map/ppermute | solution.py:25
  68.3 4.8 %collective-permute-start.18 = (bf16[2,4,128,128]{3,2,1,0:T(8,128)(2,1)S(1)}, bf16[2,4,128,128]{3,2,1,0:T(8,128)(2,1)S(1)}, u32[]{:S(2)}, u32[]{:S(2)}) collective-permute-start(bf16[2,4,128,128]{3,2,1,0:T(8,128)(2,1)S(1)} %collective-permute-done.17.refs_2_), channel_id=1, source_target_pairs={{0,16},{16,0},{32,48},{48,32},{64,80},{80,64},{96,112},{112,96},{1... | collective-permute-start | bytes 786440 | tf_op jit(solution)/shard_map/ppermute | solution.py:25
  68.4 5.1 %collective-permute-start.20 = (bf16[2,4,128,128]{3,2,1,0:T(8,128)(2,1)S(1)}, bf16[2,4,128,128]{3,2,1,0:T(8,128)(2,1)S(1)}, u32[]{:S(2)}, u32[]{:S(2)}) collective-permute-start(bf16[2,4,128,128]{3,2,1,0:T(8,128)(2,1)S(1)} %collective-permute-done.19.refs_4_), channel_id=1, source_target_pairs={{0,16},{16,0},{32,48},{48,32},{64,80},{80,64},{96,112},{112,96},{1... | collective-permute-start | bytes 786440 | tf_op jit(solution)/shard_map/ppermute | solution.py:25
  71.8 2.6 %collective-permute-start.22 = (bf16[2,4,128,128]{3,2,1,0:T(8,128)(2,1)S(1)}, bf16[2,4,128,128]{3,2,1,0:T(8,128)(2,1)S(1)}, u32[]{:S(2)}, u32[]{:S(2)}) collective-permute-start(bf16[2,4,128,128]{3,2,1,0:T(8,128)(2,1)S(1)} %collective-permute-done.21.refs_6_), channel_id=1, source_target_pairs={{0,16},{16,0},{32,48},{48,32},{64,80},{80,64},{96,112},{112,96},{1... | collective-permute-start | bytes 786440 | tf_op jit(solution)/shard_map/ppermute | solution.py:25
  71.8 3.6 %collective-permute-start.25 = (bf16[2,4,128,128]{3,2,1,0:T(8,128)(2,1)S(1)}, bf16[2,4,128,128]{3,2,1,0:T(8,128)(2,1)S(1)}, u32[]{:S(2)}, u32[]{:S(2)}) collective-permute-start(bf16[2,4,128,128]{3,2,1,0:T(8,128)(2,1)S(1)} %get-tuple-element.78.refs_0_), channel_id=1, source_target_pairs={{0,16},{16,0},{32,48},{48,32},{64,80},{80,64},{96,112},{112,96},{1... | collective-permute-start | bytes 786440 | tf_op jit(solution)/shard_map/ppermute | solution.py:25
  72.3 9.2 %collective-permute-start.26 = (bf16[2,4,128,128]{3,2,1,0:T(8,128)(2,1)S(1)}, bf16[2,4,128,128]{3,2,1,0:T(8,128)(2,1)S(1)}, u32[]{:S(2)}, u32[]{:S(2)}) collective-permute-start(bf16[2,4,128,128]{3,2,1,0:T(8,128)(2,1)S(1)} %get-tuple-element.80), channel_id=1, source_target_pairs={{0,96},{16,112},{32,0},{48,16},{64,32},{80,48},{96,64},{112,80},{1... | collective-permute-start | bytes 786440 | tf_op jit(solution)/shard_map/ppermute | solution.py:21
  73.1 10.8 %collective-permute-start.28 = (bf16[2,4,128,128]{3,2,1,0:T(8,128)(2,1)S(1)}, bf16[2,4,128,128]{3,2,1,0:T(8,128)(2,1)S(1)}, u32[]{:S(2)}, u32[]{:S(2)}) collective-permute-start(bf16[2,4,128,128]{3,2,1,0:T(8,128)(2,1)S(1)} %get-tuple-element.82), channel_id=1, source_target_pairs={{0,64},{16,80},{32,96},{48,112},{64,0},{80,16},{96,32},{112,48},{1... | collective-permute-start | bytes 786440 | tf_op jit(solution)/shard_map/ppermute | solution.py:21
  73.5 14.7 %collective-permute-start.30 = (bf16[2,4,128,128]{3,2,1,0:T(8,128)(2,1)S(1)}, bf16[2,4,128,128]{3,2,1,0:T(8,128)(2,1)S(1)}, u32[]{:S(2)}, u32[]{:S(2)}) collective-permute-start(bf16[2,4,128,128]{3,2,1,0:T(8,128)(2,1)S(1)} %get-tuple-element.84), channel_id=1, source_target_pairs={{0,32},{16,48},{32,64},{48,80},{64,96},{80,112},{96,0},{112,16},{1... | collective-permute-start | bytes 786440 | tf_op jit(solution)/shard_map/ppermute | solution.py:21
  75.3 16.8 %collective-permute-start.23 = (bf16[2,128,1024]{2,1,0:T(8,128)(2,1)S(1)}, bf16[2,128,1024]{2,1,0:T(8,128)(2,1)S(1)}, u32[]{:S(2)}, u32[]{:S(2)}) collective-permute-start(bf16[2,128,1024]{2,1,0:T(8,128)(2,1)S(1)} %get-tuple-element.76.high_ref), channel_id=1, source_target_pairs={{0,1},{1,2},{2,3},{3,4},{4,5},{5,6},{6,7},{7,8},{8,9},{9,10},{10,1... | collective-permute-start | bytes 1572872 | tf_op jit(solution)/shard_map/ppermute | solution.py:21
  75.3 16.7 %collective-permute-start.24 = (bf16[2,128,1024]{2,1,0:T(8,128)(2,1)S(1)}, bf16[2,128,1024]{2,1,0:T(8,128)(2,1)S(1)}, u32[]{:S(2)}, u32[]{:S(2)}) collective-permute-start(bf16[2,128,1024]{2,1,0:T(8,128)(2,1)S(1)} %get-tuple-element.77.low_ref), channel_id=1, source_target_pairs={{0,15},{1,0},{2,1},{3,2},{4,3},{5,4},{6,5},{7,6},{8,7},{9,8},{10,9... | collective-permute-start | bytes 1572872 | tf_op jit(solution)/shard_map/ppermute | solution.py:21
  81.5 6.8 %collective-permute-start.27 = (bf16[2,4,128,128]{3,2,1,0:T(8,128)(2,1)S(1)}, bf16[2,4,128,128]{3,2,1,0:T(8,128)(2,1)S(1)}, u32[]{:S(2)}, u32[]{:S(2)}) collective-permute-start(bf16[2,4,128,128]{3,2,1,0:T(8,128)(2,1)S(1)} %collective-permute-done.26.refs_2_), channel_id=1, source_target_pairs={{0,16},{16,0},{32,48},{48,32},{64,80},{80,64},{96,112},{112,96},{1... | collective-permute-start | bytes 786440 | tf_op jit(solution)/shard_map/ppermute | solution.py:25
  83.9 4.3 %collective-permute-start.29 = (bf16[2,4,128,128]{3,2,1,0:T(8,128)(2,1)S(1)}, bf16[2,4,128,128]{3,2,1,0:T(8,128)(2,1)S(1)}, u32[]{:S(2)}, u32[]{:S(2)}) collective-permute-start(bf16[2,4,128,128]{3,2,1,0:T(8,128)(2,1)S(1)} %collective-permute-done.28.refs_4_), channel_id=1, source_target_pairs={{0,16},{16,0},{32,48},{48,32},{64,80},{80,64},{96,112},{112,96},{1... | collective-permute-start | bytes 786440 | tf_op jit(solution)/shard_map/ppermute | solution.py:25
  88.2 1.5 %collective-permute-start.31 = (bf16[2,4,128,128]{3,2,1,0:T(8,128)(2,1)S(1)}, bf16[2,4,128,128]{3,2,1,0:T(8,128)(2,1)S(1)}, u32[]{:S(2)}, u32[]{:S(2)}) collective-permute-start(bf16[2,4,128,128]{3,2,1,0:T(8,128)(2,1)S(1)} %collective-permute-done.30.refs_6_), channel_id=1, source_target_pairs={{0,16},{16,0},{32,48},{48,32},{64,80},{80,64},{96,112},{112,96},{1... | collective-permute-start | bytes 786440 | tf_op jit(solution)/shard_map/ppermute | solution.py:25

commit v3 on v2

--- a/solution.py
+++ b/solution.py
@@ -10,6 +10,10 @@
 STEP = 32
 CHIPS = 4
 ROWS = 8
+INNER = [1, 2, 3, 4, 5, 6]
+OUTER = [-1, 0, 1, 2, 5, 6, 7, 8]
+LAST = [-1, 0, 1, 6, 7, 8]
+KEPT = [1, 2, 5, 6]
 PACK = 16
 MIB = 2**20
 SHRINK = 64
@@ -33,7 +37,7 @@
     return pltpu.with_memory_space_constraint(value, pltpu.HBM)
 
 
-def call(body, name, place, operands, outs, scratch, mib, flops, smem=0, far=()):
+def call(body, name, place, operands, outs, scratch, mib, flops, smem=0, far=(), out_far=False):
     vmem_spec = pl.BlockSpec(memory_space=pltpu.VMEM)
     smem_spec = pl.BlockSpec(memory_space=pltpu.SMEM)
     specs = [smem_spec] * (1 + smem) + [vmem_spec] * (len(operands) - smem)
@@ -45,7 +49,7 @@
     return pl.pallas_call(
         body,
         in_specs=specs,
-        out_specs=[vmem_spec] * len(outs),
+        out_specs=[pl.BlockSpec(memory_space=pl.ANY) if out_far else vmem_spec] * len(outs),
         out_shape=outs,
         scratch_shapes=scratch,
         compiler_params=pltpu.CompilerParams(vmem_limit_bytes=mib * MIB),
@@ -141,15 +145,15 @@
         pltpu.SemaphoreType.DMA((bins // STEP,)),
         pltpu.SemaphoreType.DMA(()),
     ]
-    return call(edge_kernel, "edge_rows", place, (flat, courant), outs, scratch, 8, 8 * STEP * flat.size, far=(0, 1))
-
-
-def fill_coefs(coef, rates, first_row, last_row):
-    for row in range(first_row, last_row + 1):
+    return call(edge_kernel, "edge_rows", place, (flat, courant), outs, scratch, 4, 8 * STEP * flat.size, far=(0, 1))
+
+
+def fill_coefs(coef, rates, rows):
+    for index, row in enumerate(rows):
         face_x, face_y, under = rates(0, row), rates(1, row), rates(0, row - 1)
         face_x, face_y, under = (jnp.broadcast_to(v, (8, v.shape[1])) for v in (face_x, face_y, under))
         left = pltpu.roll(face_y, 1, 1)
-        base = 5 * (row - first_row)
+        base = 5 * index
         own = 1.0 - jnp.maximum(face_x, 0.0) + jnp.minimum(under, 0.0)
         coef[base] = own - jnp.maximum(face_y, 0.0) + jnp.minimum(left, 0.0)
         coef[base + 1] = -jnp.minimum(face_x, 0.0)
@@ -158,23 +162,24 @@
         coef[base + 4] = jnp.maximum(left, 0.0)
 
 
-def substep(coef, base, before, value, after):
-    width = value.shape[-1]
+def substep(coef, index, before, value, after):
+    width, base = value.shape[-1], 5 * index
     total = coef[base][None] * value + coef[base + 1][None] * after + coef[base + 2][None] * before
     total += coef[base + 3][None] * pltpu.roll(value, width - 1, 2)
     return total + coef[base + 4][None] * pltpu.roll(value, 1, 2)
 
 
-def two_substeps(coef, first_row, load, rows, store):
+def two_substeps(coef, held, load, rows, store, keep=lambda row, value: None):
     start, stop = rows[0], rows[-1]
     once = {}
     raw = {row: load(row) for row in (start - 2, start - 1)}
     for row in range(start - 1, stop + 2):
         raw[row + 1] = load(row + 1)
-        once[row] = substep(coef, 5 * (row - first_row), raw[row - 1], raw[row], raw[row + 1])
+        once[row] = substep(coef, held.index(row), raw[row - 1], raw[row], raw[row + 1])
+        keep(row, once[row])
         if row - 1 >= start:
             mid = row - 1
-            store(mid, substep(coef, 5 * (mid - first_row), once[mid - 1], once[mid], once[mid + 1]))
+            store(mid, substep(coef, held.index(mid), once[mid - 1], once[mid], once[mid + 1]))
 
 
 def grouped(value):
@@ -191,13 +196,13 @@
 
 def inner_kernel(place_ref, rate_ref, x_ref, out0, out1, out2, out3, coef, onehot, field, tiles):
     onehot[...] = rows_first(range(ROWS))
-    fill_coefs(coef, lambda k, row: rate_ref[k, row : row + 1, :], 1, 6)
+    fill_coefs(coef, lambda k, row: rate_ref[k, row : row + 1, :], INNER)
 
     def step(start):
         transpose_in(onehot, x_ref, field, start)
         load = lambda row: grouped(field[row])
         store = lambda row, value: send_row(place_ref, tiles, (out0, out1, out2, out3), row - 2, start, value)
-        two_substeps(coef, 1, load, range(2, 6), store)
+        two_substeps(coef, INNER, load, range(2, 6), store)
 
     steps(out0.shape[2], step)
 
@@ -224,8 +229,8 @@
 def inner_rows(place, courant, flat):
     width, bins = flat.shape[1], flat.shape[0] // ROWS
     outs = [struct((2, 4, bins, 128), flat.dtype)] * CHIPS
-    scratch = first_scratch(6, width, flat.dtype)
-    return call(inner_kernel, "inner_rows", place, (courant, flat), outs, scratch, 12, 120 * bins * width)
+    scratch = first_scratch(len(INNER), width, flat.dtype)
+    return call(inner_kernel, "inner_rows", place, (courant, flat), outs, scratch, 6, 120 * bins * width)
 
 
 def all_rates(below_ref, rate_ref, above_ref):
@@ -241,7 +246,7 @@
 
 def outer_kernel(place_ref, rate_ref, under_ref, x_ref, over_ref, out0, out1, out2, out3, coef, onehot, field, tiles):
     onehot[...] = rows_first(range(ROWS))
-    fill_coefs(coef, all_rates(under_ref, rate_ref, over_ref), -1, 8)
+    fill_coefs(coef, all_rates(under_ref, rate_ref, over_ref), OUTER)
 
     def step(start):
         transpose_in(onehot, x_ref, field, start)
@@ -256,8 +261,8 @@
         def store(row, value):
             send_row(place_ref, tiles, (out0, out1, out2, out3), row if row < 2 else row - 4, start, value)
 
-        two_substeps(coef, -1, load, range(0, 2), store)
-        two_substeps(coef, -1, load, range(6, 8), store)
+        two_substeps(coef, OUTER, load, range(0, 2), store)
+        two_substeps(coef, OUTER, load, range(6, 8), store)
 
     steps(out0.shape[2], step)
 
@@ -265,35 +270,47 @@
 def outer_rows(place, courant, under, flat, over):
     width, bins = flat.shape[1], flat.shape[0] // ROWS
     outs = [struct((2, 4, bins, 128), flat.dtype)] * CHIPS
-    scratch = first_scratch(10, width, flat.dtype)
+    scratch = first_scratch(len(OUTER), width, flat.dtype)
     operands = (courant, under, flat, over)
-    return call(outer_kernel, "outer_rows", place, operands, outs, scratch, 12, 144 * bins * width)
-
-
-def arrived_kernel(place_ref, *refs):
-    slots, (low_ref, high_ref) = refs[:8], refs[8:]
-    core = place_ref[1]
+    return call(outer_kernel, "outer_rows", place, operands, outs, scratch, 6, 144 * bins * width)
+
+
+def paired_kernel(place_ref, own_ref, *refs):
+    for away in range(1, CHIPS):
+        out_ref = refs[CHIPS - 2 + away]
+        out_ref[0] = own_ref[away]
+        out_ref[1] = refs[away - 1][...]
+
+
+def paired_travel(place, own, *gives):
+    got = [swapped(give) for give in gives]
+    outs = [struct((2, *gives[0].shape), own.dtype)] * (CHIPS - 1)
+    parts = call(paired_kernel, "paired", place, (own, *got[1:]), outs, [], 2, 0)
+    return [own, got[0]] + [shifted(part, "bins", -2 * (away + 1)) for away, part in enumerate(parts)]
+
+
+def arrived_kernel(place_ref, own_ref, got_ref, *refs):
+    parts, (low_ref, high_ref) = refs[: CHIPS - 1], refs[CHIPS - 1 :]
     for away in range(CHIPS):
         for other in range(2):
-            tile = 2 * lax.rem(place_ref[0] + away, CHIPS) + lax.bitwise_xor(core, other)
+            tile = 2 * lax.rem(place_ref[0] + away, CHIPS) + lax.bitwise_xor(place_ref[1], other)
             lanes = pl.ds(pl.multiple_of(tile * 128, 128), 128)
+            slot = parts[away - 1].at[other] if away else got_ref if other else own_ref.at[0]
             for row in range(2):
-                low_ref[row, :, lanes] = slots[2 * away + other][core, row]
-                high_ref[row, :, lanes] = slots[2 * away + other][core, row + 2]
+                low_ref[row, :, lanes] = slot[row]
+                high_ref[row, :, lanes] = slot[row + 2]
 
 
 def arrived_rows(place, slots):
-    _, _, bins, lanes = slots[0].shape
+    _, bins, lanes = slots[1].shape
     outs = [struct((2, bins, 2 * CHIPS * lanes), slots[0].dtype)] * 2
     return call(arrived_kernel, "arrived_rows", place, slots, outs, [], 4, 0)
 
 
-def final_kernel(place_ref, first_under, rate_ref, first_over, under_ref, low_ref, high_ref, over_ref, *refs):
-    slots, (out_ref, coef, onehot, tiles, back) = refs[:8], refs[8:]
-    width = out_ref.shape[1]
+def middle_kernel(place_ref, rate_ref, low_ref, high_ref, *refs):
+    slots, (mid_ref, kept_ref, coef, tiles) = refs[:8], refs[8:]
     core = place_ref[1]
-    onehot[...] = bins_first()
-    fill_coefs(coef, all_rates(first_under, rate_ref, first_over), -1, 8)
+    fill_coefs(coef, lambda k, row: rate_ref[k, row : row + 1, :], INNER)
 
     def step(start):
         at = pl.ds(start, STEP)
@@ -304,41 +321,100 @@
                     tiles[tile, row] = slots[2 * away + other][core, row, at, :]
 
         def load(row):
-            for ref, first, stop in ((under_ref, -2, 0), (low_ref, 0, 2), (high_ref, 6, 8), (over_ref, 8, 10)):
-                if first <= row < stop:
-                    return grouped(ref[row - first, at, :])
+            if row < 2:
+                return grouped(low_ref[row, at, :])
+            if row > 5:
+                return grouped(high_ref[row - 6, at, :])
             return grouped(jnp.concatenate([tiles[tile, row - 2] for tile in range(2 * CHIPS)], 1))
+
+        def store(row, value):
+            mid_ref[row - 2, at, :] = value.reshape(STEP, value.shape[-1]).astype(jnp.bfloat16)
+
+        def keep(row, value):
+            if row in KEPT:
+                kept_ref[KEPT.index(row), at, :] = value.reshape(STEP, value.shape[-1])
+
+        two_substeps(coef, INNER, load, range(2, 6), store, keep)
+
+    steps(low_ref.shape[1], step)
+
+
+def middle_rows(place, courant, low, high, slots):
+    _, bins, width = low.shape
+    outs = [struct((4, bins, width), low.dtype), struct((4, bins, width), jnp.float32)]
+    scratch = [
+        pltpu.VMEM((5 * len(INNER), 8, width), jnp.float32),
+        pltpu.VMEM((2 * CHIPS, 4, STEP, 128), low.dtype),
+    ]
+    operands = (courant, low, high, *slots)
+    return call(middle_kernel, "middle_rows", place, operands, outs, scratch, 5, 120 * bins * width)
+
+
+def final_kernel(
+    place_ref, first_under, rate_ref, first_over, under_ref, low_ref, mid_ref, kept_ref, high_ref, over_ref,
+    far_ref, coef, onehot, back, out_ref, sems,
+):
+    width = out_ref.shape[1]
+    onehot[...] = bins_first()
+    fill_coefs(coef, all_rates(first_under, rate_ref, first_over), LAST)
+    size = STEP * ROWS
+    count = low_ref.shape[1] // STEP
+    copies = []
+    for index in range(count):
+        at = slice(index * STEP, (index + 1) * STEP)
+        field = lambda ref, row: grouped(ref[row, at, :])
 
         def store(row, value):
             back[row * STEP : (row + 1) * STEP, :] = value.reshape(STEP, width).astype(jnp.bfloat16)
 
-        two_substeps(coef, -1, load, range(ROWS), store)
-        target = pl.ds(pl.multiple_of(start * ROWS, STEP * ROWS), STEP * ROWS)
+        def once(row, before, value, after):
+            return substep(coef, LAST.index(row), before, value, after)
+
+        zero, one = field(low_ref, 0), field(kept_ref, 0)
+        edge = once(-1, field(under_ref, 0), field(under_ref, 1), zero)
+        first = once(0, field(under_ref, 1), zero, field(low_ref, 1))
+        store(0, once(0, edge, first, one))
+        store(1, once(1, first, one, field(kept_ref, 1)))
+        seven, six = field(high_ref, 1), field(kept_ref, 3)
+        edge = once(8, seven, field(over_ref, 0), field(over_ref, 1))
+        last = once(7, field(high_ref, 0), seven, field(over_ref, 0))
+        store(7, once(7, six, last, edge))
+        store(6, once(6, field(kept_ref, 2), six, last))
+        for row in range(4):
+            back[(row + 2) * STEP : (row + 3) * STEP, :] = mid_ref[row, at, :]
+        target = slice(index * size, (index + 1) * size)
         for lane in range(0, width, 256):
             part = jnp.dot(onehot[...], back[:, lane : lane + 256], preferred_element_type=jnp.float32)
             out_ref[target, lane : lane + 256] = part.astype(out_ref.dtype)
-
-    steps(low_ref.shape[1], step)
-
-
-def final_rows(place, courant, first_under, first_over, under, low, slots, high, over):
+        copy = pltpu.make_async_copy(out_ref.at[pl.ds(index * size, size)], far_ref.at[pl.ds(index * size, size)], sems.at[index])
+        copy.start()
+        copies.append(copy)
+    for copy in copies:
+        copy.wait()
+
+
+def final_rows(place, courant, first_under, first_over, under, low, mid, kept, high, over):
     _, bins, width = low.shape
     scratch = [
-        pltpu.VMEM((50, 8, width), jnp.float32),
+        pltpu.VMEM((5 * len(LAST), 8, width), jnp.float32),
         pltpu.VMEM((ROWS * STEP, ROWS * STEP), jnp.bfloat16),
-        pltpu.VMEM((2 * CHIPS, 4, STEP, 128), low.dtype),
         pltpu.VMEM((ROWS * STEP, width), low.dtype),
-    ]
-    operands = (first_under, courant, first_over, under, low, high, over, *slots)
+        pltpu.VMEM((bins * ROWS, width), low.dtype),
+        pltpu.SemaphoreType.DMA((bins // STEP,)),
+    ]
+    operands = (first_under, courant, first_over, under, low, mid, kept, high, over)
     outs = [struct((bins * ROWS, width), low.dtype)]
-    return call(final_kernel, "final_rows", place, operands, outs, scratch, 12, 216 * bins * width)[0]
+    return call(final_kernel, "final_rows", place, operands, outs, scratch, 7, 96 * bins * width, out_far=True)[0]
 
 
 def block_of(place_ref, away, other):
     return 2 * lax.rem(place_ref[0] + CHIPS - away, CHIPS) + lax.bitwise_xor(place_ref[1], other)
 
 
-def matrices_kernel(place_ref, pair_ref, count_ref, growth_ref, far_kernel, far_redist, first_ref, second_ref, wide_ref, flags, kernel_ref, redist_ref, sems):
+def matrices_kernel(
+    place_ref, count_ref, far_pairs, growth_ref, far_kernel, far_redist, first_ref, second_ref, wide_ref,
+    flags, pair_ref, kernel_ref, redist_ref, sems, pair_sem,
+):
     nblocks, size = kernel_ref.shape[0], kernel_ref.shape[2]
     tile = place_ref[2]
     count = count_ref[tile]
@@ -350,11 +426,14 @@
             for side, (far, near) in enumerate(((far_kernel, kernel_ref), (far_redist, redist_ref)))
         ]
 
+    pairs = pltpu.make_async_copy(far_pairs, pair_ref, pair_sem)
+    pairs.start()
     for slot in range(nblocks):
         for copy in copies(slot):
             copy.start()
+    pairs.wait()
     for index in range(nblocks * nblocks):
-        flags[pair_ref[tile, index]] = jnp.where(index < count, 1, 0)
+        flags[pair_ref[index, tile]] = jnp.where(index < count, 1, 0)
     blocks = [block_of(place_ref, away, other) for away in range(CHIPS) for other in range(2)]
 
     def row_step(slot, carry):
@@ -379,18 +458,20 @@
     bins = nblocks * size
     matrix = struct((bins, bins), kernel.dtype)
     outs = [matrix, matrix, struct((bins, size), jnp.float32)]
-    operands = (pair_lists, active_count, growth, kernel, redist)
+    operands = (active_count, pair_lists, growth, kernel, redist)
     scratch = [
         pltpu.SMEM((nblocks * nblocks,), jnp.int32),
+        pltpu.SMEM(pair_lists.shape, jnp.int32),
         pltpu.VMEM(kernel.shape, kernel.dtype),
         pltpu.VMEM(redist.shape, redist.dtype),
         pltpu.SemaphoreType.DMA((2, nblocks)),
-    ]
-    return call(matrices_kernel, "matrices", place, operands, outs, scratch, 8, 0, smem=2, far=(3, 4))
-
-
-def coagulate_kernel(picked, place_ref, satur_ref, growth_ref, first_ref, second_ref, *refs):
-    slots, outs, (field, losses, kept, moved) = refs[:8], refs[8:12], refs[12:]
+        pltpu.SemaphoreType.DMA(()),
+    ]
+    return call(matrices_kernel, "matrices", place, operands, outs, scratch, 6, 0, smem=1, far=(1, 3, 4))
+
+
+def coagulate_kernel(picked, swap_first, place_ref, satur_ref, growth_ref, first_ref, second_ref, *refs):
+    slots, outs, (field, losses, kept, moved) = refs[:8], refs[8:-4], refs[-4:]
     rows, size, lanes = slots[0].shape[1:]
     bins, cells = field.shape
     chip, core = place_ref[0], place_ref[1]
@@ -427,22 +508,31 @@
         inflow = jnp.where(lax.broadcasted_iota(jnp.int32, inflow.shape, 0) == 0, last, inflow)
         middle = (kept[at, :] + inflow).astype(jnp.bfloat16)
         for r in range(rows):
-            outs[away][lax.bitwise_xor(core, other), r] = middle[:, r * lanes : (r + 1) * lanes]
-
-
-def coagulate(picked, place, satur, growth, first, second, slots):
+            part = middle[:, r * lanes : (r + 1) * lanes]
+            if not swap_first:
+                outs[away][lax.bitwise_xor(core, other), r] = part
+            elif other:
+                outs[1 + away][r] = part
+            else:
+                outs[0][away, r] = part
+
+
+def coagulate(picked, swap_first, place, satur, growth, first, second, slots):
     _, rows, size, lanes = slots[0].shape
     bins, cells = 2 * CHIPS * size, rows * lanes
-    outs = [struct(slots[0].shape, slots[0].dtype)] * CHIPS
+    shape, dtype = slots[0].shape[1:], slots[0].dtype
+    outs = [struct((2, *shape), dtype)] * CHIPS
+    if swap_first:
+        outs = [struct((CHIPS, *shape), dtype)] + [struct(shape, dtype)] * CHIPS
     scratch = [
         pltpu.VMEM((bins, cells), jnp.bfloat16),
         pltpu.VMEM((bins, cells), jnp.bfloat16),
         pltpu.VMEM((bins, cells), jnp.float32),
         pltpu.VMEM((bins, cells), jnp.float32),
     ]
-    body = functools.partial(coagulate_kernel, picked)
+    body = functools.partial(coagulate_kernel, picked, swap_first)
     operands = (satur, growth, first, second, *slots)
-    return call(body, "coagulate", place, operands, outs, scratch, 16, 4 * bins * bins * cells)
+    return call(body, "coagulate", place, operands, outs, scratch, 10, 4 * bins * bins * cells)
 
 
 def travel(parts, direction):
@@ -465,19 +555,21 @@
     low, high, flat, courant = edge_rows(place, flat, courant)
     first_under, first_over = shifted(high, "cells", 1), shifted(low, "cells", -1)
     inner = inner_rows(place, courant, tied(flat, low))
+    outer = outer_rows(place, courant, first_under, tied(flat, inner[0]), first_over)
+    inner_slots = with_other_core([tied(part, outer[0]) for part in travel(inner, 1)])
     growth = growth.reshape(2 * CHIPS, bins)
-    first, second, growth = matrices(tied(place, inner[0]), pair_lists, active_count, growth, kernel, redist)
-    outer = outer_rows(place, courant, first_under, tied(flat, inner[0], first), first_over)
-    inner_slots = with_other_core([tied(part, outer[0]) for part in travel(inner, 1)])
-    inner = coagulate((2, 3, 4, 5), place, saturation, growth, first, second, inner_slots)
+    at = tied(place, *inner_slots[3::2])
+    first, second, growth = matrices(at, pair_lists.T, active_count, growth, kernel, redist)
+    inner = coagulate((2, 3, 4, 5), False, place, saturation, growth, first, second, inner_slots)
     outer_slots = with_other_core([tied(part, inner[0]) for part in travel(outer, 1)])
-    outer = coagulate((0, 1, 6, 7), place, saturation, growth, first, second, outer_slots)
-
-    outer_slots = with_other_core(travel(outer, -1))
+    outer = coagulate((0, 1, 6, 7), True, place, saturation, growth, first, second, outer_slots)
+
+    outer_slots = paired_travel(place, *outer)
     inner_slots = with_other_core(travel([tied(part, outer[0]) for part in inner], -1))
     low, high = arrived_rows(place, outer_slots)
     under, over = shifted(high, "cells", 1), shifted(low, "cells", -1)
-    out = final_rows(place, courant, first_under, first_over, under, low, inner_slots, high, over)
+    mid, kept = middle_rows(place, courant, low, high, inner_slots)
+    out = final_rows(place, courant, first_under, first_over, under, low, mid, kept, high, over)
     return out.reshape(bins, rows, width)
 
 

time: 100 us -> 96.1 us (0.961)
  waiting for transfers between devices: 34.6 us -> 27.6 us
  starting transfers between devices: 28.9 us -> 35.3 us
  Pallas kernels: 35.3 us -> 32.7 us
    ppermute x16, waiting for transfers between devices: 31.6 us -> 22 us  [shifted(): return lax.ppermute(value, axis, pairs)]
    ppermute x16, starting transfers between devices: 26.6 us -> 31.9 us  [shifted(): return lax.ppermute(value, axis, pairs)]
    pallas_call x8 -> x10, Pallas kernels: 35.3 us -> 32.7 us  [call(): pl.pallas_call(body, in_specs=specs, out_specs=[pl.BlockSpec(memory_space...]
    ppermute x16, waiting for transfers between devices: 3.07 us -> 5.6 us  [swapped(): return lax.ppermute(value, 'bins', [(i, i ^ 1) for i in range(2 * CHIPS)])]
    ppermute x16, starting transfers between devices: 2.22 us -> 3.37 us  [swapped(): return lax.ppermute(value, 'bins', [(i, i ^ 1) for i in range(2 * CHIPS)])]
  transfers between devices with their start and end apart: 32 -> 32, of which waited for: 13 -> 18; matrix products, arithmetic and copies ran while one was open for 0% -> 0% of each run, Pallas kernels for 20% -> 22%
where the time goes in v3:
time: 96.1 us; the launch traced here: 96 us
  starting transfers between devices  35.3 us (37%)
  Pallas kernels  32.7 us (34%)
  waiting for transfers between devices  27.6 us (29%)
    pallas_call x10, Pallas kernels, call(): pl.pallas_call(body, in_specs=specs, out_specs=[pl.BlockSpec(memory_space...  32.7 us
    ppermute x16, starting transfers between devices, shifted(): return lax.ppermute(value, axis, pairs)  31.9 us
    ppermute x16, waiting for transfers between devices, shifted(): return lax.ppermute(value, axis, pairs)  22 us
    ppermute x16, waiting for transfers between devices, swapped(): return lax.ppermute(value, 'bins', [(i, i ^ 1) for i in range(2 * CHIPS)])  5.6 us
    ppermute x16, starting transfers between devices, swapped(): return lax.ppermute(value, 'bins', [(i, i ^ 1) for i in range(2 * CHIPS)])  3.37 us
  transfers between devices with their start and end apart: 32, of which 18 were waited for; matrix products, arithmetic and copies ran while one was open for 0% of the time, Pallas kernels for 22%

profile of v3, /device:TPU:0, one launch (start us, length us, event | category | flops | bytes accessed | tf_op | source)
XLA Modules:
  0.0 96.0 jit_solution(7158624128928067491)
XLA Ops:
  0.0 0.1 pad_add_fusion.place_ref
  0.1 2.7 %edge_rows.1 = (bf16[2,144,1024]{2,1,0:T(8,128)(2,1)S(1)}, bf16[2,144,1024]{2,1,0:T(8,128)(2,1)S(1)}, bf16[1024,1024]{1,0:T(8,128)(2,1)S(1)}, f32[2,8,1024]{2,1,0:T(8,128)S(1)}) custom-call(s32[3]{0:T(128)S(1)} %pad_add_fusion.place_ref, bf16[1024,1024]{1,0:T(8,128)(2,1)} %bitcast.8, f32[2,8,1024]{2,1,0:T(8,128)} %far_rate_ref.1), custom_call_target="tpu_custom_call" | custom-call | flops 4194304 | bytes 86016 | tf_op jit(solution)/shard_map/edge_rows/pallas_call | solution.py:49
  2.8 1.6 %collective-permute-start = (bf16[2,144,1024]{2,1,0:T(8,128)(2,1)S(1)}, bf16[2,144,1024]{2,1,0:T(8,128)(2,1)S(1)}, u32[]{:S(2)}, u32[]{:S(2)}) collective-permute-start(bf16[2,144,1024]{2,1,0:T(8,128)(2,1)S(1)} %get-tuple-element.51), channel_id=1, source_target_pairs={{0,1},{1,2},{2,3},{3,4},{4,5},{5,6},{6,7},{7,8},{8,9},{9,10},{10,1... | collective-permute-start | bytes 1769480 | tf_op jit(solution)/shard_map/ppermute | solution.py:25
  4.4 4.8 %collective-permute-start.1 = (bf16[2,144,1024]{2,1,0:T(8,128)(2,1)S(1)}, bf16[2,144,1024]{2,1,0:T(8,128)(2,1)S(1)}, u32[]{:S(2)}, u32[]{:S(2)}) collective-permute-start(bf16[2,144,1024]{2,1,0:T(8,128)(2,1)S(1)} %get-tuple-element.53), channel_id=1, source_target_pairs={{0,15},{1,0},{2,1},{3,2},{4,3},{5,4},{6,5},{7,6},{8,7},{9,8},{10,9... | collective-permute-start | bytes 1769480 | tf_op jit(solution)/shard_map/ppermute | solution.py:25
  9.2 4.8 %inner_rows.1 = (bf16[2,4,128,128]{3,2,1,0:T(8,128)(2,1)S(1)}, bf16[2,4,128,128]{3,2,1,0:T(8,128)(2,1)S(1)}, bf16[2,4,128,128]{3,2,1,0:T(8,128)(2,1)S(1)}, bf16[2,4,128,128]{3,2,1,0:T(8,128)(2,1)S(1)}) custom-call(s32[3]{0:T(128)S(1)} %pad_add_fusion.place_ref, f32[2,8,1024]{2,1,0:T(8,128)S(1)} %get-tuple-element.52.rate_ref, ...), custom_call_target="tpu_custom_call" | custom-call | flops 245760 | bytes 50176 | tf_op jit(solution)/shard_map/inner_rows/pallas_call | solution.py:49
  14.1 0.0 copy-start.1
  14.1 0.0 copy-start.2
  14.1 1.6 %collective-permute-start.2 = (bf16[2,4,128,128]{3,2,1,0:T(8,128)(2,1)S(1)}, bf16[2,4,128,128]{3,2,1,0:T(8,128)(2,1)S(1)}, u32[]{:S(2)}, u32[]{:S(2)}) collective-permute-start(bf16[2,4,128,128]{3,2,1,0:T(8,128)(2,1)S(1)} %get-tuple-element.56), channel_id=1, source_target_pairs={{0,32},{16,48},{32,64},{48,80},{64,96},{80,112},{96,0},{112,16},{1... | collective-permute-start | bytes 786440 | tf_op jit(solution)/shard_map/ppermute | solution.py:25
  15.7 2.9 %collective-permute-start.4 = (bf16[2,4,128,128]{3,2,1,0:T(8,128)(2,1)S(1)}, bf16[2,4,128,128]{3,2,1,0:T(8,128)(2,1)S(1)}, u32[]{:S(2)}, u32[]{:S(2)}) collective-permute-start(bf16[2,4,128,128]{3,2,1,0:T(8,128)(2,1)S(1)} %get-tuple-element.61), channel_id=1, source_target_pairs={{0,64},{16,80},{32,96},{48,112},{64,0},{80,16},{96,32},{112,48},{1... | collective-permute-start | bytes 786440 | tf_op jit(solution)/shard_map/ppermute | solution.py:25
  18.6 1.3 %collective-permute-start.6 = (bf16[2,4,128,128]{3,2,1,0:T(8,128)(2,1)S(1)}, bf16[2,4,128,128]{3,2,1,0:T(8,128)(2,1)S(1)}, u32[]{:S(2)}, u32[]{:S(2)}) collective-permute-start(bf16[2,4,128,128]{3,2,1,0:T(8,128)(2,1)S(1)} %get-tuple-element.63), channel_id=1, source_target_pairs={{0,96},{16,112},{32,0},{48,16},{64,32},{80,48},{96,64},{112,80},{1... | collective-permute-start | bytes 786440 | tf_op jit(solution)/shard_map/ppermute | solution.py:25
  20.0 2.5 %collective-permute-done.under_ref.first_under = bf16[2,144,1024]{2,1,0:T(8,128)(2,1)S(1)} collective-permute-done((bf16[2,144,1024]{2,1,0:T(8,128)(2,1)S(1)}, bf16[2,144,1024]{2,1,0:T(8,128)(2,1)S(1)}, u32[]{:S(2)}, u32[]{:S(2)}) %collective-permute-start) | collective-permute-done | bytes 589856 | tf_op jit(solution)/shard_map/ppermute | solution.py:25
  22.5 5.3 %outer_rows.1 = (bf16[2,4,128,128]{3,2,1,0:T(8,128)(2,1)S(1)}, bf16[2,4,128,128]{3,2,1,0:T(8,128)(2,1)S(1)}, bf16[2,4,128,128]{3,2,1,0:T(8,128)(2,1)S(1)}, bf16[2,4,128,128]{3,2,1,0:T(8,128)(2,1)S(1)}) custom-call(s32[3]{0:T(128)S(1)} %pad_add_fusion.place_ref, f32[2,8,1024]{2,1,0:T(8,128)S(1)} %get-tuple-element.52.rate_ref, ...), custom_call_target="tpu_custom_call" | custom-call | flops 294912 | bytes 68608 | tf_op jit(solution)/shard_map/outer_rows/pallas_call | solution.py:49
  27.8 0.1 collective-permute-start.3
  27.9 2.1 %collective-permute-done.4.refs_4_ = bf16[2,4,128,128]{3,2,1,0:T(8,128)(2,1)S(1)} collective-permute-done((bf16[2,4,128,128]{3,2,1,0:T(8,128)(2,1)S(1)}, bf16[2,4,128,128]{3,2,1,0:T(8,128)(2,1)S(1)}, u32[]{:S(2)}, u32[]{:S(2)}) %collective-permute-start.4) | collective-permute-done | bytes 262176 | tf_op jit(solution)/shard_map/ppermute | solution.py:25
  30.0 0.0 collective-permute-start.5
  30.0 0.0 collective-permute-done.6.refs_6_
  30.0 0.5 collective-permute-start.7
  30.5 0.0 collective-permute-start.8
  30.5 2.2 %collective-permute-start.14 = (bf16[2,4,128,128]{3,2,1,0:T(8,128)(2,1)S(1)}, bf16[2,4,128,128]{3,2,1,0:T(8,128)(2,1)S(1)}, u32[]{:S(2)}, u32[]{:S(2)}) collective-permute-start(bf16[2,4,128,128]{3,2,1,0:T(8,128)(2,1)S(1)} %get-tuple-element.76), channel_id=1, source_target_pairs={{0,96},{16,112},{32,0},{48,16},{64,32},{80,48},{96,64},{112,80},{1... | collective-permute-start | bytes 786440 | tf_op jit(solution)/shard_map/ppermute | solution.py:25
  32.7 1.1 %collective-permute-start.12 = (bf16[2,4,128,128]{3,2,1,0:T(8,128)(2,1)S(1)}, bf16[2,4,128,128]{3,2,1,0:T(8,128)(2,1)S(1)}, u32[]{:S(2)}, u32[]{:S(2)}) collective-permute-start(bf16[2,4,128,128]{3,2,1,0:T(8,128)(2,1)S(1)} %get-tuple-element.74), channel_id=1, source_target_pairs={{0,64},{16,80},{32,96},{48,112},{64,0},{80,16},{96,32},{112,48},{1... | collective-permute-start | bytes 786440 | tf_op jit(solution)/shard_map/ppermute | solution.py:25
  33.8 0.7 collective-permute-start.10
  34.5 0.0 copy-start
  34.5 3.6 %matrices.1 = (bf16[1024,1024]{1,0:T(8,128)(2,1)S(1)}, bf16[1024,1024]{1,0:T(8,128)(2,1)S(1)}, f32[1024,128]{1,0:T(8,128)S(1)}) custom-call(s32[3]{0:T(128)S(1)} %pad_add_fusion.place_ref, s32[128]{0:T(128)S(1)} %copy-done.2, s32[64,128]{1,0:T(8,128)} %bitcast.9, f32[8,128]{1,0:T(8,128)S(1)} %bitcast.7, bf16[8,8,128,128]{3,2,1,0:T(8,128)(2,1)} %far_kernel.1, ...), custom_call_target="tpu_custom_call" | custom-call | bytes 139848 | tf_op jit(solution)/shard_map/matrices/pallas_call | solution.py:49
  38.1 3.5 %coagulate.2 = (bf16[2,4,128,128]{3,2,1,0:T(8,128)(2,1)S(1)}, bf16[2,4,128,128]{3,2,1,0:T(8,128)(2,1)S(1)}, bf16[2,4,128,128]{3,2,1,0:T(8,128)(2,1)S(1)}, bf16[2,4,128,128]{3,2,1,0:T(8,128)(2,1)S(1)}) custom-call(s32[3]{0:T(128)S(1)} %pad_add_fusion.place_ref, f32[8,128]{1,0:T(8,128)S(1)} %copy-done, f32[1024,128]{1,0:T(8,128)S(1)} %get-tuple-element.66.growth_ref, ...), custom_call_target="tpu_custom_call" | custom-call | flops 33554432 | bytes 122944 | tf_op jit(solution)/shard_map/coagulate/pallas_call | solution.py:49
  41.7 0.0 collective-permute-done.14.refs_6_
  41.7 1.7 %collective-permute-done.12.refs_4_ = bf16[2,4,128,128]{3,2,1,0:T(8,128)(2,1)S(1)} collective-permute-done((bf16[2,4,128,128]{3,2,1,0:T(8,128)(2,1)S(1)}, bf16[2,4,128,128]{3,2,1,0:T(8,128)(2,1)S(1)}, u32[]{:S(2)}, u32[]{:S(2)}) %collective-permute-start.12) | collective-permute-done | bytes 262176 | tf_op jit(solution)/shard_map/ppermute | solution.py:25
  43.4 4.3 %collective-permute-done.10.refs_2_ = bf16[2,4,128,128]{3,2,1,0:T(8,128)(2,1)S(1)} collective-permute-done((bf16[2,4,128,128]{3,2,1,0:T(8,128)(2,1)S(1)}, bf16[2,4,128,128]{3,2,1,0:T(8,128)(2,1)S(1)}, u32[]{:S(2)}, u32[]{:S(2)}) %collective-permute-start.10) | collective-permute-done | bytes 262176 | tf_op jit(solution)/shard_map/ppermute | solution.py:25
  47.7 0.0 collective-permute-start.9
  47.8 0.5 collective-permute-start.11
  48.3 0.0 collective-permute-start.13
  48.3 0.5 collective-permute-start.15
  48.8 0.5 collective-permute-done.9.refs_1_
  49.3 0.4 collective-permute-done.11.refs_3_
  49.7 0.4 collective-permute-done.13.refs_5_
  50.0 0.4 collective-permute-done.15.refs_7_
  50.4 3.5 %coagulate.3 = (bf16[4,4,128,128]{3,2,1,0:T(8,128)(2,1)S(1)}, bf16[4,128,128]{2,1,0:T(8,128)(2,1)S(1)}, bf16[4,128,128]{2,1,0:T(8,128)(2,1)S(1)}, bf16[4,128,128...) custom-call(s32[3]{0:T(128)S(1)} %pad_add_fusion.place_ref, f32[8,128]{1,0:T(8,128)S(1)} %copy-done, ...), custom_call_target="tpu_custom_call" | custom-call | flops 33554432 | bytes 122944 | tf_op jit(solution)/shard_map/coagulate/pallas_call | solution.py:49
  53.9 0.2 collective-permute-start.17
  54.1 0.4 collective-permute-start.18
  54.5 0.1 collective-permute-start.19
  54.6 0.7 collective-permute-done.17.refs_0_
  55.3 0.2 collective-permute-done.18.refs_1_
  55.5 0.3 collective-permute-done.19.refs_2_
  55.8 0.6 paired.1
  56.4 0.7 collective-permute-start.20
  57.1 1.1 %collective-permute-start.21 = (bf16[2,4,128,128]{3,2,1,0:T(8,128)(2,1)S(1)}, bf16[2,4,128,128]{3,2,1,0:T(8,128)(2,1)S(1)}, u32[]{:S(2)}, u32[]{:S(2)}) collective-permute-start(bf16[2,4,128,128]{3,2,1,0:T(8,128)(2,1)S(1)} %get-tuple-element.84), channel_id=1, source_target_pairs={{0,64},{16,80},{32,96},{48,112},{64,0},{80,16},{96,32},{112,48},{1... | collective-permute-start | bytes 786440 | tf_op jit(solution)/shard_map/ppermute | solution.py:25
  58.2 0.8 collective-permute-start.22
  59.1 0.5 collective-permute-start.16
  59.6 1.2 %collective-permute-done.16.got_ref = bf16[4,128,128]{2,1,0:T(8,128)(2,1)S(1)} collective-permute-done((bf16[4,128,128]{2,1,0:T(8,128)(2,1)S(1)}, bf16[4,128,128]{2,1,0:T(8,128)(2,1)S(1)}, u32[]{:S(2)}, u32[]{:S(2)}) %collective-permute-start.16) | collective-permute-done | bytes 131104 | tf_op jit(solution)/shard_map/ppermute | solution.py:29
  60.8 2.4 %collective-permute-start.25 = (bf16[2,4,128,128]{3,2,1,0:T(8,128)(2,1)S(1)}, bf16[2,4,128,128]{3,2,1,0:T(8,128)(2,1)S(1)}, u32[]{:S(2)}, u32[]{:S(2)}) collective-permute-start(bf16[2,4,128,128]{3,2,1,0:T(8,128)(2,1)S(1)} %get-tuple-element.90), channel_id=1, source_target_pairs={{0,96},{16,112},{32,0},{48,16},{64,32},{80,48},{96,64},{112,80},{1... | collective-permute-start | bytes 786440 | tf_op jit(solution)/shard_map/ppermute | solution.py:25
  63.2 2.4 %collective-permute-done.20.refs_0_ = bf16[2,4,128,128]{3,2,1,0:T(8,128)(2,1)S(1)} collective-permute-done((bf16[2,4,128,128]{3,2,1,0:T(8,128)(2,1)S(1)}, bf16[2,4,128,128]{3,2,1,0:T(8,128)(2,1)S(1)}, u32[]{:S(2)}, u32[]{:S(2)}) %collective-permute-start.20) | collective-permute-done | bytes 262176 | tf_op jit(solution)/shard_map/ppermute | solution.py:25
  65.7 1.1 %collective-permute-start.27 = (bf16[2,4,128,128]{3,2,1,0:T(8,128)(2,1)S(1)}, bf16[2,4,128,128]{3,2,1,0:T(8,128)(2,1)S(1)}, u32[]{:S(2)}, u32[]{:S(2)}) collective-permute-start(bf16[2,4,128,128]{3,2,1,0:T(8,128)(2,1)S(1)} %get-tuple-element.92), channel_id=1, source_target_pairs={{0,64},{16,80},{32,96},{48,112},{64,0},{80,16},{96,32},{112,48},{1... | collective-permute-start | bytes 786440 | tf_op jit(solution)/shard_map/ppermute | solution.py:25
  66.8 1.1 %collective-permute-done.21.refs_1_ = bf16[2,4,128,128]{3,2,1,0:T(8,128)(2,1)S(1)} collective-permute-done((bf16[2,4,128,128]{3,2,1,0:T(8,128)(2,1)S(1)}, bf16[2,4,128,128]{3,2,1,0:T(8,128)(2,1)S(1)}, u32[]{:S(2)}, u32[]{:S(2)}) %collective-permute-start.21) | collective-permute-done | bytes 262176 | tf_op jit(solution)/shard_map/ppermute | solution.py:25
  67.8 4.0 %collective-permute-start.29 = (bf16[2,4,128,128]{3,2,1,0:T(8,128)(2,1)S(1)}, bf16[2,4,128,128]{3,2,1,0:T(8,128)(2,1)S(1)}, u32[]{:S(2)}, u32[]{:S(2)}) collective-permute-start(bf16[2,4,128,128]{3,2,1,0:T(8,128)(2,1)S(1)} %get-tuple-element.94), channel_id=1, source_target_pairs={{0,32},{16,48},{32,64},{48,80},{64,96},{80,112},{96,0},{112,16},{1... | collective-permute-start | bytes 786440 | tf_op jit(solution)/shard_map/ppermute | solution.py:25
  71.8 1.5 %collective-permute-done.22.refs_2_ = bf16[2,4,128,128]{3,2,1,0:T(8,128)(2,1)S(1)} collective-permute-done((bf16[2,4,128,128]{3,2,1,0:T(8,128)(2,1)S(1)}, bf16[2,4,128,128]{3,2,1,0:T(8,128)(2,1)S(1)}, u32[]{:S(2)}, u32[]{:S(2)}) %collective-permute-start.22) | collective-permute-done | bytes 262176 | tf_op jit(solution)/shard_map/ppermute | solution.py:25
  73.4 0.8 arrived_rows.1
  74.2 0.1 collective-permute-start.23
  74.3 5.3 %collective-permute-start.31 = (bf16[2,128,1024]{2,1,0:T(8,128)(2,1)S(1)}, bf16[2,128,1024]{2,1,0:T(8,128)(2,1)S(1)}, u32[]{:S(2)}, u32[]{:S(2)}) collective-permute-start(bf16[2,128,1024]{2,1,0:T(8,128)(2,1)S(1)} %get-tuple-element.87.low_ref), channel_id=1, source_target_pairs={{0,15},{1,0},{2,1},{3,2},{4,3},{5,4},{6,5},{7,6},{8,7},{9,8},{10,9... | collective-permute-start | bytes 1572872 | tf_op jit(solution)/shard_map/ppermute | solution.py:25
  79.7 0.5 collective-permute-start.28
  80.2 3.5 %collective-permute-done.29.refs_6_ = bf16[2,4,128,128]{3,2,1,0:T(8,128)(2,1)S(1)} collective-permute-done((bf16[2,4,128,128]{3,2,1,0:T(8,128)(2,1)S(1)}, bf16[2,4,128,128]{3,2,1,0:T(8,128)(2,1)S(1)}, u32[]{:S(2)}, u32[]{:S(2)}) %collective-permute-start.29) | collective-permute-done | bytes 262176 | tf_op jit(solution)/shard_map/ppermute | solution.py:25
  83.6 0.0 collective-permute-start.30
  83.6 1.5 %collective-permute-done.30.refs_7_ = bf16[2,4,128,128]{3,2,1,0:T(8,128)(2,1)S(1)} collective-permute-done((bf16[2,4,128,128]{3,2,1,0:T(8,128)(2,1)S(1)}, bf16[2,4,128,128]{3,2,1,0:T(8,128)(2,1)S(1)}, u32[]{:S(2)}, u32[]{:S(2)}) %collective-permute-start.30) | collective-permute-done | bytes 262176 | tf_op jit(solution)/shard_map/ppermute | solution.py:29
  85.2 3.4 %middle_rows.1 = (bf16[4,128,1024]{2,1,0:T(8,128)(2,1)S(1)}, f32[4,128,1024]{2,1,0:T(8,128)S(1)}) custom-call(s32[3]{0:T(128)S(1)} %pad_add_fusion.place_ref, f32[2,8,1024]{2,1,0:T(8,128)S(1)} %get-tuple-element.52.rate_ref, bf16[2,128,1024]{2,1,0:T(8,128)(2,1)S(1)} %get-tuple-element.87.low_ref, bf16[2,128,1024]{2,1,0:T(8,128)(2,1)S(1)} %get-tuple-element.86.high_ref, ...), custom_call_target="tpu_custom_call" | custom-call | flops 245760 | bytes 99328 | tf_op jit(solution)/shard_map/middle_rows/pallas_call | solution.py:49
  88.6 2.8 %collective-permute-done.23.under_ref = bf16[2,128,1024]{2,1,0:T(8,128)(2,1)S(1)} collective-permute-done((bf16[2,128,1024]{2,1,0:T(8,128)(2,1)S(1)}, bf16[2,128,1024]{2,1,0:T(8,128)(2,1)S(1)}, u32[]{:S(2)}, u32[]{:S(2)}) %collective-permute-start.23) | collective-permute-done | bytes 524320 | tf_op jit(solution)/shard_map/ppermute | solution.py:25
  91.4 4.5 %final_rows.1 = bf16[1024,1024]{1,0:T(8,128)(2,1)} custom-call(s32[3]{0:T(128)S(1)} %pad_add_fusion.place_ref, bf16[2,144,1024]{2,1,0:T(8,128)(2,1)S(1)} %collective-permute-done.under_ref.first_under, f32[2,8,1024]{2,1,0:T(8,128)S(1)} %get-tuple-element.52.rate_ref, bf16[2,144,1024]{2,1,0:T(8,128)(2,1)S(1)} %collective-permute-done.1.over_ref.first_over, ...), custom_call_target="tpu_custom_call" | custom-call | flops 196608 | bytes 134144 | tf_op jit(solution)/shard_map/final_rows/pallas_call | solution.py:49
  (17 shorter events, 0.0 us)
Async XLA Ops:
  2.8 19.7 %collective-permute-start = (bf16[2,144,1024]{2,1,0:T(8,128)(2,1)S(1)}, bf16[2,144,1024]{2,1,0:T(8,128)(2,1)S(1)}, u32[]{:S(2)}, u32[]{:S(2)}) collective-permute-start(bf16[2,144,1024]{2,1,0:T(8,128)(2,1)S(1)} %get-tuple-element.51), channel_id=1, source_target_pairs={{0,1},{1,2},{2,3},{3,4},{4,5},{5,6},{6,7},{7,8},{8,9},{9,10},{10,1... | collective-permute-start | bytes 1769480 | tf_op jit(solution)/shard_map/ppermute | solution.py:25
  4.4 18.1 %collective-permute-start.1 = (bf16[2,144,1024]{2,1,0:T(8,128)(2,1)S(1)}, bf16[2,144,1024]{2,1,0:T(8,128)(2,1)S(1)}, u32[]{:S(2)}, u32[]{:S(2)}) collective-permute-start(bf16[2,144,1024]{2,1,0:T(8,128)(2,1)S(1)} %get-tuple-element.53), channel_id=1, source_target_pairs={{0,15},{1,0},{2,1},{3,2},{4,3},{5,4},{6,5},{7,6},{8,7},{9,8},{10,9... | collective-permute-start | bytes 1769480 | tf_op jit(solution)/shard_map/ppermute | solution.py:25
  14.1 20.4 %copy-start.1 = (f32[1024]{0:T(1024)S(1)}, f32[1024]{0:T(1024)}, u32[]{:S(2)}) copy-start(f32[1024]{0:T(1024)} %param.11) | copy-start | bytes 12292
  14.1 20.4 %copy-start.2 = (s32[128]{0:T(128)S(1)}, s32[128]{0:T(128)}, u32[]{:S(2)}) copy-start(s32[128]{0:T(128)} %count_ref.1) | copy-start | bytes 1540
  14.1 13.6 %collective-permute-start.2 = (bf16[2,4,128,128]{3,2,1,0:T(8,128)(2,1)S(1)}, bf16[2,4,128,128]{3,2,1,0:T(8,128)(2,1)S(1)}, u32[]{:S(2)}, u32[]{:S(2)}) collective-permute-start(bf16[2,4,128,128]{3,2,1,0:T(8,128)(2,1)S(1)} %get-tuple-element.56), channel_id=1, source_target_pairs={{0,32},{16,48},{32,64},{48,80},{64,96},{80,112},{96,0},{112,16},{1... | collective-permute-start | bytes 786440 | tf_op jit(solution)/shard_map/ppermute | solution.py:25
  15.7 14.3 %collective-permute-start.4 = (bf16[2,4,128,128]{3,2,1,0:T(8,128)(2,1)S(1)}, bf16[2,4,128,128]{3,2,1,0:T(8,128)(2,1)S(1)}, u32[]{:S(2)}, u32[]{:S(2)}) collective-permute-start(bf16[2,4,128,128]{3,2,1,0:T(8,128)(2,1)S(1)} %get-tuple-element.61), channel_id=1, source_target_pairs={{0,64},{16,80},{32,96},{48,112},{64,0},{80,16},{96,32},{112,48},{1... | collective-permute-start | bytes 786440 | tf_op jit(solution)/shard_map/ppermute | solution.py:25
  18.6 11.4 %collective-permute-start.6 = (bf16[2,4,128,128]{3,2,1,0:T(8,128)(2,1)S(1)}, bf16[2,4,128,128]{3,2,1,0:T(8,128)(2,1)S(1)}, u32[]{:S(2)}, u32[]{:S(2)}) collective-permute-start(bf16[2,4,128,128]{3,2,1,0:T(8,128)(2,1)S(1)} %get-tuple-element.63), channel_id=1, source_target_pairs={{0,96},{16,112},{32,0},{48,16},{64,32},{80,48},{96,64},{112,80},{1... | collective-permute-start | bytes 786440 | tf_op jit(solution)/shard_map/ppermute | solution.py:25
  27.8 4.9 %collective-permute-start.3 = (bf16[2,4,128,128]{3,2,1,0:T(8,128)(2,1)S(1)}, bf16[2,4,128,128]{3,2,1,0:T(8,128)(2,1)S(1)}, u32[]{:S(2)}, u32[]{:S(2)}) collective-permute-start(bf16[2,4,128,128]{3,2,1,0:T(8,128)(2,1)S(1)} %collective-permute-done.2.refs_2_), channel_id=1, source_target_pairs={{0,16},{16,0},{32,48},{48,32},{64,80},{80,64},{96,112},{112,96},{1... | collective-permute-start | bytes 786440 | tf_op jit(solution)/shard_map/ppermute | solution.py:29
  30.0 3.8 %collective-permute-start.5 = (bf16[2,4,128,128]{3,2,1,0:T(8,128)(2,1)S(1)}, bf16[2,4,128,128]{3,2,1,0:T(8,128)(2,1)S(1)}, u32[]{:S(2)}, u32[]{:S(2)}) collective-permute-start(bf16[2,4,128,128]{3,2,1,0:T(8,128)(2,1)S(1)} %collective-permute-done.4.refs_4_), channel_id=1, source_target_pairs={{0,16},{16,0},{32,48},{48,32},{64,80},{80,64},{96,112},{112,96},{1... | collective-permute-start | bytes 786440 | tf_op jit(solution)/shard_map/ppermute | solution.py:29
  30.0 4.5 %collective-permute-start.7 = (bf16[2,4,128,128]{3,2,1,0:T(8,128)(2,1)S(1)}, bf16[2,4,128,128]{3,2,1,0:T(8,128)(2,1)S(1)}, u32[]{:S(2)}, u32[]{:S(2)}) collective-permute-start(bf16[2,4,128,128]{3,2,1,0:T(8,128)(2,1)S(1)} %collective-permute-done.6.refs_6_), channel_id=1, source_target_pairs={{0,16},{16,0},{32,48},{48,32},{64,80},{80,64},{96,112},{112,96},{1... | collective-permute-start | bytes 786440 | tf_op jit(solution)/shard_map/ppermute | solution.py:29
  30.5 7.6 %collective-permute-start.8 = (bf16[2,4,128,128]{3,2,1,0:T(8,128)(2,1)S(1)}, bf16[2,4,128,128]{3,2,1,0:T(8,128)(2,1)S(1)}, u32[]{:S(2)}, u32[]{:S(2)}) collective-permute-start(bf16[2,4,128,128]{3,2,1,0:T(8,128)(2,1)S(1)} %get-tuple-element.69.refs_0_), channel_id=1, source_target_pairs={{0,16},{16,0},{32,48},{48,32},{64,80},{80,64},{96,112},{112,96},{1... | collective-permute-start | bytes 786440 | tf_op jit(solution)/shard_map/ppermute | solution.py:29
  30.5 11.2 %collective-permute-start.14 = (bf16[2,4,128,128]{3,2,1,0:T(8,128)(2,1)S(1)}, bf16[2,4,128,128]{3,2,1,0:T(8,128)(2,1)S(1)}, u32[]{:S(2)}, u32[]{:S(2)}) collective-permute-start(bf16[2,4,128,128]{3,2,1,0:T(8,128)(2,1)S(1)} %get-tuple-element.76), channel_id=1, source_target_pairs={{0,96},{16,112},{32,0},{48,16},{64,32},{80,48},{96,64},{112,80},{1... | collective-permute-start | bytes 786440 | tf_op jit(solution)/shard_map/ppermute | solution.py:25
  32.7 10.8 %collective-permute-start.12 = (bf16[2,4,128,128]{3,2,1,0:T(8,128)(2,1)S(1)}, bf16[2,4,128,128]{3,2,1,0:T(8,128)(2,1)S(1)}, u32[]{:S(2)}, u32[]{:S(2)}) collective-permute-start(bf16[2,4,128,128]{3,2,1,0:T(8,128)(2,1)S(1)} %get-tuple-element.74), channel_id=1, source_target_pairs={{0,64},{16,80},{32,96},{48,112},{64,0},{80,16},{96,32},{112,48},{1... | collective-permute-start | bytes 786440 | tf_op jit(solution)/shard_map/ppermute | solution.py:25
  33.8 13.9 %collective-permute-start.10 = (bf16[2,4,128,128]{3,2,1,0:T(8,128)(2,1)S(1)}, bf16[2,4,128,128]{3,2,1,0:T(8,128)(2,1)S(1)}, u32[]{:S(2)}, u32[]{:S(2)}) collective-permute-start(bf16[2,4,128,128]{3,2,1,0:T(8,128)(2,1)S(1)} %get-tuple-element.72), channel_id=1, source_target_pairs={{0,32},{16,48},{32,64},{48,80},{64,96},{80,112},{96,0},{112,16},{1... | collective-permute-start | bytes 786440 | tf_op jit(solution)/shard_map/ppermute | solution.py:25
  34.5 3.6 %copy-start = (f32[8,128]{1,0:T(8,128)S(1)}, f32[8,128]{1,0:T(8,128)}, u32[]{:S(2)}) copy-start(f32[8,128]{1,0:T(8,128)} %satur_ref.3) | copy-start | bytes 12292
  47.7 1.5 %collective-permute-start.9 = (bf16[2,4,128,128]{3,2,1,0:T(8,128)(2,1)S(1)}, bf16[2,4,128,128]{3,2,1,0:T(8,128)(2,1)S(1)}, u32[]{:S(2)}, u32[]{:S(2)}) collective-permute-start(bf16[2,4,128,128]{3,2,1,0:T(8,128)(2,1)S(1)} %get-tuple-element.71.refs_0_), channel_id=1, source_target_pairs={{0,16},{16,0},{32,48},{48,32},{64,80},{80,64},{96,112},{112,96},{1... | collective-permute-start | bytes 786440 | tf_op jit(solution)/shard_map/ppermute | solution.py:29
  47.8 1.9 %collective-permute-start.11 = (bf16[2,4,128,128]{3,2,1,0:T(8,128)(2,1)S(1)}, bf16[2,4,128,128]{3,2,1,0:T(8,128)(2,1)S(1)}, u32[]{:S(2)}, u32[]{:S(2)}) collective-permute-start(bf16[2,4,128,128]{3,2,1,0:T(8,128)(2,1)S(1)} %collective-permute-done.10.refs_2_), channel_id=1, source_target_pairs={{0,16},{16,0},{32,48},{48,32},{64,80},{80,64},{96,112},{112,96},{1... | collective-permute-start | bytes 786440 | tf_op jit(solution)/shard_map/ppermute | solution.py:29
  48.3 1.8 %collective-permute-start.13 = (bf16[2,4,128,128]{3,2,1,0:T(8,128)(2,1)S(1)}, bf16[2,4,128,128]{3,2,1,0:T(8,128)(2,1)S(1)}, u32[]{:S(2)}, u32[]{:S(2)}) collective-permute-start(bf16[2,4,128,128]{3,2,1,0:T(8,128)(2,1)S(1)} %collective-permute-done.12.refs_4_), channel_id=1, source_target_pairs={{0,16},{16,0},{32,48},{48,32},{64,80},{80,64},{96,112},{112,96},{1... | collective-permute-start | bytes 786440 | tf_op jit(solution)/shard_map/ppermute | solution.py:29
  48.3 2.1 %collective-permute-start.15 = (bf16[2,4,128,128]{3,2,1,0:T(8,128)(2,1)S(1)}, bf16[2,4,128,128]{3,2,1,0:T(8,128)(2,1)S(1)}, u32[]{:S(2)}, u32[]{:S(2)}) collective-permute-start(bf16[2,4,128,128]{3,2,1,0:T(8,128)(2,1)S(1)} %collective-permute-done.14.refs_6_), channel_id=1, source_target_pairs={{0,16},{16,0},{32,48},{48,32},{64,80},{80,64},{96,112},{112,96},{1... | collective-permute-start | bytes 786440 | tf_op jit(solution)/shard_map/ppermute | solution.py:29
  53.9 1.4 %collective-permute-start.17 = (bf16[4,128,128]{2,1,0:T(8,128)(2,1)S(1)}, bf16[4,128,128]{2,1,0:T(8,128)(2,1)S(1)}, u32[]{:S(2)}, u32[]{:S(2)}) collective-permute-start(bf16[4,128,128]{2,1,0:T(8,128)(2,1)S(1)} %get-tuple-element.80), channel_id=1, source_target_pairs={{0,16},{16,0},{32,48},{48,32},{64,80},{80,64},{96,112},{112,96},{1... | collective-permute-start | bytes 393224 | tf_op jit(solution)/shard_map/ppermute | solution.py:29
  54.1 1.4 %collective-permute-start.18 = (bf16[4,128,128]{2,1,0:T(8,128)(2,1)S(1)}, bf16[4,128,128]{2,1,0:T(8,128)(2,1)S(1)}, u32[]{:S(2)}, u32[]{:S(2)}) collective-permute-start(bf16[4,128,128]{2,1,0:T(8,128)(2,1)S(1)} %get-tuple-element.81), channel_id=1, source_target_pairs={{0,16},{16,0},{32,48},{48,32},{64,80},{80,64},{96,112},{112,96},{1... | collective-permute-start | bytes 393224 | tf_op jit(solution)/shard_map/ppermute | solution.py:29
  54.5 1.3 %collective-permute-start.19 = (bf16[4,128,128]{2,1,0:T(8,128)(2,1)S(1)}, bf16[4,128,128]{2,1,0:T(8,128)(2,1)S(1)}, u32[]{:S(2)}, u32[]{:S(2)}) collective-permute-start(bf16[4,128,128]{2,1,0:T(8,128)(2,1)S(1)} %get-tuple-element.82), channel_id=1, source_target_pairs={{0,16},{16,0},{32,48},{48,32},{64,80},{80,64},{96,112},{112,96},{1... | collective-permute-start | bytes 393224 | tf_op jit(solution)/shard_map/ppermute | solution.py:29
  56.4 9.2 %collective-permute-start.20 = (bf16[2,4,128,128]{3,2,1,0:T(8,128)(2,1)S(1)}, bf16[2,4,128,128]{3,2,1,0:T(8,128)(2,1)S(1)}, u32[]{:S(2)}, u32[]{:S(2)}) collective-permute-start(bf16[2,4,128,128]{3,2,1,0:T(8,128)(2,1)S(1)} %get-tuple-element.83), channel_id=1, source_target_pairs={{0,96},{16,112},{32,0},{48,16},{64,32},{80,48},{96,64},{112,80},{1... | collective-permute-start | bytes 786440 | tf_op jit(solution)/shard_map/ppermute | solution.py:25
  57.1 10.7 %collective-permute-start.21 = (bf16[2,4,128,128]{3,2,1,0:T(8,128)(2,1)S(1)}, bf16[2,4,128,128]{3,2,1,0:T(8,128)(2,1)S(1)}, u32[]{:S(2)}, u32[]{:S(2)}) collective-permute-start(bf16[2,4,128,128]{3,2,1,0:T(8,128)(2,1)S(1)} %get-tuple-element.84), channel_id=1, source_target_pairs={{0,64},{16,80},{32,96},{48,112},{64,0},{80,16},{96,32},{112,48},{1... | collective-permute-start | bytes 786440 | tf_op jit(solution)/shard_map/ppermute | solution.py:25
  58.2 15.1 %collective-permute-start.22 = (bf16[2,4,128,128]{3,2,1,0:T(8,128)(2,1)S(1)}, bf16[2,4,128,128]{3,2,1,0:T(8,128)(2,1)S(1)}, u32[]{:S(2)}, u32[]{:S(2)}) collective-permute-start(bf16[2,4,128,128]{3,2,1,0:T(8,128)(2,1)S(1)} %get-tuple-element.85), channel_id=1, source_target_pairs={{0,32},{16,48},{32,64},{48,80},{64,96},{80,112},{96,0},{112,16},{1... | collective-permute-start | bytes 786440 | tf_op jit(solution)/shard_map/ppermute | solution.py:25
  59.1 15.2 %collective-permute-start.24 = (bf16[2,4,128,128]{3,2,1,0:T(8,128)(2,1)S(1)}, bf16[2,4,128,128]{3,2,1,0:T(8,128)(2,1)S(1)}, u32[]{:S(2)}, u32[]{:S(2)}) collective-permute-start(bf16[2,4,128,128]{3,2,1,0:T(8,128)(2,1)S(1)} %get-tuple-element.88.refs_0_), channel_id=1, source_target_pairs={{0,16},{16,0},{32,48},{48,32},{64,80},{80,64},{96,112},{112,96},{1... | collective-permute-start | bytes 786440 | tf_op jit(solution)/shard_map/ppermute | solution.py:29
  59.1 1.7 %collective-permute-start.16 = (bf16[4,128,128]{2,1,0:T(8,128)(2,1)S(1)}, bf16[4,128,128]{2,1,0:T(8,128)(2,1)S(1)}, u32[]{:S(2)}, u32[]{:S(2)}) collective-permute-start(bf16[4,128,128]{2,1,0:T(8,128)(2,1)S(1)} %get-tuple-element.79), channel_id=1, source_target_pairs={{0,16},{16,0},{32,48},{48,32},{64,80},{80,64},{96,112},{112,96},{1... | collective-permute-start | bytes 393224 | tf_op jit(solution)/shard_map/ppermute | solution.py:29
  60.8 18.9 %collective-permute-start.25 = (bf16[2,4,128,128]{3,2,1,0:T(8,128)(2,1)S(1)}, bf16[2,4,128,128]{3,2,1,0:T(8,128)(2,1)S(1)}, u32[]{:S(2)}, u32[]{:S(2)}) collective-permute-start(bf16[2,4,128,128]{3,2,1,0:T(8,128)(2,1)S(1)} %get-tuple-element.90), channel_id=1, source_target_pairs={{0,96},{16,112},{32,0},{48,16},{64,32},{80,48},{96,64},{112,80},{1... | collective-permute-start | bytes 786440 | tf_op jit(solution)/shard_map/ppermute | solution.py:25
  65.7 14.0 %collective-permute-start.27 = (bf16[2,4,128,128]{3,2,1,0:T(8,128)(2,1)S(1)}, bf16[2,4,128,128]{3,2,1,0:T(8,128)(2,1)S(1)}, u32[]{:S(2)}, u32[]{:S(2)}) collective-permute-start(bf16[2,4,128,128]{3,2,1,0:T(8,128)(2,1)S(1)} %get-tuple-element.92), channel_id=1, source_target_pairs={{0,64},{16,80},{32,96},{48,112},{64,0},{80,16},{96,32},{112,48},{1... | collective-permute-start | bytes 786440 | tf_op jit(solution)/shard_map/ppermute | solution.py:25
  67.8 15.8 %collective-permute-start.29 = (bf16[2,4,128,128]{3,2,1,0:T(8,128)(2,1)S(1)}, bf16[2,4,128,128]{3,2,1,0:T(8,128)(2,1)S(1)}, u32[]{:S(2)}, u32[]{:S(2)}) collective-permute-start(bf16[2,4,128,128]{3,2,1,0:T(8,128)(2,1)S(1)} %get-tuple-element.94), channel_id=1, source_target_pairs={{0,32},{16,48},{32,64},{48,80},{64,96},{80,112},{96,0},{112,16},{1... | collective-permute-start | bytes 786440 | tf_op jit(solution)/shard_map/ppermute | solution.py:25
  74.2 17.1 %collective-permute-start.23 = (bf16[2,128,1024]{2,1,0:T(8,128)(2,1)S(1)}, bf16[2,128,1024]{2,1,0:T(8,128)(2,1)S(1)}, u32[]{:S(2)}, u32[]{:S(2)}) collective-permute-start(bf16[2,128,1024]{2,1,0:T(8,128)(2,1)S(1)} %get-tuple-element.86.high_ref), channel_id=1, source_target_pairs={{0,1},{1,2},{2,3},{3,4},{4,5},{5,6},{6,7},{7,8},{8,9},{9,10},{10,1... | collective-permute-start | bytes 1572872 | tf_op jit(solution)/shard_map/ppermute | solution.py:25
  74.3 17.0 %collective-permute-start.31 = (bf16[2,128,1024]{2,1,0:T(8,128)(2,1)S(1)}, bf16[2,128,1024]{2,1,0:T(8,128)(2,1)S(1)}, u32[]{:S(2)}, u32[]{:S(2)}) collective-permute-start(bf16[2,128,1024]{2,1,0:T(8,128)(2,1)S(1)} %get-tuple-element.87.low_ref), channel_id=1, source_target_pairs={{0,15},{1,0},{2,1},{3,2},{4,3},{5,4},{6,5},{7,6},{8,7},{9,8},{10,9... | collective-permute-start | bytes 1572872 | tf_op jit(solution)/shard_map/ppermute | solution.py:25
  79.6 4.0 %collective-permute-start.26 = (bf16[2,4,128,128]{3,2,1,0:T(8,128)(2,1)S(1)}, bf16[2,4,128,128]{3,2,1,0:T(8,128)(2,1)S(1)}, u32[]{:S(2)}, u32[]{:S(2)}) collective-permute-start(bf16[2,4,128,128]{3,2,1,0:T(8,128)(2,1)S(1)} %collective-permute-done.25.refs_2_), channel_id=1, source_target_pairs={{0,16},{16,0},{32,48},{48,32},{64,80},{80,64},{96,112},{112,96},{1... | collective-permute-start | bytes 786440 | tf_op jit(solution)/shard_map/ppermute | solution.py:29
  79.7 4.0 %collective-permute-start.28 = (bf16[2,4,128,128]{3,2,1,0:T(8,128)(2,1)S(1)}, bf16[2,4,128,128]{3,2,1,0:T(8,128)(2,1)S(1)}, u32[]{:S(2)}, u32[]{:S(2)}) collective-permute-start(bf16[2,4,128,128]{3,2,1,0:T(8,128)(2,1)S(1)} %collective-permute-done.27.refs_4_), channel_id=1, source_target_pairs={{0,16},{16,0},{32,48},{48,32},{64,80},{80,64},{96,112},{112,96},{1... | collective-permute-start | bytes 786440 | tf_op jit(solution)/shard_map/ppermute | solution.py:29
  83.6 1.5 %collective-permute-start.30 = (bf16[2,4,128,128]{3,2,1,0:T(8,128)(2,1)S(1)}, bf16[2,4,128,128]{3,2,1,0:T(8,128)(2,1)S(1)}, u32[]{:S(2)}, u32[]{:S(2)}) collective-permute-start(bf16[2,4,128,128]{3,2,1,0:T(8,128)(2,1)S(1)} %collective-permute-done.29.refs_6_), channel_id=1, source_target_pairs={{0,16},{16,0},{32,48},{48,32},{64,80},{80,64},{96,112},{112,96},{1... | collective-permute-start | bytes 786440 | tf_op jit(solution)/shard_map/ppermute | solution.py:29

commit v4 on v3

--- a/solution.py
+++ b/solution.py
@@ -194,17 +194,27 @@
         field[:, :, lane : lane + 256] = part.reshape(ROWS, STEP, 256)
 
 
-def inner_kernel(place_ref, rate_ref, x_ref, out0, out1, out2, out3, coef, onehot, field, tiles):
+def inner_kernel(place_ref, rate_ref, x_ref, own_ref, *refs):
+    gives, (coef, onehot, field, tiles) = refs[:CHIPS], refs[CHIPS:]
     onehot[...] = rows_first(range(ROWS))
     fill_coefs(coef, lambda k, row: rate_ref[k, row : row + 1, :], INNER)
 
     def step(start):
         transpose_in(onehot, x_ref, field, start)
         load = lambda row: grouped(field[row])
-        store = lambda row, value: send_row(place_ref, tiles, (out0, out1, out2, out3), row - 2, start, value)
+
+        def store(row, value):
+            value = value.reshape(STEP, value.shape[-1]).astype(jnp.bfloat16)
+            for tile in range(2 * CHIPS):
+                tiles[tile] = value[:, tile * 128 : (tile + 1) * 128]
+            for away in range(CHIPS):
+                chip, core = lax.rem(place_ref[0] + away, CHIPS), place_ref[1]
+                own_ref[away, row - 2, pl.ds(start, STEP), :] = tiles[2 * chip + core]
+                gives[away][row - 2, pl.ds(start, STEP), :] = tiles[2 * chip + 1 - core]
+
         two_substeps(coef, INNER, load, range(2, 6), store)
 
-    steps(out0.shape[2], step)
+    steps(own_ref.shape[2], step)
 
 
 def send_row(place_ref, tiles, outs, slot, start, value):
@@ -226,9 +236,13 @@
     ]
 
 
+def sides(shape, dtype):
+    return [struct((CHIPS, *shape), dtype)] + [struct(shape, dtype)] * CHIPS
+
+
 def inner_rows(place, courant, flat):
     width, bins = flat.shape[1], flat.shape[0] // ROWS
-    outs = [struct((2, 4, bins, 128), flat.dtype)] * CHIPS
+    outs = sides((4, bins, 128), flat.dtype)
     scratch = first_scratch(len(INNER), width, flat.dtype)
     return call(inner_kernel, "inner_rows", place, (courant, flat), outs, scratch, 6, 120 * bins * width)
 
@@ -282,20 +296,28 @@
         out_ref[1] = refs[away - 1][...]
 
 
-def paired_travel(place, own, *gives):
+def paired(place, own, *gives, early=False):
     got = [swapped(give) for give in gives]
+    place = tied(place, got[0]) if early else place
     outs = [struct((2, *gives[0].shape), own.dtype)] * (CHIPS - 1)
-    parts = call(paired_kernel, "paired", place, (own, *got[1:]), outs, [], 2, 0)
-    return [own, got[0]] + [shifted(part, "bins", -2 * (away + 1)) for away, part in enumerate(parts)]
-
-
-def arrived_kernel(place_ref, own_ref, got_ref, *refs):
-    parts, (low_ref, high_ref) = refs[: CHIPS - 1], refs[CHIPS - 1 :]
+    return own, got[0], call(paired_kernel, "paired", place, (own, *got[1:]), outs, [], 2, 0)
+
+
+def spread(own, got, parts, direction):
+    return [own, got] + [shifted(parts[away - 1], "bins", 2 * direction * away) for away in (2, 1, 3)]
+
+
+def paired_slot(refs, away, other):
+    return refs[(0, 3, 2, 4)[away]].at[other] if away else refs[1] if other else refs[0].at[0]
+
+
+def arrived_kernel(place_ref, *refs):
+    slots, (low_ref, high_ref) = refs[: CHIPS + 1], refs[CHIPS + 1 :]
     for away in range(CHIPS):
         for other in range(2):
             tile = 2 * lax.rem(place_ref[0] + away, CHIPS) + lax.bitwise_xor(place_ref[1], other)
             lanes = pl.ds(pl.multiple_of(tile * 128, 128), 128)
-            slot = parts[away - 1].at[other] if away else got_ref if other else own_ref.at[0]
+            slot = paired_slot(slots, away, other)
             for row in range(2):
                 low_ref[row, :, lanes] = slot[row]
                 high_ref[row, :, lanes] = slot[row + 2]
@@ -471,15 +493,17 @@
 
 
 def coagulate_kernel(picked, swap_first, place_ref, satur_ref, growth_ref, first_ref, second_ref, *refs):
-    slots, outs, (field, losses, kept, moved) = refs[:8], refs[8:-4], refs[-4:]
-    rows, size, lanes = slots[0].shape[1:]
+    count = 2 * CHIPS if swap_first else CHIPS + 1
+    slots, outs, (field, losses, kept, moved) = refs[:count], refs[count:-4], refs[-4:]
+    rows, size, lanes = slots[1].shape[-3:]
     bins, cells = field.shape
     chip, core = place_ref[0], place_ref[1]
     half = bins // 2
     blocks = [block_of(place_ref, away, other) for away in range(CHIPS) for other in range(2)]
     for slot in range(2 * CHIPS):
+        source = slots[slot].at[core] if swap_first else paired_slot(slots, *divmod(slot, 2))
         for r in range(rows):
-            field[slot * size : (slot + 1) * size, r * lanes : (r + 1) * lanes] = slots[slot][core, r]
+            field[slot * size : (slot + 1) * size, r * lanes : (r + 1) * lanes] = source[r]
     for start in (0, half):
         at = slice(start, start + half)
         collide = jnp.dot(first_ref[at, :], field[...], preferred_element_type=jnp.float32)
@@ -518,12 +542,12 @@
 
 
 def coagulate(picked, swap_first, place, satur, growth, first, second, slots):
-    _, rows, size, lanes = slots[0].shape
+    rows, size, lanes = slots[1].shape[-3:]
     bins, cells = 2 * CHIPS * size, rows * lanes
-    shape, dtype = slots[0].shape[1:], slots[0].dtype
+    shape, dtype = slots[1].shape[-3:], slots[1].dtype
     outs = [struct((2, *shape), dtype)] * CHIPS
     if swap_first:
-        outs = [struct((CHIPS, *shape), dtype)] + [struct(shape, dtype)] * CHIPS
+        outs = sides(shape, dtype)
     scratch = [
         pltpu.VMEM((bins, cells), jnp.bfloat16),
         pltpu.VMEM((bins, cells), jnp.bfloat16),
@@ -536,7 +560,8 @@
 
 
 def travel(parts, direction):
-    return [parts[0]] + [shifted(parts[away], "bins", 2 * direction * away) for away in range(1, CHIPS)]
+    sent = {away: shifted(parts[away], "bins", 2 * direction * away) for away in (1, 3, 2)}
+    return [parts[0]] + [sent[away] for away in range(1, CHIPS)]
 
 
 def with_other_core(parts):
@@ -554,17 +579,17 @@
     flat = concen.reshape(bins * rows, width)
     low, high, flat, courant = edge_rows(place, flat, courant)
     first_under, first_over = shifted(high, "cells", 1), shifted(low, "cells", -1)
-    inner = inner_rows(place, courant, tied(flat, low))
-    outer = outer_rows(place, courant, first_under, tied(flat, inner[0]), first_over)
-    inner_slots = with_other_core([tied(part, outer[0]) for part in travel(inner, 1)])
+    inner = paired(place, *inner_rows(place, courant, tied(flat, low)), early=True)
+    outer = outer_rows(place, courant, first_under, tied(flat, inner[2][0]), first_over)
+    inner = spread(*inner, 1)
     growth = growth.reshape(2 * CHIPS, bins)
-    at = tied(place, *inner_slots[3::2])
+    at = tied(place, outer[0])
     first, second, growth = matrices(at, pair_lists.T, active_count, growth, kernel, redist)
-    inner = coagulate((2, 3, 4, 5), False, place, saturation, growth, first, second, inner_slots)
+    inner = coagulate((2, 3, 4, 5), False, place, saturation, growth, first, second, inner)
     outer_slots = with_other_core([tied(part, inner[0]) for part in travel(outer, 1)])
     outer = coagulate((0, 1, 6, 7), True, place, saturation, growth, first, second, outer_slots)
 
-    outer_slots = paired_travel(place, *outer)
+    outer_slots = spread(*paired(place, *outer), -1)
     inner_slots = with_other_core(travel([tied(part, outer[0]) for part in inner], -1))
     low, high = arrived_rows(place, outer_slots)
     under, over = shifted(high, "cells", 1), shifted(low, "cells", -1)

time: 96.1 us -> 92.5 us (0.963)
  waiting for transfers between devices: 27.6 us -> 24.2 us
    ppermute x16, waiting for transfers between devices: 22 us -> 16.5 us  [shifted(): return lax.ppermute(value, axis, pairs)]
    ppermute x16, waiting for transfers between devices: 5.6 us -> 7.65 us  [swapped(): return lax.ppermute(value, 'bins', [(i, i ^ 1) for i in range(2 * CHIPS)])]
    pallas_call x10 -> x11, Pallas kernels: 32.7 us -> 33.3 us  [call(): pl.pallas_call(body, in_specs=specs, out_specs=[pl.BlockSpec(memory_space...]
  transfers between devices with their start and end apart: 32 -> 32, of which waited for: 18 -> 18; matrix products, arithmetic and copies ran while one was open for 0% -> 0% of each run, Pallas kernels for 22% -> 24%
where the time goes in v4:
time: 92.5 us; the launch traced here: 92.4 us
  starting transfers between devices  34.5 us (37%)
  Pallas kernels  33.3 us (36%)
  waiting for transfers between devices  24.2 us (26%)
    pallas_call x11, Pallas kernels, call(): pl.pallas_call(body, in_specs=specs, out_specs=[pl.BlockSpec(memory_space...  33.3 us
    ppermute x16, starting transfers between devices, shifted(): return lax.ppermute(value, axis, pairs)  31.4 us
    ppermute x16, waiting for transfers between devices, shifted(): return lax.ppermute(value, axis, pairs)  16.5 us
    ppermute x16, waiting for transfers between devices, swapped(): return lax.ppermute(value, 'bins', [(i, i ^ 1) for i in range(2 * CHIPS)])  7.65 us
    ppermute x16, starting transfers between devices, swapped(): return lax.ppermute(value, 'bins', [(i, i ^ 1) for i in range(2 * CHIPS)])  3.19 us
  transfers between devices with their start and end apart: 32, of which 18 were waited for; matrix products, arithmetic and copies ran while one was open for 0% of the time, Pallas kernels for 24%

profile of v4, /device:TPU:0, one launch (start us, length us, event | category | flops | bytes accessed | tf_op | source)
XLA Modules:
  0.0 92.4 jit_solution(4274446535209716480)
XLA Ops:
  0.0 0.1 pad_add_fusion.place_ref
  0.1 2.7 %edge_rows.1 = (bf16[2,144,1024]{2,1,0:T(8,128)(2,1)S(1)}, bf16[2,144,1024]{2,1,0:T(8,128)(2,1)S(1)}, bf16[1024,1024]{1,0:T(8,128)(2,1)S(1)}, f32[2,8,1024]{2,1,0:T(8,128)S(1)}) custom-call(s32[3]{0:T(128)S(1)} %pad_add_fusion.place_ref, bf16[1024,1024]{1,0:T(8,128)(2,1)} %bitcast.8, f32[2,8,1024]{2,1,0:T(8,128)} %far_rate_ref.1), custom_call_target="tpu_custom_call" | custom-call | flops 4194304 | bytes 86016 | tf_op jit(solution)/shard_map/edge_rows/pallas_call | solution.py:49
  2.8 1.6 %collective-permute-start = (bf16[2,144,1024]{2,1,0:T(8,128)(2,1)S(1)}, bf16[2,144,1024]{2,1,0:T(8,128)(2,1)S(1)}, u32[]{:S(2)}, u32[]{:S(2)}) collective-permute-start(bf16[2,144,1024]{2,1,0:T(8,128)(2,1)S(1)} %get-tuple-element.52), channel_id=1, source_target_pairs={{0,1},{1,2},{2,3},{3,4},{4,5},{5,6},{6,7},{7,8},{8,9},{9,10},{10,1... | collective-permute-start | bytes 1769480 | tf_op jit(solution)/shard_map/ppermute | solution.py:25
  4.4 4.8 %collective-permute-start.1 = (bf16[2,144,1024]{2,1,0:T(8,128)(2,1)S(1)}, bf16[2,144,1024]{2,1,0:T(8,128)(2,1)S(1)}, u32[]{:S(2)}, u32[]{:S(2)}) collective-permute-start(bf16[2,144,1024]{2,1,0:T(8,128)(2,1)S(1)} %get-tuple-element.54), channel_id=1, source_target_pairs={{0,15},{1,0},{2,1},{3,2},{4,3},{5,4},{6,5},{7,6},{8,7},{9,8},{10,9... | collective-permute-start | bytes 1769480 | tf_op jit(solution)/shard_map/ppermute | solution.py:25
  9.2 4.8 %inner_rows.1 = (bf16[4,4,128,128]{3,2,1,0:T(8,128)(2,1)S(1)}, bf16[4,128,128]{2,1,0:T(8,128)(2,1)S(1)}, bf16[4,128,128]{2,1,0:T(8,128)(2,1)S(1)}, bf16[4,128,12...) custom-call(s32[3]{0:T(128)S(1)} %pad_add_fusion.place_ref, f32[2,8,1024]{2,1,0:T(8,128)S(1)} %get-tuple-element.53.rate_ref, ...), custom_call_target="tpu_custom_call" | custom-call | flops 245760 | bytes 50176 | tf_op jit(solution)/shard_map/inner_rows/pallas_call | solution.py:49
  14.1 0.1 collective-permute-start.2
  14.2 0.5 collective-permute-start.3
  14.7 0.1 collective-permute-start.4
  14.8 0.7 collective-permute-done.2.refs_1_
  15.5 0.1 collective-permute-start.5
  15.7 0.0 collective-permute-done.3.refs_0_
  15.7 0.3 collective-permute-done.4.refs_1_
  16.0 0.8 collective-permute-done.5.refs_2_
  16.9 0.6 paired.2
  17.5 3.3 %collective-permute-start.6 = (bf16[2,4,128,128]{3,2,1,0:T(8,128)(2,1)S(1)}, bf16[2,4,128,128]{3,2,1,0:T(8,128)(2,1)S(1)}, u32[]{:S(2)}, u32[]{:S(2)}) collective-permute-start(bf16[2,4,128,128]{3,2,1,0:T(8,128)(2,1)S(1)} %get-tuple-element.70), channel_id=1, source_target_pairs={{0,64},{16,80},{32,96},{48,112},{64,0},{80,16},{96,32},{112,48},{1... | collective-permute-start | bytes 786440 | tf_op jit(solution)/shard_map/ppermute | solution.py:25
  20.7 1.1 %collective-permute-start.8 = (bf16[2,4,128,128]{3,2,1,0:T(8,128)(2,1)S(1)}, bf16[2,4,128,128]{3,2,1,0:T(8,128)(2,1)S(1)}, u32[]{:S(2)}, u32[]{:S(2)}) collective-permute-start(bf16[2,4,128,128]{3,2,1,0:T(8,128)(2,1)S(1)} %get-tuple-element.71), channel_id=1, source_target_pairs={{0,96},{16,112},{32,0},{48,16},{64,32},{80,48},{96,64},{112,80},{1... | collective-permute-start | bytes 786440 | tf_op jit(solution)/shard_map/ppermute | solution.py:25
  21.8 1.0 %collective-permute-start.7 = (bf16[2,4,128,128]{3,2,1,0:T(8,128)(2,1)S(1)}, bf16[2,4,128,128]{3,2,1,0:T(8,128)(2,1)S(1)}, u32[]{:S(2)}, u32[]{:S(2)}) collective-permute-start(bf16[2,4,128,128]{3,2,1,0:T(8,128)(2,1)S(1)} %get-tuple-element.63), channel_id=1, source_target_pairs={{0,32},{16,48},{32,64},{48,80},{64,96},{80,112},{96,0},{112,16},{1... | collective-permute-start | bytes 786440 | tf_op jit(solution)/shard_map/ppermute | solution.py:25
  22.7 0.0 collective-permute-done.1.over_ref.first_over
  22.7 5.3 %outer_rows.1 = (bf16[2,4,128,128]{3,2,1,0:T(8,128)(2,1)S(1)}, bf16[2,4,128,128]{3,2,1,0:T(8,128)(2,1)S(1)}, bf16[2,4,128,128]{3,2,1,0:T(8,128)(2,1)S(1)}, bf16[2,4,128,128]{3,2,1,0:T(8,128)(2,1)S(1)}) custom-call(s32[3]{0:T(128)S(1)} %pad_add_fusion.place_ref, f32[2,8,1024]{2,1,0:T(8,128)S(1)} %get-tuple-element.53.rate_ref, ...), custom_call_target="tpu_custom_call" | custom-call | flops 294912 | bytes 68608 | tf_op jit(solution)/shard_map/outer_rows/pallas_call | solution.py:49
  28.0 2.8 %collective-permute-start.14 = (bf16[2,4,128,128]{3,2,1,0:T(8,128)(2,1)S(1)}, bf16[2,4,128,128]{3,2,1,0:T(8,128)(2,1)S(1)}, u32[]{:S(2)}, u32[]{:S(2)}) collective-permute-start(bf16[2,4,128,128]{3,2,1,0:T(8,128)(2,1)S(1)} %get-tuple-element.78), channel_id=1, source_target_pairs={{0,96},{16,112},{32,0},{48,16},{64,32},{80,48},{96,64},{112,80},{1... | collective-permute-start | bytes 786440 | tf_op jit(solution)/shard_map/ppermute | solution.py:25
  30.8 0.6 collective-permute-start.12
  31.4 1.0 %collective-permute-start.10 = (bf16[2,4,128,128]{3,2,1,0:T(8,128)(2,1)S(1)}, bf16[2,4,128,128]{3,2,1,0:T(8,128)(2,1)S(1)}, u32[]{:S(2)}, u32[]{:S(2)}) collective-permute-start(bf16[2,4,128,128]{3,2,1,0:T(8,128)(2,1)S(1)} %get-tuple-element.74), channel_id=1, source_target_pairs={{0,32},{16,48},{32,64},{48,80},{64,96},{80,112},{96,0},{112,16},{1... | collective-permute-start | bytes 786440 | tf_op jit(solution)/shard_map/ppermute | solution.py:25
  32.4 3.6 %matrices.1 = (bf16[1024,1024]{1,0:T(8,128)(2,1)S(1)}, bf16[1024,1024]{1,0:T(8,128)(2,1)S(1)}, f32[1024,128]{1,0:T(8,128)S(1)}) custom-call(s32[3]{0:T(128)S(1)} %pad_add_fusion.place_ref, s32[128]{0:T(128)S(1)} %copy-done.2, s32[64,128]{1,0:T(8,128)} %bitcast.9, f32[8,128]{1,0:T(8,128)S(1)} %bitcast.7, bf16[8,8,128,128]{3,2,1,0:T(8,128)(2,1)} %far_kernel.1, ...), custom_call_target="tpu_custom_call" | custom-call | bytes 139848 | tf_op jit(solution)/shard_map/matrices/pallas_call | solution.py:49
  36.0 0.0 collective-permute-done.7.refs_3_
  36.0 3.5 %coagulate.2 = (bf16[2,4,128,128]{3,2,1,0:T(8,128)(2,1)S(1)}, bf16[2,4,128,128]{3,2,1,0:T(8,128)(2,1)S(1)}, bf16[2,4,128,128]{3,2,1,0:T(8,128)(2,1)S(1)}, bf16[2,4,128,128]{3,2,1,0:T(8,128)(2,1)S(1)}) custom-call(s32[3]{0:T(128)S(1)} %pad_add_fusion.place_ref, f32[8,128]{1,0:T(8,128)S(1)} %copy-done, f32[1024,128]{1,0:T(8,128)S(1)} %get-tuple-element.67.growth_ref, ...), custom_call_target="tpu_custom_call" | custom-call | flops 33554432 | bytes 112704 | tf_op jit(solution)/shard_map/coagulate/pallas_call | solution.py:49
  39.6 0.1 collective-permute-start.9
  39.6 0.1 collective-permute-done.14.refs_6_
  39.8 1.8 %collective-permute-done.12.refs_4_ = bf16[2,4,128,128]{3,2,1,0:T(8,128)(2,1)S(1)} collective-permute-done((bf16[2,4,128,128]{3,2,1,0:T(8,128)(2,1)S(1)}, bf16[2,4,128,128]{3,2,1,0:T(8,128)(2,1)S(1)}, u32[]{:S(2)}, u32[]{:S(2)}) %collective-permute-start.12) | collective-permute-done | bytes 262176 | tf_op jit(solution)/shard_map/ppermute | solution.py:25
  41.6 3.6 %collective-permute-done.10.refs_2_ = bf16[2,4,128,128]{3,2,1,0:T(8,128)(2,1)S(1)} collective-permute-done((bf16[2,4,128,128]{3,2,1,0:T(8,128)(2,1)S(1)}, bf16[2,4,128,128]{3,2,1,0:T(8,128)(2,1)S(1)}, u32[]{:S(2)}, u32[]{:S(2)}) %collective-permute-start.10) | collective-permute-done | bytes 262176 | tf_op jit(solution)/shard_map/ppermute | solution.py:25
  45.2 0.0 collective-permute-start.11
  45.2 0.5 collective-permute-start.13
  45.7 0.0 collective-permute-start.15
  45.7 0.0 collective-permute-done.9.refs_1_
  45.7 1.0 %collective-permute-done.11.refs_3_ = bf16[2,4,128,128]{3,2,1,0:T(8,128)(2,1)S(1)} collective-permute-done((bf16[2,4,128,128]{3,2,1,0:T(8,128)(2,1)S(1)}, bf16[2,4,128,128]{3,2,1,0:T(8,128)(2,1)S(1)}, u32[]{:S(2)}, u32[]{:S(2)}) %collective-permute-start.11) | collective-permute-done | bytes 262176 | tf_op jit(solution)/shard_map/ppermute | solution.py:29
  46.7 0.4 collective-permute-done.13.refs_5_
  47.1 0.4 collective-permute-done.15.refs_7_
  47.4 3.5 %coagulate.3 = (bf16[4,4,128,128]{3,2,1,0:T(8,128)(2,1)S(1)}, bf16[4,128,128]{2,1,0:T(8,128)(2,1)S(1)}, bf16[4,128,128]{2,1,0:T(8,128)(2,1)S(1)}, bf16[4,128,128...) custom-call(s32[3]{0:T(128)S(1)} %pad_add_fusion.place_ref, f32[8,128]{1,0:T(8,128)S(1)} %copy-done, ...), custom_call_target="tpu_custom_call" | custom-call | flops 33554432 | bytes 122944 | tf_op jit(solution)/shard_map/coagulate/pallas_call | solution.py:49
  51.0 0.2 collective-permute-start.17
  51.2 0.4 collective-permute-start.18
  51.5 0.1 collective-permute-start.19
  51.7 0.7 collective-permute-done.17.refs_0_
  52.4 0.2 collective-permute-done.18.refs_1_
  52.6 0.3 collective-permute-done.19.refs_2_
  52.9 0.6 paired.3
  53.5 2.4 %collective-permute-start.20 = (bf16[2,4,128,128]{3,2,1,0:T(8,128)(2,1)S(1)}, bf16[2,4,128,128]{3,2,1,0:T(8,128)(2,1)S(1)}, u32[]{:S(2)}, u32[]{:S(2)}) collective-permute-start(bf16[2,4,128,128]{3,2,1,0:T(8,128)(2,1)S(1)} %get-tuple-element.85), channel_id=1, source_target_pairs={{0,64},{16,80},{32,96},{48,112},{64,0},{80,16},{96,32},{112,48},{1... | collective-permute-start | bytes 786440 | tf_op jit(solution)/shard_map/ppermute | solution.py:25
  55.9 1.3 %collective-permute-start.21 = (bf16[2,4,128,128]{3,2,1,0:T(8,128)(2,1)S(1)}, bf16[2,4,128,128]{3,2,1,0:T(8,128)(2,1)S(1)}, u32[]{:S(2)}, u32[]{:S(2)}) collective-permute-start(bf16[2,4,128,128]{3,2,1,0:T(8,128)(2,1)S(1)} %get-tuple-element.86), channel_id=1, source_target_pairs={{0,96},{16,112},{32,0},{48,16},{64,32},{80,48},{96,64},{112,80},{1... | collective-permute-start | bytes 786440 | tf_op jit(solution)/shard_map/ppermute | solution.py:25
  57.1 0.8 collective-permute-start.22
  57.9 0.5 collective-permute-start.16
  58.4 1.2 %collective-permute-done.16.refs_1_ = bf16[4,128,128]{2,1,0:T(8,128)(2,1)S(1)} collective-permute-done((bf16[4,128,128]{2,1,0:T(8,128)(2,1)S(1)}, bf16[4,128,128]{2,1,0:T(8,128)(2,1)S(1)}, u32[]{:S(2)}, u32[]{:S(2)}) %collective-permute-start.16) | collective-permute-done | bytes 131104 | tf_op jit(solution)/shard_map/ppermute | solution.py:29
  59.6 2.5 %collective-permute-start.25 = (bf16[2,4,128,128]{3,2,1,0:T(8,128)(2,1)S(1)}, bf16[2,4,128,128]{3,2,1,0:T(8,128)(2,1)S(1)}, u32[]{:S(2)}, u32[]{:S(2)}) collective-permute-start(bf16[2,4,128,128]{3,2,1,0:T(8,128)(2,1)S(1)} %get-tuple-element.92), channel_id=1, source_target_pairs={{0,96},{16,112},{32,0},{48,16},{64,32},{80,48},{96,64},{112,80},{1... | collective-permute-start | bytes 786440 | tf_op jit(solution)/shard_map/ppermute | solution.py:25
  62.1 2.2 %collective-permute-done.20.refs_2_ = bf16[2,4,128,128]{3,2,1,0:T(8,128)(2,1)S(1)} collective-permute-done((bf16[2,4,128,128]{3,2,1,0:T(8,128)(2,1)S(1)}, bf16[2,4,128,128]{3,2,1,0:T(8,128)(2,1)S(1)}, u32[]{:S(2)}, u32[]{:S(2)}) %collective-permute-start.20) | collective-permute-done | bytes 262176 | tf_op jit(solution)/shard_map/ppermute | solution.py:25
  64.3 2.3 %collective-permute-start.27 = (bf16[2,4,128,128]{3,2,1,0:T(8,128)(2,1)S(1)}, bf16[2,4,128,128]{3,2,1,0:T(8,128)(2,1)S(1)}, u32[]{:S(2)}, u32[]{:S(2)}) collective-permute-start(bf16[2,4,128,128]{3,2,1,0:T(8,128)(2,1)S(1)} %get-tuple-element.94), channel_id=1, source_target_pairs={{0,64},{16,80},{32,96},{48,112},{64,0},{80,16},{96,32},{112,48},{1... | collective-permute-start | bytes 786440 | tf_op jit(solution)/shard_map/ppermute | solution.py:25
  66.5 2.8 %collective-permute-done.21.refs_3_ = bf16[2,4,128,128]{3,2,1,0:T(8,128)(2,1)S(1)} collective-permute-done((bf16[2,4,128,128]{3,2,1,0:T(8,128)(2,1)S(1)}, bf16[2,4,128,128]{3,2,1,0:T(8,128)(2,1)S(1)}, u32[]{:S(2)}, u32[]{:S(2)}) %collective-permute-start.21) | collective-permute-done | bytes 262176 | tf_op jit(solution)/shard_map/ppermute | solution.py:25
  69.4 0.7 collective-permute-start.29
  70.0 0.8 arrived_rows.1
  70.9 0.1 collective-permute-start.23
  71.0 5.3 %collective-permute-start.31 = (bf16[2,128,1024]{2,1,0:T(8,128)(2,1)S(1)}, bf16[2,128,1024]{2,1,0:T(8,128)(2,1)S(1)}, u32[]{:S(2)}, u32[]{:S(2)}) collective-permute-start(bf16[2,128,1024]{2,1,0:T(8,128)(2,1)S(1)} %get-tuple-element.89.low_ref), channel_id=1, source_target_pairs={{0,15},{1,0},{2,1},{3,2},{4,3},{5,4},{6,5},{7,6},{8,7},{9,8},{10,9... | collective-permute-start | bytes 1572872 | tf_op jit(solution)/shard_map/ppermute | solution.py:25
  76.3 0.5 collective-permute-start.28
  76.8 3.5 %collective-permute-done.29.refs_6_ = bf16[2,4,128,128]{3,2,1,0:T(8,128)(2,1)S(1)} collective-permute-done((bf16[2,4,128,128]{3,2,1,0:T(8,128)(2,1)S(1)}, bf16[2,4,128,128]{3,2,1,0:T(8,128)(2,1)S(1)}, u32[]{:S(2)}, u32[]{:S(2)}) %collective-permute-start.29) | collective-permute-done | bytes 262176 | tf_op jit(solution)/shard_map/ppermute | solution.py:25
  80.4 0.0 collective-permute-start.30
  80.4 1.5 %collective-permute-done.30.refs_7_ = bf16[2,4,128,128]{3,2,1,0:T(8,128)(2,1)S(1)} collective-permute-done((bf16[2,4,128,128]{3,2,1,0:T(8,128)(2,1)S(1)}, bf16[2,4,128,128]{3,2,1,0:T(8,128)(2,1)S(1)}, u32[]{:S(2)}, u32[]{:S(2)}) %collective-permute-start.30) | collective-permute-done | bytes 262176 | tf_op jit(solution)/shard_map/ppermute | solution.py:29
  81.9 3.4 %middle_rows.1 = (bf16[4,128,1024]{2,1,0:T(8,128)(2,1)S(1)}, f32[4,128,1024]{2,1,0:T(8,128)S(1)}) custom-call(s32[3]{0:T(128)S(1)} %pad_add_fusion.place_ref, f32[2,8,1024]{2,1,0:T(8,128)S(1)} %get-tuple-element.53.rate_ref, bf16[2,128,1024]{2,1,0:T(8,128)(2,1)S(1)} %get-tuple-element.89.low_ref, bf16[2,128,1024]{2,1,0:T(8,128)(2,1)S(1)} %get-tuple-element.88.high_ref, ...), custom_call_target="tpu_custom_call" | custom-call | flops 245760 | bytes 99328 | tf_op jit(solution)/shard_map/middle_rows/pallas_call | solution.py:49
  85.3 2.4 %collective-permute-done.23.under_ref = bf16[2,128,1024]{2,1,0:T(8,128)(2,1)S(1)} collective-permute-done((bf16[2,128,1024]{2,1,0:T(8,128)(2,1)S(1)}, bf16[2,128,1024]{2,1,0:T(8,128)(2,1)S(1)}, u32[]{:S(2)}, u32[]{:S(2)}) %collective-permute-start.23) | collective-permute-done | bytes 524320 | tf_op jit(solution)/shard_map/ppermute | solution.py:25
  87.8 4.5 %final_rows.1 = bf16[1024,1024]{1,0:T(8,128)(2,1)} custom-call(s32[3]{0:T(128)S(1)} %pad_add_fusion.place_ref, bf16[2,144,1024]{2,1,0:T(8,128)(2,1)S(1)} %collective-permute-done.under_ref.first_under, f32[2,8,1024]{2,1,0:T(8,128)S(1)} %get-tuple-element.53.rate_ref, bf16[2,144,1024]{2,1,0:T(8,128)(2,1)S(1)} %collective-permute-done.1.over_ref.first_over, ...), custom_call_target="tpu_custom_call" | custom-call | flops 196608 | bytes 134144 | tf_op jit(solution)/shard_map/final_rows/pallas_call | solution.py:49
  (18 shorter events, 0.0 us)
Async XLA Ops:
  2.8 20.0 %collective-permute-start = (bf16[2,144,1024]{2,1,0:T(8,128)(2,1)S(1)}, bf16[2,144,1024]{2,1,0:T(8,128)(2,1)S(1)}, u32[]{:S(2)}, u32[]{:S(2)}) collective-permute-start(bf16[2,144,1024]{2,1,0:T(8,128)(2,1)S(1)} %get-tuple-element.52), channel_id=1, source_target_pairs={{0,1},{1,2},{2,3},{3,4},{4,5},{5,6},{6,7},{7,8},{8,9},{9,10},{10,1... | collective-permute-start | bytes 1769480 | tf_op jit(solution)/shard_map/ppermute | solution.py:25
  4.4 18.3 %collective-permute-start.1 = (bf16[2,144,1024]{2,1,0:T(8,128)(2,1)S(1)}, bf16[2,144,1024]{2,1,0:T(8,128)(2,1)S(1)}, u32[]{:S(2)}, u32[]{:S(2)}) collective-permute-start(bf16[2,144,1024]{2,1,0:T(8,128)(2,1)S(1)} %get-tuple-element.54), channel_id=1, source_target_pairs={{0,15},{1,0},{2,1},{3,2},{4,3},{5,4},{6,5},{7,6},{8,7},{9,8},{10,9... | collective-permute-start | bytes 1769480 | tf_op jit(solution)/shard_map/ppermute | solution.py:25
  14.1 1.4 %collective-permute-start.2 = (bf16[4,128,128]{2,1,0:T(8,128)(2,1)S(1)}, bf16[4,128,128]{2,1,0:T(8,128)(2,1)S(1)}, u32[]{:S(2)}, u32[]{:S(2)}) collective-permute-start(bf16[4,128,128]{2,1,0:T(8,128)(2,1)S(1)} %get-tuple-element.57), channel_id=1, source_target_pairs={{0,16},{16,0},{32,48},{48,32},{64,80},{80,64},{96,112},{112,96},{1... | collective-permute-start | bytes 393224 | tf_op jit(solution)/shard_map/ppermute | solution.py:29
  14.2 1.5 %collective-permute-start.3 = (bf16[4,128,128]{2,1,0:T(8,128)(2,1)S(1)}, bf16[4,128,128]{2,1,0:T(8,128)(2,1)S(1)}, u32[]{:S(2)}, u32[]{:S(2)}) collective-permute-start(bf16[4,128,128]{2,1,0:T(8,128)(2,1)S(1)} %get-tuple-element.60), channel_id=1, source_target_pairs={{0,16},{16,0},{32,48},{48,32},{64,80},{80,64},{96,112},{112,96},{1... | collective-permute-start | bytes 393224 | tf_op jit(solution)/shard_map/ppermute | solution.py:29
  14.7 1.3 %collective-permute-start.4 = (bf16[4,128,128]{2,1,0:T(8,128)(2,1)S(1)}, bf16[4,128,128]{2,1,0:T(8,128)(2,1)S(1)}, u32[]{:S(2)}, u32[]{:S(2)}) collective-permute-start(bf16[4,128,128]{2,1,0:T(8,128)(2,1)S(1)} %get-tuple-element.61), channel_id=1, source_target_pairs={{0,16},{16,0},{32,48},{48,32},{64,80},{80,64},{96,112},{112,96},{1... | collective-permute-start | bytes 393224 | tf_op jit(solution)/shard_map/ppermute | solution.py:29
  15.5 1.3 %collective-permute-start.5 = (bf16[4,128,128]{2,1,0:T(8,128)(2,1)S(1)}, bf16[4,128,128]{2,1,0:T(8,128)(2,1)S(1)}, u32[]{:S(2)}, u32[]{:S(2)}) collective-permute-start(bf16[4,128,128]{2,1,0:T(8,128)(2,1)S(1)} %get-tuple-element.62), channel_id=1, source_target_pairs={{0,16},{16,0},{32,48},{48,32},{64,80},{80,64},{96,112},{112,96},{1... | collective-permute-start | bytes 393224 | tf_op jit(solution)/shard_map/ppermute | solution.py:29
  16.9 15.6 %copy-start.1 = (f32[1024]{0:T(1024)S(1)}, f32[1024]{0:T(1024)}, u32[]{:S(2)}) copy-start(f32[1024]{0:T(1024)} %param.11) | copy-start | bytes 12292
  16.9 15.6 %copy-start.2 = (s32[128]{0:T(128)S(1)}, s32[128]{0:T(128)}, u32[]{:S(2)}) copy-start(s32[128]{0:T(128)} %count_ref.1) | copy-start | bytes 1540
  17.5 14.0 %collective-permute-start.6 = (bf16[2,4,128,128]{3,2,1,0:T(8,128)(2,1)S(1)}, bf16[2,4,128,128]{3,2,1,0:T(8,128)(2,1)S(1)}, u32[]{:S(2)}, u32[]{:S(2)}) collective-permute-start(bf16[2,4,128,128]{3,2,1,0:T(8,128)(2,1)S(1)} %get-tuple-element.70), channel_id=1, source_target_pairs={{0,64},{16,80},{32,96},{48,112},{64,0},{80,16},{96,32},{112,48},{1... | collective-permute-start | bytes 786440 | tf_op jit(solution)/shard_map/ppermute | solution.py:25
  20.7 15.3 %collective-permute-start.8 = (bf16[2,4,128,128]{3,2,1,0:T(8,128)(2,1)S(1)}, bf16[2,4,128,128]{3,2,1,0:T(8,128)(2,1)S(1)}, u32[]{:S(2)}, u32[]{:S(2)}) collective-permute-start(bf16[2,4,128,128]{3,2,1,0:T(8,128)(2,1)S(1)} %get-tuple-element.71), channel_id=1, source_target_pairs={{0,96},{16,112},{32,0},{48,16},{64,32},{80,48},{96,64},{112,80},{1... | collective-permute-start | bytes 786440 | tf_op jit(solution)/shard_map/ppermute | solution.py:25
  21.8 14.3 %collective-permute-start.7 = (bf16[2,4,128,128]{3,2,1,0:T(8,128)(2,1)S(1)}, bf16[2,4,128,128]{3,2,1,0:T(8,128)(2,1)S(1)}, u32[]{:S(2)}, u32[]{:S(2)}) collective-permute-start(bf16[2,4,128,128]{3,2,1,0:T(8,128)(2,1)S(1)} %get-tuple-element.63), channel_id=1, source_target_pairs={{0,32},{16,48},{32,64},{48,80},{64,96},{80,112},{96,0},{112,16},{1... | collective-permute-start | bytes 786440 | tf_op jit(solution)/shard_map/ppermute | solution.py:25
  28.0 11.8 %collective-permute-start.14 = (bf16[2,4,128,128]{3,2,1,0:T(8,128)(2,1)S(1)}, bf16[2,4,128,128]{3,2,1,0:T(8,128)(2,1)S(1)}, u32[]{:S(2)}, u32[]{:S(2)}) collective-permute-start(bf16[2,4,128,128]{3,2,1,0:T(8,128)(2,1)S(1)} %get-tuple-element.78), channel_id=1, source_target_pairs={{0,96},{16,112},{32,0},{48,16},{64,32},{80,48},{96,64},{112,80},{1... | collective-permute-start | bytes 786440 | tf_op jit(solution)/shard_map/ppermute | solution.py:25
  30.8 10.7 %collective-permute-start.12 = (bf16[2,4,128,128]{3,2,1,0:T(8,128)(2,1)S(1)}, bf16[2,4,128,128]{3,2,1,0:T(8,128)(2,1)S(1)}, u32[]{:S(2)}, u32[]{:S(2)}) collective-permute-start(bf16[2,4,128,128]{3,2,1,0:T(8,128)(2,1)S(1)} %get-tuple-element.76), channel_id=1, source_target_pairs={{0,64},{16,80},{32,96},{48,112},{64,0},{80,16},{96,32},{112,48},{1... | collective-permute-start | bytes 786440 | tf_op jit(solution)/shard_map/ppermute | solution.py:25
  31.4 13.7 %collective-permute-start.10 = (bf16[2,4,128,128]{3,2,1,0:T(8,128)(2,1)S(1)}, bf16[2,4,128,128]{3,2,1,0:T(8,128)(2,1)S(1)}, u32[]{:S(2)}, u32[]{:S(2)}) collective-permute-start(bf16[2,4,128,128]{3,2,1,0:T(8,128)(2,1)S(1)} %get-tuple-element.74), channel_id=1, source_target_pairs={{0,32},{16,48},{32,64},{48,80},{64,96},{80,112},{96,0},{112,16},{1... | collective-permute-start | bytes 786440 | tf_op jit(solution)/shard_map/ppermute | solution.py:25
  32.4 3.6 %copy-start = (f32[8,128]{1,0:T(8,128)S(1)}, f32[8,128]{1,0:T(8,128)}, u32[]{:S(2)}) copy-start(f32[8,128]{1,0:T(8,128)} %satur_ref.3) | copy-start | bytes 12292
  39.6 6.1 %collective-permute-start.9 = (bf16[2,4,128,128]{3,2,1,0:T(8,128)(2,1)S(1)}, bf16[2,4,128,128]{3,2,1,0:T(8,128)(2,1)S(1)}, u32[]{:S(2)}, u32[]{:S(2)}) collective-permute-start(bf16[2,4,128,128]{3,2,1,0:T(8,128)(2,1)S(1)} %get-tuple-element.73.refs_0_), channel_id=1, source_target_pairs={{0,16},{16,0},{32,48},{48,32},{64,80},{80,64},{96,112},{112,96},{1... | collective-permute-start | bytes 786440 | tf_op jit(solution)/shard_map/ppermute | solution.py:29
  45.2 1.5 %collective-permute-start.11 = (bf16[2,4,128,128]{3,2,1,0:T(8,128)(2,1)S(1)}, bf16[2,4,128,128]{3,2,1,0:T(8,128)(2,1)S(1)}, u32[]{:S(2)}, u32[]{:S(2)}) collective-permute-start(bf16[2,4,128,128]{3,2,1,0:T(8,128)(2,1)S(1)} %collective-permute-done.10.refs_2_), channel_id=1, source_target_pairs={{0,16},{16,0},{32,48},{48,32},{64,80},{80,64},{96,112},{112,96},{1... | collective-permute-start | bytes 786440 | tf_op jit(solution)/shard_map/ppermute | solution.py:29
  45.2 1.9 %collective-permute-start.13 = (bf16[2,4,128,128]{3,2,1,0:T(8,128)(2,1)S(1)}, bf16[2,4,128,128]{3,2,1,0:T(8,128)(2,1)S(1)}, u32[]{:S(2)}, u32[]{:S(2)}) collective-permute-start(bf16[2,4,128,128]{3,2,1,0:T(8,128)(2,1)S(1)} %collective-permute-done.12.refs_4_), channel_id=1, source_target_pairs={{0,16},{16,0},{32,48},{48,32},{64,80},{80,64},{96,112},{112,96},{1... | collective-permute-start | bytes 786440 | tf_op jit(solution)/shard_map/ppermute | solution.py:29
  45.7 1.8 %collective-permute-start.15 = (bf16[2,4,128,128]{3,2,1,0:T(8,128)(2,1)S(1)}, bf16[2,4,128,128]{3,2,1,0:T(8,128)(2,1)S(1)}, u32[]{:S(2)}, u32[]{:S(2)}) collective-permute-start(bf16[2,4,128,128]{3,2,1,0:T(8,128)(2,1)S(1)} %collective-permute-done.14.refs_6_), channel_id=1, source_target_pairs={{0,16},{16,0},{32,48},{48,32},{64,80},{80,64},{96,112},{112,96},{1... | collective-permute-start | bytes 786440 | tf_op jit(solution)/shard_map/ppermute | solution.py:29
  51.0 1.4 %collective-permute-start.17 = (bf16[4,128,128]{2,1,0:T(8,128)(2,1)S(1)}, bf16[4,128,128]{2,1,0:T(8,128)(2,1)S(1)}, u32[]{:S(2)}, u32[]{:S(2)}) collective-permute-start(bf16[4,128,128]{2,1,0:T(8,128)(2,1)S(1)} %get-tuple-element.82), channel_id=1, source_target_pairs={{0,16},{16,0},{32,48},{48,32},{64,80},{80,64},{96,112},{112,96},{1... | collective-permute-start | bytes 393224 | tf_op jit(solution)/shard_map/ppermute | solution.py:29
  51.2 1.4 %collective-permute-start.18 = (bf16[4,128,128]{2,1,0:T(8,128)(2,1)S(1)}, bf16[4,128,128]{2,1,0:T(8,128)(2,1)S(1)}, u32[]{:S(2)}, u32[]{:S(2)}) collective-permute-start(bf16[4,128,128]{2,1,0:T(8,128)(2,1)S(1)} %get-tuple-element.83), channel_id=1, source_target_pairs={{0,16},{16,0},{32,48},{48,32},{64,80},{80,64},{96,112},{112,96},{1... | collective-permute-start | bytes 393224 | tf_op jit(solution)/shard_map/ppermute | solution.py:29
  51.5 1.3 %collective-permute-start.19 = (bf16[4,128,128]{2,1,0:T(8,128)(2,1)S(1)}, bf16[4,128,128]{2,1,0:T(8,128)(2,1)S(1)}, u32[]{:S(2)}, u32[]{:S(2)}) collective-permute-start(bf16[4,128,128]{2,1,0:T(8,128)(2,1)S(1)} %get-tuple-element.84), channel_id=1, source_target_pairs={{0,16},{16,0},{32,48},{48,32},{64,80},{80,64},{96,112},{112,96},{1... | collective-permute-start | bytes 393224 | tf_op jit(solution)/shard_map/ppermute | solution.py:29
  53.5 10.8 %collective-permute-start.20 = (bf16[2,4,128,128]{3,2,1,0:T(8,128)(2,1)S(1)}, bf16[2,4,128,128]{3,2,1,0:T(8,128)(2,1)S(1)}, u32[]{:S(2)}, u32[]{:S(2)}) collective-permute-start(bf16[2,4,128,128]{3,2,1,0:T(8,128)(2,1)S(1)} %get-tuple-element.85), channel_id=1, source_target_pairs={{0,64},{16,80},{32,96},{48,112},{64,0},{80,16},{96,32},{112,48},{1... | collective-permute-start | bytes 786440 | tf_op jit(solution)/shard_map/ppermute | solution.py:25
  55.9 13.5 %collective-permute-start.21 = (bf16[2,4,128,128]{3,2,1,0:T(8,128)(2,1)S(1)}, bf16[2,4,128,128]{3,2,1,0:T(8,128)(2,1)S(1)}, u32[]{:S(2)}, u32[]{:S(2)}) collective-permute-start(bf16[2,4,128,128]{3,2,1,0:T(8,128)(2,1)S(1)} %get-tuple-element.86), channel_id=1, source_target_pairs={{0,96},{16,112},{32,0},{48,16},{64,32},{80,48},{96,64},{112,80},{1... | collective-permute-start | bytes 786440 | tf_op jit(solution)/shard_map/ppermute | solution.py:25
  57.1 12.9 %collective-permute-start.22 = (bf16[2,4,128,128]{3,2,1,0:T(8,128)(2,1)S(1)}, bf16[2,4,128,128]{3,2,1,0:T(8,128)(2,1)S(1)}, u32[]{:S(2)}, u32[]{:S(2)}) collective-permute-start(bf16[2,4,128,128]{3,2,1,0:T(8,128)(2,1)S(1)} %get-tuple-element.87), channel_id=1, source_target_pairs={{0,32},{16,48},{32,64},{48,80},{64,96},{80,112},{96,0},{112,16},{1... | collective-permute-start | bytes 786440 | tf_op jit(solution)/shard_map/ppermute | solution.py:25
  57.9 13.1 %collective-permute-start.24 = (bf16[2,4,128,128]{3,2,1,0:T(8,128)(2,1)S(1)}, bf16[2,4,128,128]{3,2,1,0:T(8,128)(2,1)S(1)}, u32[]{:S(2)}, u32[]{:S(2)}) collective-permute-start(bf16[2,4,128,128]{3,2,1,0:T(8,128)(2,1)S(1)} %get-tuple-element.90.refs_0_), channel_id=1, source_target_pairs={{0,16},{16,0},{32,48},{48,32},{64,80},{80,64},{96,112},{112,96},{1... | collective-permute-start | bytes 786440 | tf_op jit(solution)/shard_map/ppermute | solution.py:29
  57.9 1.7 %collective-permute-start.16 = (bf16[4,128,128]{2,1,0:T(8,128)(2,1)S(1)}, bf16[4,128,128]{2,1,0:T(8,128)(2,1)S(1)}, u32[]{:S(2)}, u32[]{:S(2)}) collective-permute-start(bf16[4,128,128]{2,1,0:T(8,128)(2,1)S(1)} %get-tuple-element.81), channel_id=1, source_target_pairs={{0,16},{16,0},{32,48},{48,32},{64,80},{80,64},{96,112},{112,96},{1... | collective-permute-start | bytes 393224 | tf_op jit(solution)/shard_map/ppermute | solution.py:29
  59.6 16.7 %collective-permute-start.25 = (bf16[2,4,128,128]{3,2,1,0:T(8,128)(2,1)S(1)}, bf16[2,4,128,128]{3,2,1,0:T(8,128)(2,1)S(1)}, u32[]{:S(2)}, u32[]{:S(2)}) collective-permute-start(bf16[2,4,128,128]{3,2,1,0:T(8,128)(2,1)S(1)} %get-tuple-element.92), channel_id=1, source_target_pairs={{0,96},{16,112},{32,0},{48,16},{64,32},{80,48},{96,64},{112,80},{1... | collective-permute-start | bytes 786440 | tf_op jit(solution)/shard_map/ppermute | solution.py:25
  64.3 12.1 %collective-permute-start.27 = (bf16[2,4,128,128]{3,2,1,0:T(8,128)(2,1)S(1)}, bf16[2,4,128,128]{3,2,1,0:T(8,128)(2,1)S(1)}, u32[]{:S(2)}, u32[]{:S(2)}) collective-permute-start(bf16[2,4,128,128]{3,2,1,0:T(8,128)(2,1)S(1)} %get-tuple-element.94), channel_id=1, source_target_pairs={{0,64},{16,80},{32,96},{48,112},{64,0},{80,16},{96,32},{112,48},{1... | collective-permute-start | bytes 786440 | tf_op jit(solution)/shard_map/ppermute | solution.py:25
  69.4 11.0 %collective-permute-start.29 = (bf16[2,4,128,128]{3,2,1,0:T(8,128)(2,1)S(1)}, bf16[2,4,128,128]{3,2,1,0:T(8,128)(2,1)S(1)}, u32[]{:S(2)}, u32[]{:S(2)}) collective-permute-start(bf16[2,4,128,128]{3,2,1,0:T(8,128)(2,1)S(1)} %get-tuple-element.96), channel_id=1, source_target_pairs={{0,32},{16,48},{32,64},{48,80},{64,96},{80,112},{96,0},{112,16},{1... | collective-permute-start | bytes 786440 | tf_op jit(solution)/shard_map/ppermute | solution.py:25
  70.9 16.9 %collective-permute-start.23 = (bf16[2,128,1024]{2,1,0:T(8,128)(2,1)S(1)}, bf16[2,128,1024]{2,1,0:T(8,128)(2,1)S(1)}, u32[]{:S(2)}, u32[]{:S(2)}) collective-permute-start(bf16[2,128,1024]{2,1,0:T(8,128)(2,1)S(1)} %get-tuple-element.88.high_ref), channel_id=1, source_target_pairs={{0,1},{1,2},{2,3},{3,4},{4,5},{5,6},{6,7},{7,8},{8,9},{9,10},{10,1... | collective-permute-start | bytes 1572872 | tf_op jit(solution)/shard_map/ppermute | solution.py:25
  71.0 16.8 %collective-permute-start.31 = (bf16[2,128,1024]{2,1,0:T(8,128)(2,1)S(1)}, bf16[2,128,1024]{2,1,0:T(8,128)(2,1)S(1)}, u32[]{:S(2)}, u32[]{:S(2)}) collective-permute-start(bf16[2,128,1024]{2,1,0:T(8,128)(2,1)S(1)} %get-tuple-element.89.low_ref), channel_id=1, source_target_pairs={{0,15},{1,0},{2,1},{3,2},{4,3},{5,4},{6,5},{7,6},{8,7},{9,8},{10,9... | collective-permute-start | bytes 1572872 | tf_op jit(solution)/shard_map/ppermute | solution.py:25
  76.3 4.1 %collective-permute-start.26 = (bf16[2,4,128,128]{3,2,1,0:T(8,128)(2,1)S(1)}, bf16[2,4,128,128]{3,2,1,0:T(8,128)(2,1)S(1)}, u32[]{:S(2)}, u32[]{:S(2)}) collective-permute-start(bf16[2,4,128,128]{3,2,1,0:T(8,128)(2,1)S(1)} %collective-permute-done.25.refs_2_), channel_id=1, source_target_pairs={{0,16},{16,0},{32,48},{48,32},{64,80},{80,64},{96,112},{112,96},{1... | collective-permute-start | bytes 786440 | tf_op jit(solution)/shard_map/ppermute | solution.py:29
  76.3 4.1 %collective-permute-start.28 = (bf16[2,4,128,128]{3,2,1,0:T(8,128)(2,1)S(1)}, bf16[2,4,128,128]{3,2,1,0:T(8,128)(2,1)S(1)}, u32[]{:S(2)}, u32[]{:S(2)}) collective-permute-start(bf16[2,4,128,128]{3,2,1,0:T(8,128)(2,1)S(1)} %collective-permute-done.27.refs_4_), channel_id=1, source_target_pairs={{0,16},{16,0},{32,48},{48,32},{64,80},{80,64},{96,112},{112,96},{1... | collective-permute-start | bytes 786440 | tf_op jit(solution)/shard_map/ppermute | solution.py:29
  80.4 1.5 %collective-permute-start.30 = (bf16[2,4,128,128]{3,2,1,0:T(8,128)(2,1)S(1)}, bf16[2,4,128,128]{3,2,1,0:T(8,128)(2,1)S(1)}, u32[]{:S(2)}, u32[]{:S(2)}) collective-permute-start(bf16[2,4,128,128]{3,2,1,0:T(8,128)(2,1)S(1)} %collective-permute-done.29.refs_6_), channel_id=1, source_target_pairs={{0,16},{16,0},{32,48},{48,32},{64,80},{80,64},{96,112},{112,96},{1... | collective-permute-start | bytes 786440 | tf_op jit(solution)/shard_map/ppermute | solution.py:29

commit v5 on v4

--- a/solution.py
+++ b/solution.py
@@ -11,9 +11,9 @@
 CHIPS = 4
 ROWS = 8
 INNER = [1, 2, 3, 4, 5, 6]
-OUTER = [-1, 0, 1, 2, 5, 6, 7, 8]
 LAST = [-1, 0, 1, 6, 7, 8]
 KEPT = [1, 2, 5, 6]
+LISTED = (0, 1, 3, 2)
 PACK = 16
 MIB = 2**20
 SHRINK = 64
@@ -46,13 +46,15 @@
         specs[1 + index] = pl.BlockSpec(memory_space=pl.ANY)
         operands[index] = in_hbm(operands[index])
     moved = sum(a.size * a.dtype.itemsize for a in (*operands, *outs))
+    near = [a for index, a in enumerate(operands) if index >= smem and index not in far] + ([] if out_far else list(outs))
+    room = sum(a.size * a.dtype.itemsize for a in near) + mib * MIB
     return pl.pallas_call(
         body,
         in_specs=specs,
         out_specs=[pl.BlockSpec(memory_space=pl.ANY) if out_far else vmem_spec] * len(outs),
         out_shape=outs,
         scratch_shapes=scratch,
-        compiler_params=pltpu.CompilerParams(vmem_limit_bytes=mib * MIB),
+        compiler_params=pltpu.CompilerParams(vmem_limit_bytes=room),
         cost_estimate=pl.CostEstimate(flops=flops // SHRINK, bytes_accessed=moved // SHRINK, transcendentals=0),
         name=name,
     )(place, *operands)
@@ -195,7 +197,7 @@
 
 
 def inner_kernel(place_ref, rate_ref, x_ref, own_ref, *refs):
-    gives, (coef, onehot, field, tiles) = refs[:CHIPS], refs[CHIPS:]
+    gives, (kept_ref, coef, onehot, field, tiles) = refs[:CHIPS], refs[CHIPS:]
     onehot[...] = rows_first(range(ROWS))
     fill_coefs(coef, lambda k, row: rate_ref[k, row : row + 1, :], INNER)
 
@@ -212,7 +214,11 @@
                 own_ref[away, row - 2, pl.ds(start, STEP), :] = tiles[2 * chip + core]
                 gives[away][row - 2, pl.ds(start, STEP), :] = tiles[2 * chip + 1 - core]
 
-        two_substeps(coef, INNER, load, range(2, 6), store)
+        def keep(row, value):
+            if row in KEPT:
+                kept_ref[KEPT.index(row), pl.ds(start, STEP), :] = value.reshape(STEP, value.shape[-1])
+
+        two_substeps(coef, INNER, load, range(2, 6), store, keep)
 
     steps(own_ref.shape[2], step)
 
@@ -242,7 +248,7 @@
 
 def inner_rows(place, courant, flat):
     width, bins = flat.shape[1], flat.shape[0] // ROWS
-    outs = sides((4, bins, 128), flat.dtype)
+    outs = [*sides((4, bins, 128), flat.dtype), struct((4, bins, width), jnp.float32)]
     scratch = first_scratch(len(INNER), width, flat.dtype)
     return call(inner_kernel, "inner_rows", place, (courant, flat), outs, scratch, 6, 120 * bins * width)
 
@@ -258,35 +264,48 @@
     return rates
 
 
-def outer_kernel(place_ref, rate_ref, under_ref, x_ref, over_ref, out0, out1, out2, out3, coef, onehot, field, tiles):
-    onehot[...] = rows_first(range(ROWS))
-    fill_coefs(coef, all_rates(under_ref, rate_ref, over_ref), OUTER)
+def end_rows(coef, under_ref, low_ref, kept_ref, high_ref, over_ref, at, store):
+    field = lambda ref, row: grouped(ref[row, at, :])
+
+    def once(row, before, value, after):
+        return substep(coef, LAST.index(row), before, value, after)
+
+    zero, one = field(low_ref, 0), field(kept_ref, 0)
+    edge = once(-1, field(under_ref, 0), field(under_ref, 1), zero)
+    first = once(0, field(under_ref, 1), zero, field(low_ref, 1))
+    store(0, once(0, edge, first, one))
+    store(1, once(1, first, one, field(kept_ref, 1)))
+    seven, six = field(high_ref, 1), field(kept_ref, 3)
+    edge = once(8, seven, field(over_ref, 0), field(over_ref, 1))
+    last = once(7, field(high_ref, 0), seven, field(over_ref, 0))
+    store(7, once(7, six, last, edge))
+    store(6, once(6, field(kept_ref, 2), six, last))
+
+
+def outer_kernel(place_ref, rate_ref, under_ref, low_ref, kept_ref, high_ref, over_ref, out0, out1, out2, out3, coef, tiles):
+    fill_coefs(coef, all_rates(under_ref, rate_ref, over_ref), LAST)
 
     def step(start):
-        transpose_in(onehot, x_ref, field, start)
-
-        def load(row):
-            if row < 0:
-                return grouped(under_ref[row + 2, pl.ds(start, STEP), :])
-            if row > 7:
-                return grouped(over_ref[row - 8, pl.ds(start, STEP), :])
-            return grouped(field[row])
-
         def store(row, value):
-            send_row(place_ref, tiles, (out0, out1, out2, out3), row if row < 2 else row - 4, start, value)
-
-        two_substeps(coef, OUTER, load, range(0, 2), store)
-        two_substeps(coef, OUTER, load, range(6, 8), store)
+            value = value.reshape(STEP, value.shape[-1]).astype(jnp.bfloat16)
+            for tile in range(2 * CHIPS):
+                tiles[tile] = value[:, tile * 128 : (tile + 1) * 128]
+            for away, out_ref in enumerate((out0, out1, out2, out3)):
+                chip = lax.rem(place_ref[0] + away, CHIPS)
+                for core in range(2):
+                    out_ref[core, row if row < 2 else row - 4, pl.ds(start, STEP), :] = tiles[2 * chip + core]
+
+        end_rows(coef, under_ref, low_ref, kept_ref, high_ref, over_ref, pl.ds(start, STEP), store)
 
     steps(out0.shape[2], step)
 
 
-def outer_rows(place, courant, under, flat, over):
-    width, bins = flat.shape[1], flat.shape[0] // ROWS
-    outs = [struct((2, 4, bins, 128), flat.dtype)] * CHIPS
-    scratch = first_scratch(len(OUTER), width, flat.dtype)
-    operands = (courant, under, flat, over)
-    return call(outer_kernel, "outer_rows", place, operands, outs, scratch, 6, 144 * bins * width)
+def outer_rows(place, courant, under, low, kept, high, over):
+    _, bins, width = kept.shape
+    outs = [struct((2, 4, bins, 128), low.dtype)] * CHIPS
+    scratch = [pltpu.VMEM((5 * len(LAST), 8, width), jnp.float32), pltpu.VMEM((2 * CHIPS, STEP, 128), low.dtype)]
+    operands = (courant, under, low, kept, high, over)
+    return call(outer_kernel, "outer_rows", place, operands, outs, scratch, 6, 96 * bins * width)
 
 
 def paired_kernel(place_ref, own_ref, *refs):
@@ -384,29 +403,16 @@
     copies = []
     for index in range(count):
         at = slice(index * STEP, (index + 1) * STEP)
-        field = lambda ref, row: grouped(ref[row, at, :])
 
         def store(row, value):
-            back[row * STEP : (row + 1) * STEP, :] = value.reshape(STEP, width).astype(jnp.bfloat16)
-
-        def once(row, before, value, after):
-            return substep(coef, LAST.index(row), before, value, after)
-
-        zero, one = field(low_ref, 0), field(kept_ref, 0)
-        edge = once(-1, field(under_ref, 0), field(under_ref, 1), zero)
-        first = once(0, field(under_ref, 1), zero, field(low_ref, 1))
-        store(0, once(0, edge, first, one))
-        store(1, once(1, first, one, field(kept_ref, 1)))
-        seven, six = field(high_ref, 1), field(kept_ref, 3)
-        edge = once(8, seven, field(over_ref, 0), field(over_ref, 1))
-        last = once(7, field(high_ref, 0), seven, field(over_ref, 0))
-        store(7, once(7, six, last, edge))
-        store(6, once(6, field(kept_ref, 2), six, last))
+            back[index, row * STEP : (row + 1) * STEP, :] = value.reshape(STEP, width).astype(jnp.bfloat16)
+
+        end_rows(coef, under_ref, low_ref, kept_ref, high_ref, over_ref, at, store)
         for row in range(4):
-            back[(row + 2) * STEP : (row + 3) * STEP, :] = mid_ref[row, at, :]
+            back[index, (row + 2) * STEP : (row + 3) * STEP, :] = mid_ref[row, at, :]
         target = slice(index * size, (index + 1) * size)
         for lane in range(0, width, 256):
-            part = jnp.dot(onehot[...], back[:, lane : lane + 256], preferred_element_type=jnp.float32)
+            part = jnp.dot(onehot[...], back[index, :, lane : lane + 256], preferred_element_type=jnp.float32)
             out_ref[target, lane : lane + 256] = part.astype(out_ref.dtype)
         copy = pltpu.make_async_copy(out_ref.at[pl.ds(index * size, size)], far_ref.at[pl.ds(index * size, size)], sems.at[index])
         copy.start()
@@ -420,13 +426,13 @@
     scratch = [
         pltpu.VMEM((5 * len(LAST), 8, width), jnp.float32),
         pltpu.VMEM((ROWS * STEP, ROWS * STEP), jnp.bfloat16),
-        pltpu.VMEM((ROWS * STEP, width), low.dtype),
+        pltpu.VMEM((bins // STEP, ROWS * STEP, width), low.dtype),
         pltpu.VMEM((bins * ROWS, width), low.dtype),
         pltpu.SemaphoreType.DMA((bins // STEP,)),
     ]
     operands = (first_under, courant, first_over, under, low, mid, kept, high, over)
     outs = [struct((bins * ROWS, width), low.dtype)]
-    return call(final_kernel, "final_rows", place, operands, outs, scratch, 7, 96 * bins * width, out_far=True)[0]
+    return call(final_kernel, "final_rows", place, operands, outs, scratch, 10, 96 * bins * width, out_far=True)[0]
 
 
 def block_of(place_ref, away, other):
@@ -501,7 +507,11 @@
     half = bins // 2
     blocks = [block_of(place_ref, away, other) for away in range(CHIPS) for other in range(2)]
     for slot in range(2 * CHIPS):
-        source = slots[slot].at[core] if swap_first else paired_slot(slots, *divmod(slot, 2))
+        away, other = divmod(slot, 2)
+        if swap_first:
+            source = slots[2 * LISTED.index(away) + other].at[core]
+        else:
+            source = paired_slot(slots, away, other)
         for r in range(rows):
             field[slot * size : (slot + 1) * size, r * lanes : (r + 1) * lanes] = source[r]
     for start in (0, half):
@@ -564,10 +574,10 @@
     return [parts[0]] + [sent[away] for away in range(1, CHIPS)]
 
 
-def with_other_core(parts):
+def with_other_core(parts, listed=range(CHIPS)):
     slots = []
-    for part in parts:
-        slots += [part, swapped(part)]
+    for away in listed:
+        slots += [parts[away], swapped(parts[away])]
     return slots
 
 
@@ -579,14 +589,16 @@
     flat = concen.reshape(bins * rows, width)
     low, high, flat, courant = edge_rows(place, flat, courant)
     first_under, first_over = shifted(high, "cells", 1), shifted(low, "cells", -1)
-    inner = paired(place, *inner_rows(place, courant, tied(flat, low)), early=True)
-    outer = outer_rows(place, courant, first_under, tied(flat, inner[2][0]), first_over)
+    *inner, kept = inner_rows(place, courant, tied(flat, low))
+    inner = paired(place, *inner, early=True)
+    at = tied(place, inner[2][0])
+    outer = outer_rows(at, courant, first_under, low, kept, high, first_over)
     inner = spread(*inner, 1)
     growth = growth.reshape(2 * CHIPS, bins)
     at = tied(place, outer[0])
     first, second, growth = matrices(at, pair_lists.T, active_count, growth, kernel, redist)
     inner = coagulate((2, 3, 4, 5), False, place, saturation, growth, first, second, inner)
-    outer_slots = with_other_core([tied(part, inner[0]) for part in travel(outer, 1)])
+    outer_slots = with_other_core([tied(part, inner[0]) for part in travel(outer, 1)], LISTED)
     outer = coagulate((0, 1, 6, 7), True, place, saturation, growth, first, second, outer_slots)
 
     outer_slots = spread(*paired(place, *outer), -1)

time: 92.5 us -> 92.5 us (level)
  Pallas kernels: 33.3 us -> 31.4 us
  starting transfers between devices: 34.5 us -> 36.2 us
    pallas_call x11, Pallas kernels: 33.3 us -> 31.4 us  [call(): pl.pallas_call(body, in_specs=specs, out_specs=[pl.BlockSpec(memory_space...]
    ppermute x16, starting transfers between devices: 31.4 us -> 33 us  [shifted(): return lax.ppermute(value, axis, pairs)]
  transfers between devices with their start and end apart: 32 -> 32, of which waited for: 18 -> 17; matrix products, arithmetic and copies ran while one was open for 0% -> 0% of each run, Pallas kernels for 24% -> 22%
where the time goes in v5:
time: 92.5 us; the launch traced here: 92.4 us
  starting transfers between devices  36.2 us (39%)
  Pallas kernels  31.4 us (34%)
  waiting for transfers between devices  24.4 us (26%)
    ppermute x16, starting transfers between devices, shifted(): return lax.ppermute(value, axis, pairs)  33 us
    pallas_call x11, Pallas kernels, call(): pl.pallas_call(body, in_specs=specs, out_specs=[pl.BlockSpec(memory_space...  31.4 us
    ppermute x16, waiting for transfers between devices, shifted(): return lax.ppermute(value, axis, pairs)  16.8 us
    ppermute x16, waiting for transfers between devices, swapped(): return lax.ppermute(value, 'bins', [(i, i ^ 1) for i in range(2 * CHIPS)])  7.67 us
    ppermute x16, starting transfers between devices, swapped(): return lax.ppermute(value, 'bins', [(i, i ^ 1) for i in range(2 * CHIPS)])  3.17 us
  transfers between devices with their start and end apart: 32, of which 17 were waited for; matrix products, arithmetic and copies ran while one was open for 0% of the time, Pallas kernels for 22%

profile of v5, /device:TPU:0, one launch (start us, length us, event | category | flops | bytes accessed | tf_op | source)
XLA Modules:
  0.0 92.4 jit_solution(17015964446920600485)
XLA Ops:
  0.0 0.1 pad_add_fusion.place_ref
  0.1 2.7 %edge_rows.1 = (bf16[2,144,1024]{2,1,0:T(8,128)(2,1)S(1)}, bf16[2,144,1024]{2,1,0:T(8,128)(2,1)S(1)}, bf16[1024,1024]{1,0:T(8,128)(2,1)S(1)}, f32[2,8,1024]{2,1,0:T(8,128)S(1)}) custom-call(s32[3]{0:T(128)S(1)} %pad_add_fusion.place_ref, bf16[1024,1024]{1,0:T(8,128)(2,1)} %bitcast.8, f32[2,8,1024]{2,1,0:T(8,128)} %far_rate_ref.1), custom_call_target="tpu_custom_call" | custom-call | flops 4194304 | bytes 86016 | tf_op jit(solution)/shard_map/edge_rows/pallas_call | solution.py:51
  2.8 1.6 %collective-permute-start = (bf16[2,144,1024]{2,1,0:T(8,128)(2,1)S(1)}, bf16[2,144,1024]{2,1,0:T(8,128)(2,1)S(1)}, u32[]{:S(2)}, u32[]{:S(2)}) collective-permute-start(bf16[2,144,1024]{2,1,0:T(8,128)(2,1)S(1)} %get-tuple-element.53.high_ref), channel_id=1, source_target_pairs={{0,1},{1,2},{2,3},{3,4},{4,5},{5,6},{6,7},{7,8},{8,9},{9,10},{10,1... | collective-permute-start | bytes 1769480 | tf_op jit(solution)/shard_map/ppermute | solution.py:25
  4.4 4.8 %collective-permute-start.1 = (bf16[2,144,1024]{2,1,0:T(8,128)(2,1)S(1)}, bf16[2,144,1024]{2,1,0:T(8,128)(2,1)S(1)}, u32[]{:S(2)}, u32[]{:S(2)}) collective-permute-start(bf16[2,144,1024]{2,1,0:T(8,128)(2,1)S(1)} %get-tuple-element.55.low_ref), channel_id=1, source_target_pairs={{0,15},{1,0},{2,1},{3,2},{4,3},{5,4},{6,5},{7,6},{8,7},{9,8},{10,9... | collective-permute-start | bytes 1769480 | tf_op jit(solution)/shard_map/ppermute | solution.py:25
  9.2 4.8 %inner_rows.1 = (bf16[4,4,128,128]{3,2,1,0:T(8,128)(2,1)S(1)}, bf16[4,128,128]{2,1,0:T(8,128)(2,1)S(1)}, bf16[4,128,128]{2,1,0:T(8,128)(2,1)S(1)}, bf16[4,128,12...) custom-call(s32[3]{0:T(128)S(1)} %pad_add_fusion.place_ref, ...), custom_call_target="tpu_custom_call" | custom-call | flops 245760 | bytes 82944 | tf_op jit(solution)/shard_map/inner_rows/pallas_call | solution.py:51
  14.1 0.1 collective-permute-start.2
  14.2 0.5 collective-permute-start.3
  14.7 0.1 collective-permute-start.4
  14.7 0.7 collective-permute-done.2.refs_1_
  15.5 0.1 collective-permute-start.5
  15.6 0.0 collective-permute-done.3.refs_0_
  15.7 0.3 collective-permute-done.4.refs_1_
  16.0 0.8 collective-permute-done.5.refs_2_
  16.8 0.6 paired.2
  17.4 3.2 %collective-permute-start.6 = (bf16[2,4,128,128]{3,2,1,0:T(8,128)(2,1)S(1)}, bf16[2,4,128,128]{3,2,1,0:T(8,128)(2,1)S(1)}, u32[]{:S(2)}, u32[]{:S(2)}) collective-permute-start(bf16[2,4,128,128]{3,2,1,0:T(8,128)(2,1)S(1)} %get-tuple-element.72), channel_id=1, source_target_pairs={{0,64},{16,80},{32,96},{48,112},{64,0},{80,16},{96,32},{112,48},{1... | collective-permute-start | bytes 786440 | tf_op jit(solution)/shard_map/ppermute | solution.py:25
  20.7 1.1 %collective-permute-start.8 = (bf16[2,4,128,128]{3,2,1,0:T(8,128)(2,1)S(1)}, bf16[2,4,128,128]{3,2,1,0:T(8,128)(2,1)S(1)}, u32[]{:S(2)}, u32[]{:S(2)}) collective-permute-start(bf16[2,4,128,128]{3,2,1,0:T(8,128)(2,1)S(1)} %get-tuple-element.73), channel_id=1, source_target_pairs={{0,96},{16,112},{32,0},{48,16},{64,32},{80,48},{96,64},{112,80},{1... | collective-permute-start | bytes 786440 | tf_op jit(solution)/shard_map/ppermute | solution.py:25
  21.8 1.0 %collective-permute-start.7 = (bf16[2,4,128,128]{3,2,1,0:T(8,128)(2,1)S(1)}, bf16[2,4,128,128]{3,2,1,0:T(8,128)(2,1)S(1)}, u32[]{:S(2)}, u32[]{:S(2)}) collective-permute-start(bf16[2,4,128,128]{3,2,1,0:T(8,128)(2,1)S(1)} %get-tuple-element.64), channel_id=1, source_target_pairs={{0,32},{16,48},{32,64},{48,80},{64,96},{80,112},{96,0},{112,16},{1... | collective-permute-start | bytes 786440 | tf_op jit(solution)/shard_map/ppermute | solution.py:25
  22.7 0.0 collective-permute-done.under_ref.first_under
  22.7 0.0 collective-permute-done.1.over_ref.first_over
  22.7 0.0 copy-start.2
  22.7 3.4 %outer_rows.1 = (bf16[2,4,128,128]{3,2,1,0:T(8,128)(2,1)S(1)}, bf16[2,4,128,128]{3,2,1,0:T(8,128)(2,1)S(1)}, bf16[2,4,128,128]{3,2,1,0:T(8,128)(2,1)S(1)}, bf16[2,4,128,128]{3,2,1,0:T(8,128)(2,1)S(1)}) custom-call(s32[3]{0:T(128)S(1)} %pad_add_fusion.place_ref, f32[2,8,1024]{2,1,0:T(8,128)S(1)} %get-tuple-element.54.rate_ref, ...), custom_call_target="tpu_custom_call" | custom-call | flops 196608 | bytes 87040 | tf_op jit(solution)/shard_map/outer_rows/pallas_call | solution.py:51
  26.2 3.0 %collective-permute-start.14 = (bf16[2,4,128,128]{3,2,1,0:T(8,128)(2,1)S(1)}, bf16[2,4,128,128]{3,2,1,0:T(8,128)(2,1)S(1)}, u32[]{:S(2)}, u32[]{:S(2)}) collective-permute-start(bf16[2,4,128,128]{3,2,1,0:T(8,128)(2,1)S(1)} %get-tuple-element.80), channel_id=1, source_target_pairs={{0,64},{16,80},{32,96},{48,112},{64,0},{80,16},{96,32},{112,48},{1... | collective-permute-start | bytes 786440 | tf_op jit(solution)/shard_map/ppermute | solution.py:25
  29.2 1.1 %collective-permute-start.12 = (bf16[2,4,128,128]{3,2,1,0:T(8,128)(2,1)S(1)}, bf16[2,4,128,128]{3,2,1,0:T(8,128)(2,1)S(1)}, u32[]{:S(2)}, u32[]{:S(2)}) collective-permute-start(bf16[2,4,128,128]{3,2,1,0:T(8,128)(2,1)S(1)} %get-tuple-element.78), channel_id=1, source_target_pairs={{0,96},{16,112},{32,0},{48,16},{64,32},{80,48},{96,64},{112,80},{1... | collective-permute-start | bytes 786440 | tf_op jit(solution)/shard_map/ppermute | solution.py:25
  30.2 0.0 collective-permute-done.6.refs_2_
  30.2 1.0 %collective-permute-start.10 = (bf16[2,4,128,128]{3,2,1,0:T(8,128)(2,1)S(1)}, bf16[2,4,128,128]{3,2,1,0:T(8,128)(2,1)S(1)}, u32[]{:S(2)}, u32[]{:S(2)}) collective-permute-start(bf16[2,4,128,128]{3,2,1,0:T(8,128)(2,1)S(1)} %get-tuple-element.76), channel_id=1, source_target_pairs={{0,32},{16,48},{32,64},{48,80},{64,96},{80,112},{96,0},{112,16},{1... | collective-permute-start | bytes 786440 | tf_op jit(solution)/shard_map/ppermute | solution.py:25
  31.2 3.5 %matrices.1 = (bf16[1024,1024]{1,0:T(8,128)(2,1)S(1)}, bf16[1024,1024]{1,0:T(8,128)(2,1)S(1)}, f32[1024,128]{1,0:T(8,128)S(1)}) custom-call(s32[3]{0:T(128)S(1)} %pad_add_fusion.place_ref, s32[128]{0:T(128)S(1)} %copy-done.2, s32[64,128]{1,0:T(8,128)} %bitcast.9, f32[8,128]{1,0:T(8,128)S(1)} %bitcast.7, bf16[8,8,128,128]{3,2,1,0:T(8,128)(2,1)} %far_kernel.1, ...), custom_call_target="tpu_custom_call" | custom-call | bytes 139848 | tf_op jit(solution)/shard_map/matrices/pallas_call | solution.py:51
  34.7 0.0 collective-permute-done.7.refs_3_
  34.7 3.5 %coagulate.2 = (bf16[2,4,128,128]{3,2,1,0:T(8,128)(2,1)S(1)}, bf16[2,4,128,128]{3,2,1,0:T(8,128)(2,1)S(1)}, bf16[2,4,128,128]{3,2,1,0:T(8,128)(2,1)S(1)}, bf16[2,4,128,128]{3,2,1,0:T(8,128)(2,1)S(1)}) custom-call(s32[3]{0:T(128)S(1)} %pad_add_fusion.place_ref, f32[8,128]{1,0:T(8,128)S(1)} %copy-done, f32[1024,128]{1,0:T(8,128)S(1)} %get-tuple-element.69.growth_ref, ...), custom_call_target="tpu_custom_call" | custom-call | flops 33554432 | bytes 112704 | tf_op jit(solution)/shard_map/coagulate/pallas_call | solution.py:51
  38.3 0.1 collective-permute-start.9
  38.3 1.1 %collective-permute-done.14.refs_6_ = bf16[2,4,128,128]{3,2,1,0:T(8,128)(2,1)S(1)} collective-permute-done((bf16[2,4,128,128]{3,2,1,0:T(8,128)(2,1)S(1)}, bf16[2,4,128,128]{3,2,1,0:T(8,128)(2,1)S(1)}, u32[]{:S(2)}, u32[]{:S(2)}) %collective-permute-start.14) | collective-permute-done | bytes 262176 | tf_op jit(solution)/shard_map/ppermute | solution.py:25
  39.5 5.2 %collective-permute-done.12.refs_4_ = bf16[2,4,128,128]{3,2,1,0:T(8,128)(2,1)S(1)} collective-permute-done((bf16[2,4,128,128]{3,2,1,0:T(8,128)(2,1)S(1)}, bf16[2,4,128,128]{3,2,1,0:T(8,128)(2,1)S(1)}, u32[]{:S(2)}, u32[]{:S(2)}) %collective-permute-start.12) | collective-permute-done | bytes 262176 | tf_op jit(solution)/shard_map/ppermute | solution.py:25
  44.6 0.5 collective-permute-start.13
  45.2 0.0 collective-permute-start.15
  45.2 0.0 collective-permute-done.9.refs_1_
  45.2 1.0 %collective-permute-done.11.refs_3_ = bf16[2,4,128,128]{3,2,1,0:T(8,128)(2,1)S(1)} collective-permute-done((bf16[2,4,128,128]{3,2,1,0:T(8,128)(2,1)S(1)}, bf16[2,4,128,128]{3,2,1,0:T(8,128)(2,1)S(1)}, u32[]{:S(2)}, u32[]{:S(2)}) %collective-permute-start.11) | collective-permute-done | bytes 262176 | tf_op jit(solution)/shard_map/ppermute | solution.py:29
  46.2 0.4 collective-permute-done.13.refs_5_
  46.6 0.4 collective-permute-done.15.refs_7_
  46.9 3.5 %coagulate.3 = (bf16[4,4,128,128]{3,2,1,0:T(8,128)(2,1)S(1)}, bf16[4,128,128]{2,1,0:T(8,128)(2,1)S(1)}, bf16[4,128,128]{2,1,0:T(8,128)(2,1)S(1)}, bf16[4,128,128...) custom-call(s32[3]{0:T(128)S(1)} %pad_add_fusion.place_ref, f32[8,128]{1,0:T(8,128)S(1)} %copy-done, ...), custom_call_target="tpu_custom_call" | custom-call | flops 33554432 | bytes 122944 | tf_op jit(solution)/shard_map/coagulate/pallas_call | solution.py:51
  50.5 0.2 collective-permute-start.17
  50.7 0.4 collective-permute-start.18
  51.1 0.1 collective-permute-start.19
  51.2 0.7 collective-permute-done.17.refs_0_
  51.9 0.2 collective-permute-done.18.refs_1_
  52.1 0.3 collective-permute-done.19.refs_2_
  52.4 0.6 paired.3
  53.0 2.8 %collective-permute-start.20 = (bf16[2,4,128,128]{3,2,1,0:T(8,128)(2,1)S(1)}, bf16[2,4,128,128]{3,2,1,0:T(8,128)(2,1)S(1)}, u32[]{:S(2)}, u32[]{:S(2)}) collective-permute-start(bf16[2,4,128,128]{3,2,1,0:T(8,128)(2,1)S(1)} %get-tuple-element.87), channel_id=1, source_target_pairs={{0,64},{16,80},{32,96},{48,112},{64,0},{80,16},{96,32},{112,48},{1... | collective-permute-start | bytes 786440 | tf_op jit(solution)/shard_map/ppermute | solution.py:25
  55.8 1.3 %collective-permute-start.21 = (bf16[2,4,128,128]{3,2,1,0:T(8,128)(2,1)S(1)}, bf16[2,4,128,128]{3,2,1,0:T(8,128)(2,1)S(1)}, u32[]{:S(2)}, u32[]{:S(2)}) collective-permute-start(bf16[2,4,128,128]{3,2,1,0:T(8,128)(2,1)S(1)} %get-tuple-element.88), channel_id=1, source_target_pairs={{0,96},{16,112},{32,0},{48,16},{64,32},{80,48},{96,64},{112,80},{1... | collective-permute-start | bytes 786440 | tf_op jit(solution)/shard_map/ppermute | solution.py:25
  57.1 0.8 collective-permute-start.22
  57.9 0.5 collective-permute-start.16
  58.4 1.2 %collective-permute-done.16.refs_1_ = bf16[4,128,128]{2,1,0:T(8,128)(2,1)S(1)} collective-permute-done((bf16[4,128,128]{2,1,0:T(8,128)(2,1)S(1)}, bf16[4,128,128]{2,1,0:T(8,128)(2,1)S(1)}, u32[]{:S(2)}, u32[]{:S(2)}) %collective-permute-start.16) | collective-permute-done | bytes 131104 | tf_op jit(solution)/shard_map/ppermute | solution.py:29
  59.6 2.5 %collective-permute-start.25 = (bf16[2,4,128,128]{3,2,1,0:T(8,128)(2,1)S(1)}, bf16[2,4,128,128]{3,2,1,0:T(8,128)(2,1)S(1)}, u32[]{:S(2)}, u32[]{:S(2)}) collective-permute-start(bf16[2,4,128,128]{3,2,1,0:T(8,128)(2,1)S(1)} %get-tuple-element.94), channel_id=1, source_target_pairs={{0,96},{16,112},{32,0},{48,16},{64,32},{80,48},{96,64},{112,80},{1... | collective-permute-start | bytes 786440 | tf_op jit(solution)/shard_map/ppermute | solution.py:25
  62.1 1.7 %collective-permute-done.20.refs_2_ = bf16[2,4,128,128]{3,2,1,0:T(8,128)(2,1)S(1)} collective-permute-done((bf16[2,4,128,128]{3,2,1,0:T(8,128)(2,1)S(1)}, bf16[2,4,128,128]{3,2,1,0:T(8,128)(2,1)S(1)}, u32[]{:S(2)}, u32[]{:S(2)}) %collective-permute-start.20) | collective-permute-done | bytes 262176 | tf_op jit(solution)/shard_map/ppermute | solution.py:25
  63.8 2.8 %collective-permute-start.27 = (bf16[2,4,128,128]{3,2,1,0:T(8,128)(2,1)S(1)}, bf16[2,4,128,128]{3,2,1,0:T(8,128)(2,1)S(1)}, u32[]{:S(2)}, u32[]{:S(2)}) collective-permute-start(bf16[2,4,128,128]{3,2,1,0:T(8,128)(2,1)S(1)} %get-tuple-element.96), channel_id=1, source_target_pairs={{0,64},{16,80},{32,96},{48,112},{64,0},{80,16},{96,32},{112,48},{1... | collective-permute-start | bytes 786440 | tf_op jit(solution)/shard_map/ppermute | solution.py:25
  66.5 2.8 %collective-permute-done.21.refs_3_ = bf16[2,4,128,128]{3,2,1,0:T(8,128)(2,1)S(1)} collective-permute-done((bf16[2,4,128,128]{3,2,1,0:T(8,128)(2,1)S(1)}, bf16[2,4,128,128]{3,2,1,0:T(8,128)(2,1)S(1)}, u32[]{:S(2)}, u32[]{:S(2)}) %collective-permute-start.21) | collective-permute-done | bytes 262176 | tf_op jit(solution)/shard_map/ppermute | solution.py:25
  69.3 0.7 collective-permute-start.29
  70.0 0.8 arrived_rows.1
  70.9 0.1 collective-permute-start.23
  71.0 5.3 %collective-permute-start.31 = (bf16[2,128,1024]{2,1,0:T(8,128)(2,1)S(1)}, bf16[2,128,1024]{2,1,0:T(8,128)(2,1)S(1)}, u32[]{:S(2)}, u32[]{:S(2)}) collective-permute-start(bf16[2,128,1024]{2,1,0:T(8,128)(2,1)S(1)} %get-tuple-element.91.low_ref), channel_id=1, source_target_pairs={{0,15},{1,0},{2,1},{3,2},{4,3},{5,4},{6,5},{7,6},{8,7},{9,8},{10,9... | collective-permute-start | bytes 1572872 | tf_op jit(solution)/shard_map/ppermute | solution.py:25
  76.3 0.5 collective-permute-start.28
  76.8 3.0 %collective-permute-done.29.refs_6_ = bf16[2,4,128,128]{3,2,1,0:T(8,128)(2,1)S(1)} collective-permute-done((bf16[2,4,128,128]{3,2,1,0:T(8,128)(2,1)S(1)}, bf16[2,4,128,128]{3,2,1,0:T(8,128)(2,1)S(1)}, u32[]{:S(2)}, u32[]{:S(2)}) %collective-permute-start.29) | collective-permute-done | bytes 262176 | tf_op jit(solution)/shard_map/ppermute | solution.py:25
  79.9 1.5 %collective-permute-done.30.refs_7_ = bf16[2,4,128,128]{3,2,1,0:T(8,128)(2,1)S(1)} collective-permute-done((bf16[2,4,128,128]{3,2,1,0:T(8,128)(2,1)S(1)}, bf16[2,4,128,128]{3,2,1,0:T(8,128)(2,1)S(1)}, u32[]{:S(2)}, u32[]{:S(2)}) %collective-permute-start.30) | collective-permute-done | bytes 262176 | tf_op jit(solution)/shard_map/ppermute | solution.py:29
  81.4 3.4 %middle_rows.1 = (bf16[4,128,1024]{2,1,0:T(8,128)(2,1)S(1)}, f32[4,128,1024]{2,1,0:T(8,128)S(1)}) custom-call(s32[3]{0:T(128)S(1)} %pad_add_fusion.place_ref, f32[2,8,1024]{2,1,0:T(8,128)S(1)} %get-tuple-element.54.rate_ref, bf16[2,128,1024]{2,1,0:T(8,128)(2,1)S(1)} %get-tuple-element.91.low_ref, bf16[2,128,1024]{2,1,0:T(8,128)(2,1)S(1)} %get-tuple-element.90.high_ref, ...), custom_call_target="tpu_custom_call" | custom-call | flops 245760 | bytes 99328 | tf_op jit(solution)/shard_map/middle_rows/pallas_call | solution.py:51
  84.8 2.9 %collective-permute-done.23.under_ref = bf16[2,128,1024]{2,1,0:T(8,128)(2,1)S(1)} collective-permute-done((bf16[2,128,1024]{2,1,0:T(8,128)(2,1)S(1)}, bf16[2,128,1024]{2,1,0:T(8,128)(2,1)S(1)}, u32[]{:S(2)}, u32[]{:S(2)}) %collective-permute-start.23) | collective-permute-done | bytes 524320 | tf_op jit(solution)/shard_map/ppermute | solution.py:25
  87.8 4.5 %final_rows.1 = bf16[1024,1024]{1,0:T(8,128)(2,1)} custom-call(s32[3]{0:T(128)S(1)} %pad_add_fusion.place_ref, bf16[2,144,1024]{2,1,0:T(8,128)(2,1)S(1)} %collective-permute-done.under_ref.first_under, f32[2,8,1024]{2,1,0:T(8,128)S(1)} %get-tuple-element.54.rate_ref, bf16[2,144,1024]{2,1,0:T(8,128)(2,1)S(1)} %collective-permute-done.1.over_ref.first_over, ...), custom_call_target="tpu_custom_call" | custom-call | flops 196608 | bytes 134144 | tf_op jit(solution)/shard_map/final_rows/pallas_call | solution.py:51
  (18 shorter events, 0.0 us)
Async XLA Ops:
  2.8 20.0 %collective-permute-start = (bf16[2,144,1024]{2,1,0:T(8,128)(2,1)S(1)}, bf16[2,144,1024]{2,1,0:T(8,128)(2,1)S(1)}, u32[]{:S(2)}, u32[]{:S(2)}) collective-permute-start(bf16[2,144,1024]{2,1,0:T(8,128)(2,1)S(1)} %get-tuple-element.53.high_ref), channel_id=1, source_target_pairs={{0,1},{1,2},{2,3},{3,4},{4,5},{5,6},{6,7},{7,8},{8,9},{9,10},{10,1... | collective-permute-start | bytes 1769480 | tf_op jit(solution)/shard_map/ppermute | solution.py:25
  4.4 18.3 %collective-permute-start.1 = (bf16[2,144,1024]{2,1,0:T(8,128)(2,1)S(1)}, bf16[2,144,1024]{2,1,0:T(8,128)(2,1)S(1)}, u32[]{:S(2)}, u32[]{:S(2)}) collective-permute-start(bf16[2,144,1024]{2,1,0:T(8,128)(2,1)S(1)} %get-tuple-element.55.low_ref), channel_id=1, source_target_pairs={{0,15},{1,0},{2,1},{3,2},{4,3},{5,4},{6,5},{7,6},{8,7},{9,8},{10,9... | collective-permute-start | bytes 1769480 | tf_op jit(solution)/shard_map/ppermute | solution.py:25
  14.1 1.4 %collective-permute-start.2 = (bf16[4,128,128]{2,1,0:T(8,128)(2,1)S(1)}, bf16[4,128,128]{2,1,0:T(8,128)(2,1)S(1)}, u32[]{:S(2)}, u32[]{:S(2)}) collective-permute-start(bf16[4,128,128]{2,1,0:T(8,128)(2,1)S(1)} %get-tuple-element.58), channel_id=1, source_target_pairs={{0,16},{16,0},{32,48},{48,32},{64,80},{80,64},{96,112},{112,96},{1... | collective-permute-start | bytes 393224 | tf_op jit(solution)/shard_map/ppermute | solution.py:29
  14.2 1.5 %collective-permute-start.3 = (bf16[4,128,128]{2,1,0:T(8,128)(2,1)S(1)}, bf16[4,128,128]{2,1,0:T(8,128)(2,1)S(1)}, u32[]{:S(2)}, u32[]{:S(2)}) collective-permute-start(bf16[4,128,128]{2,1,0:T(8,128)(2,1)S(1)} %get-tuple-element.61), channel_id=1, source_target_pairs={{0,16},{16,0},{32,48},{48,32},{64,80},{80,64},{96,112},{112,96},{1... | collective-permute-start | bytes 393224 | tf_op jit(solution)/shard_map/ppermute | solution.py:29
  14.7 1.3 %collective-permute-start.4 = (bf16[4,128,128]{2,1,0:T(8,128)(2,1)S(1)}, bf16[4,128,128]{2,1,0:T(8,128)(2,1)S(1)}, u32[]{:S(2)}, u32[]{:S(2)}) collective-permute-start(bf16[4,128,128]{2,1,0:T(8,128)(2,1)S(1)} %get-tuple-element.62), channel_id=1, source_target_pairs={{0,16},{16,0},{32,48},{48,32},{64,80},{80,64},{96,112},{112,96},{1... | collective-permute-start | bytes 393224 | tf_op jit(solution)/shard_map/ppermute | solution.py:29
  15.5 1.3 %collective-permute-start.5 = (bf16[4,128,128]{2,1,0:T(8,128)(2,1)S(1)}, bf16[4,128,128]{2,1,0:T(8,128)(2,1)S(1)}, u32[]{:S(2)}, u32[]{:S(2)}) collective-permute-start(bf16[4,128,128]{2,1,0:T(8,128)(2,1)S(1)} %get-tuple-element.63), channel_id=1, source_target_pairs={{0,16},{16,0},{32,48},{48,32},{64,80},{80,64},{96,112},{112,96},{1... | collective-permute-start | bytes 393224 | tf_op jit(solution)/shard_map/ppermute | solution.py:29
  17.4 12.8 %collective-permute-start.6 = (bf16[2,4,128,128]{3,2,1,0:T(8,128)(2,1)S(1)}, bf16[2,4,128,128]{3,2,1,0:T(8,128)(2,1)S(1)}, u32[]{:S(2)}, u32[]{:S(2)}) collective-permute-start(bf16[2,4,128,128]{3,2,1,0:T(8,128)(2,1)S(1)} %get-tuple-element.72), channel_id=1, source_target_pairs={{0,64},{16,80},{32,96},{48,112},{64,0},{80,16},{96,32},{112,48},{1... | collective-permute-start | bytes 786440 | tf_op jit(solution)/shard_map/ppermute | solution.py:25
  20.7 14.0 %collective-permute-start.8 = (bf16[2,4,128,128]{3,2,1,0:T(8,128)(2,1)S(1)}, bf16[2,4,128,128]{3,2,1,0:T(8,128)(2,1)S(1)}, u32[]{:S(2)}, u32[]{:S(2)}) collective-permute-start(bf16[2,4,128,128]{3,2,1,0:T(8,128)(2,1)S(1)} %get-tuple-element.73), channel_id=1, source_target_pairs={{0,96},{16,112},{32,0},{48,16},{64,32},{80,48},{96,64},{112,80},{1... | collective-permute-start | bytes 786440 | tf_op jit(solution)/shard_map/ppermute | solution.py:25
  21.8 12.9 %collective-permute-start.7 = (bf16[2,4,128,128]{3,2,1,0:T(8,128)(2,1)S(1)}, bf16[2,4,128,128]{3,2,1,0:T(8,128)(2,1)S(1)}, u32[]{:S(2)}, u32[]{:S(2)}) collective-permute-start(bf16[2,4,128,128]{3,2,1,0:T(8,128)(2,1)S(1)} %get-tuple-element.64), channel_id=1, source_target_pairs={{0,32},{16,48},{32,64},{48,80},{64,96},{80,112},{96,0},{112,16},{1... | collective-permute-start | bytes 786440 | tf_op jit(solution)/shard_map/ppermute | solution.py:25
  22.7 8.5 %copy-start.1 = (f32[1024]{0:T(1024)S(1)}, f32[1024]{0:T(1024)}, u32[]{:S(2)}) copy-start(f32[1024]{0:T(1024)} %param.11) | copy-start | bytes 12292
  22.7 8.5 %copy-start.2 = (s32[128]{0:T(128)S(1)}, s32[128]{0:T(128)}, u32[]{:S(2)}) copy-start(s32[128]{0:T(128)} %count_ref.1) | copy-start | bytes 1540
  26.2 13.3 %collective-permute-start.14 = (bf16[2,4,128,128]{3,2,1,0:T(8,128)(2,1)S(1)}, bf16[2,4,128,128]{3,2,1,0:T(8,128)(2,1)S(1)}, u32[]{:S(2)}, u32[]{:S(2)}) collective-permute-start(bf16[2,4,128,128]{3,2,1,0:T(8,128)(2,1)S(1)} %get-tuple-element.80), channel_id=1, source_target_pairs={{0,64},{16,80},{32,96},{48,112},{64,0},{80,16},{96,32},{112,48},{1... | collective-permute-start | bytes 786440 | tf_op jit(solution)/shard_map/ppermute | solution.py:25
  29.2 15.5 %collective-permute-start.12 = (bf16[2,4,128,128]{3,2,1,0:T(8,128)(2,1)S(1)}, bf16[2,4,128,128]{3,2,1,0:T(8,128)(2,1)S(1)}, u32[]{:S(2)}, u32[]{:S(2)}) collective-permute-start(bf16[2,4,128,128]{3,2,1,0:T(8,128)(2,1)S(1)} %get-tuple-element.78), channel_id=1, source_target_pairs={{0,96},{16,112},{32,0},{48,16},{64,32},{80,48},{96,64},{112,80},{1... | collective-permute-start | bytes 786440 | tf_op jit(solution)/shard_map/ppermute | solution.py:25
  30.2 14.4 %collective-permute-start.10 = (bf16[2,4,128,128]{3,2,1,0:T(8,128)(2,1)S(1)}, bf16[2,4,128,128]{3,2,1,0:T(8,128)(2,1)S(1)}, u32[]{:S(2)}, u32[]{:S(2)}) collective-permute-start(bf16[2,4,128,128]{3,2,1,0:T(8,128)(2,1)S(1)} %get-tuple-element.76), channel_id=1, source_target_pairs={{0,32},{16,48},{32,64},{48,80},{64,96},{80,112},{96,0},{112,16},{1... | collective-permute-start | bytes 786440 | tf_op jit(solution)/shard_map/ppermute | solution.py:25
  31.2 3.5 %copy-start = (f32[8,128]{1,0:T(8,128)S(1)}, f32[8,128]{1,0:T(8,128)}, u32[]{:S(2)}) copy-start(f32[8,128]{1,0:T(8,128)} %satur_ref.3) | copy-start | bytes 12292
  38.3 6.9 %collective-permute-start.9 = (bf16[2,4,128,128]{3,2,1,0:T(8,128)(2,1)S(1)}, bf16[2,4,128,128]{3,2,1,0:T(8,128)(2,1)S(1)}, u32[]{:S(2)}, u32[]{:S(2)}) collective-permute-start(bf16[2,4,128,128]{3,2,1,0:T(8,128)(2,1)S(1)} %get-tuple-element.75.refs_0_), channel_id=1, source_target_pairs={{0,16},{16,0},{32,48},{48,32},{64,80},{80,64},{96,112},{112,96},{1... | collective-permute-start | bytes 786440 | tf_op jit(solution)/shard_map/ppermute | solution.py:29
  44.6 1.5 %collective-permute-start.11 = (bf16[2,4,128,128]{3,2,1,0:T(8,128)(2,1)S(1)}, bf16[2,4,128,128]{3,2,1,0:T(8,128)(2,1)S(1)}, u32[]{:S(2)}, u32[]{:S(2)}) collective-permute-start(bf16[2,4,128,128]{3,2,1,0:T(8,128)(2,1)S(1)} %collective-permute-done.10.refs_2_), channel_id=1, source_target_pairs={{0,16},{16,0},{32,48},{48,32},{64,80},{80,64},{96,112},{112,96},{1... | collective-permute-start | bytes 786440 | tf_op jit(solution)/shard_map/ppermute | solution.py:29
  44.6 1.9 %collective-permute-start.13 = (bf16[2,4,128,128]{3,2,1,0:T(8,128)(2,1)S(1)}, bf16[2,4,128,128]{3,2,1,0:T(8,128)(2,1)S(1)}, u32[]{:S(2)}, u32[]{:S(2)}) collective-permute-start(bf16[2,4,128,128]{3,2,1,0:T(8,128)(2,1)S(1)} %collective-permute-done.12.refs_4_), channel_id=1, source_target_pairs={{0,16},{16,0},{32,48},{48,32},{64,80},{80,64},{96,112},{112,96},{1... | collective-permute-start | bytes 786440 | tf_op jit(solution)/shard_map/ppermute | solution.py:29
  45.2 1.8 %collective-permute-start.15 = (bf16[2,4,128,128]{3,2,1,0:T(8,128)(2,1)S(1)}, bf16[2,4,128,128]{3,2,1,0:T(8,128)(2,1)S(1)}, u32[]{:S(2)}, u32[]{:S(2)}) collective-permute-start(bf16[2,4,128,128]{3,2,1,0:T(8,128)(2,1)S(1)} %collective-permute-done.14.refs_6_), channel_id=1, source_target_pairs={{0,16},{16,0},{32,48},{48,32},{64,80},{80,64},{96,112},{112,96},{1... | collective-permute-start | bytes 786440 | tf_op jit(solution)/shard_map/ppermute | solution.py:29
  50.5 1.4 %collective-permute-start.17 = (bf16[4,128,128]{2,1,0:T(8,128)(2,1)S(1)}, bf16[4,128,128]{2,1,0:T(8,128)(2,1)S(1)}, u32[]{:S(2)}, u32[]{:S(2)}) collective-permute-start(bf16[4,128,128]{2,1,0:T(8,128)(2,1)S(1)} %get-tuple-element.84), channel_id=1, source_target_pairs={{0,16},{16,0},{32,48},{48,32},{64,80},{80,64},{96,112},{112,96},{1... | collective-permute-start | bytes 393224 | tf_op jit(solution)/shard_map/ppermute | solution.py:29
  50.7 1.4 %collective-permute-start.18 = (bf16[4,128,128]{2,1,0:T(8,128)(2,1)S(1)}, bf16[4,128,128]{2,1,0:T(8,128)(2,1)S(1)}, u32[]{:S(2)}, u32[]{:S(2)}) collective-permute-start(bf16[4,128,128]{2,1,0:T(8,128)(2,1)S(1)} %get-tuple-element.85), channel_id=1, source_target_pairs={{0,16},{16,0},{32,48},{48,32},{64,80},{80,64},{96,112},{112,96},{1... | collective-permute-start | bytes 393224 | tf_op jit(solution)/shard_map/ppermute | solution.py:29
  51.1 1.3 %collective-permute-start.19 = (bf16[4,128,128]{2,1,0:T(8,128)(2,1)S(1)}, bf16[4,128,128]{2,1,0:T(8,128)(2,1)S(1)}, u32[]{:S(2)}, u32[]{:S(2)}) collective-permute-start(bf16[4,128,128]{2,1,0:T(8,128)(2,1)S(1)} %get-tuple-element.86), channel_id=1, source_target_pairs={{0,16},{16,0},{32,48},{48,32},{64,80},{80,64},{96,112},{112,96},{1... | collective-permute-start | bytes 393224 | tf_op jit(solution)/shard_map/ppermute | solution.py:29
  53.0 10.8 %collective-permute-start.20 = (bf16[2,4,128,128]{3,2,1,0:T(8,128)(2,1)S(1)}, bf16[2,4,128,128]{3,2,1,0:T(8,128)(2,1)S(1)}, u32[]{:S(2)}, u32[]{:S(2)}) collective-permute-start(bf16[2,4,128,128]{3,2,1,0:T(8,128)(2,1)S(1)} %get-tuple-element.87), channel_id=1, source_target_pairs={{0,64},{16,80},{32,96},{48,112},{64,0},{80,16},{96,32},{112,48},{1... | collective-permute-start | bytes 786440 | tf_op jit(solution)/shard_map/ppermute | solution.py:25
  55.8 13.5 %collective-permute-start.21 = (bf16[2,4,128,128]{3,2,1,0:T(8,128)(2,1)S(1)}, bf16[2,4,128,128]{3,2,1,0:T(8,128)(2,1)S(1)}, u32[]{:S(2)}, u32[]{:S(2)}) collective-permute-start(bf16[2,4,128,128]{3,2,1,0:T(8,128)(2,1)S(1)} %get-tuple-element.88), channel_id=1, source_target_pairs={{0,96},{16,112},{32,0},{48,16},{64,32},{80,48},{96,64},{112,80},{1... | collective-permute-start | bytes 786440 | tf_op jit(solution)/shard_map/ppermute | solution.py:25
  57.1 12.9 %collective-permute-start.22 = (bf16[2,4,128,128]{3,2,1,0:T(8,128)(2,1)S(1)}, bf16[2,4,128,128]{3,2,1,0:T(8,128)(2,1)S(1)}, u32[]{:S(2)}, u32[]{:S(2)}) collective-permute-start(bf16[2,4,128,128]{3,2,1,0:T(8,128)(2,1)S(1)} %get-tuple-element.89), channel_id=1, source_target_pairs={{0,32},{16,48},{32,64},{48,80},{64,96},{80,112},{96,0},{112,16},{1... | collective-permute-start | bytes 786440 | tf_op jit(solution)/shard_map/ppermute | solution.py:25
  57.9 13.1 %collective-permute-start.24 = (bf16[2,4,128,128]{3,2,1,0:T(8,128)(2,1)S(1)}, bf16[2,4,128,128]{3,2,1,0:T(8,128)(2,1)S(1)}, u32[]{:S(2)}, u32[]{:S(2)}) collective-permute-start(bf16[2,4,128,128]{3,2,1,0:T(8,128)(2,1)S(1)} %get-tuple-element.92.refs_0_), channel_id=1, source_target_pairs={{0,16},{16,0},{32,48},{48,32},{64,80},{80,64},{96,112},{112,96},{1... | collective-permute-start | bytes 786440 | tf_op jit(solution)/shard_map/ppermute | solution.py:29
  57.9 1.7 %collective-permute-start.16 = (bf16[4,128,128]{2,1,0:T(8,128)(2,1)S(1)}, bf16[4,128,128]{2,1,0:T(8,128)(2,1)S(1)}, u32[]{:S(2)}, u32[]{:S(2)}) collective-permute-start(bf16[4,128,128]{2,1,0:T(8,128)(2,1)S(1)} %get-tuple-element.83), channel_id=1, source_target_pairs={{0,16},{16,0},{32,48},{48,32},{64,80},{80,64},{96,112},{112,96},{1... | collective-permute-start | bytes 393224 | tf_op jit(solution)/shard_map/ppermute | solution.py:29
  59.6 16.7 %collective-permute-start.25 = (bf16[2,4,128,128]{3,2,1,0:T(8,128)(2,1)S(1)}, bf16[2,4,128,128]{3,2,1,0:T(8,128)(2,1)S(1)}, u32[]{:S(2)}, u32[]{:S(2)}) collective-permute-start(bf16[2,4,128,128]{3,2,1,0:T(8,128)(2,1)S(1)} %get-tuple-element.94), channel_id=1, source_target_pairs={{0,96},{16,112},{32,0},{48,16},{64,32},{80,48},{96,64},{112,80},{1... | collective-permute-start | bytes 786440 | tf_op jit(solution)/shard_map/ppermute | solution.py:25
  63.8 12.6 %collective-permute-start.27 = (bf16[2,4,128,128]{3,2,1,0:T(8,128)(2,1)S(1)}, bf16[2,4,128,128]{3,2,1,0:T(8,128)(2,1)S(1)}, u32[]{:S(2)}, u32[]{:S(2)}) collective-permute-start(bf16[2,4,128,128]{3,2,1,0:T(8,128)(2,1)S(1)} %get-tuple-element.96), channel_id=1, source_target_pairs={{0,64},{16,80},{32,96},{48,112},{64,0},{80,16},{96,32},{112,48},{1... | collective-permute-start | bytes 786440 | tf_op jit(solution)/shard_map/ppermute | solution.py:25
  69.3 10.6 %collective-permute-start.29 = (bf16[2,4,128,128]{3,2,1,0:T(8,128)(2,1)S(1)}, bf16[2,4,128,128]{3,2,1,0:T(8,128)(2,1)S(1)}, u32[]{:S(2)}, u32[]{:S(2)}) collective-permute-start(bf16[2,4,128,128]{3,2,1,0:T(8,128)(2,1)S(1)} %get-tuple-element.98), channel_id=1, source_target_pairs={{0,32},{16,48},{32,64},{48,80},{64,96},{80,112},{96,0},{112,16},{1... | collective-permute-start | bytes 786440 | tf_op jit(solution)/shard_map/ppermute | solution.py:25
  70.9 16.9 %collective-permute-start.23 = (bf16[2,128,1024]{2,1,0:T(8,128)(2,1)S(1)}, bf16[2,128,1024]{2,1,0:T(8,128)(2,1)S(1)}, u32[]{:S(2)}, u32[]{:S(2)}) collective-permute-start(bf16[2,128,1024]{2,1,0:T(8,128)(2,1)S(1)} %get-tuple-element.90.high_ref), channel_id=1, source_target_pairs={{0,1},{1,2},{2,3},{3,4},{4,5},{5,6},{6,7},{7,8},{8,9},{9,10},{10,1... | collective-permute-start | bytes 1572872 | tf_op jit(solution)/shard_map/ppermute | solution.py:25
  71.0 16.8 %collective-permute-start.31 = (bf16[2,128,1024]{2,1,0:T(8,128)(2,1)S(1)}, bf16[2,128,1024]{2,1,0:T(8,128)(2,1)S(1)}, u32[]{:S(2)}, u32[]{:S(2)}) collective-permute-start(bf16[2,128,1024]{2,1,0:T(8,128)(2,1)S(1)} %get-tuple-element.91.low_ref), channel_id=1, source_target_pairs={{0,15},{1,0},{2,1},{3,2},{4,3},{5,4},{6,5},{7,6},{8,7},{9,8},{10,9... | collective-permute-start | bytes 1572872 | tf_op jit(solution)/shard_map/ppermute | solution.py:25
  76.3 3.6 %collective-permute-start.26 = (bf16[2,4,128,128]{3,2,1,0:T(8,128)(2,1)S(1)}, bf16[2,4,128,128]{3,2,1,0:T(8,128)(2,1)S(1)}, u32[]{:S(2)}, u32[]{:S(2)}) collective-permute-start(bf16[2,4,128,128]{3,2,1,0:T(8,128)(2,1)S(1)} %collective-permute-done.25.refs_2_), channel_id=1, source_target_pairs={{0,16},{16,0},{32,48},{48,32},{64,80},{80,64},{96,112},{112,96},{1... | collective-permute-start | bytes 786440 | tf_op jit(solution)/shard_map/ppermute | solution.py:29
  76.3 3.6 %collective-permute-start.28 = (bf16[2,4,128,128]{3,2,1,0:T(8,128)(2,1)S(1)}, bf16[2,4,128,128]{3,2,1,0:T(8,128)(2,1)S(1)}, u32[]{:S(2)}, u32[]{:S(2)}) collective-permute-start(bf16[2,4,128,128]{3,2,1,0:T(8,128)(2,1)S(1)} %collective-permute-done.27.refs_4_), channel_id=1, source_target_pairs={{0,16},{16,0},{32,48},{48,32},{64,80},{80,64},{96,112},{112,96},{1... | collective-permute-start | bytes 786440 | tf_op jit(solution)/shard_map/ppermute | solution.py:29
  79.9 1.5 %collective-permute-start.30 = (bf16[2,4,128,128]{3,2,1,0:T(8,128)(2,1)S(1)}, bf16[2,4,128,128]{3,2,1,0:T(8,128)(2,1)S(1)}, u32[]{:S(2)}, u32[]{:S(2)}) collective-permute-start(bf16[2,4,128,128]{3,2,1,0:T(8,128)(2,1)S(1)} %collective-permute-done.29.refs_6_), channel_id=1, source_target_pairs={{0,16},{16,0},{32,48},{48,32},{64,80},{80,64},{96,112},{112,96},{1... | collective-permute-start | bytes 786440 | tf_op jit(solution)/shard_map/ppermute | solution.py:29
